TPU v7x, 32 devices: a whole 2x2x4 slice. The times are simulated.
32 devices in a mesh: seq: 4 (over y, x), shard: 8 (over z, core).
Axes of the slice: x: 2, y: 2, z: 4, core: 2. Of those that a mesh axis runs over, the one named last changes fastest.
Arguments:
- tokens: bfloat16 [8, 4096, 768], P('shard', 'seq'), may hold values from -6 to 6
- cotangent: bfloat16 [8, 4096, 768], P('shard', 'seq'), may hold values from -6 to 6
- seg_ids: int32 [8, 4096], P('shard'), may hold values from 0 to 2, as said below
- norm_gain: bfloat16 [2, 768], P(None, 'shard'), may hold values from 0.5 to 1.5
- in_weight: bfloat16 [2, 768, 3328], P(None, 'shard'), may hold values from -0.21875 to 0.21875
- dt_weight: bfloat16 [2, 768, 24], P(None, 'shard'), may hold values from -0.21875 to 0.21875
- conv_weight: bfloat16 [2, 4, 1792], P(None, None, 'shard'), may hold values from -3 to 3
- conv_bias: bfloat16 [2, 1792], P(None, 'shard'), may hold values from -1.5 to 1.5
- dt_bias: float32 [2, 24], P(None, 'seq'), may hold values from -6.5 to -2.3
- a_log: float32 [2, 24], P(None, 'seq'), may hold values from 0 to 2.77
- skip: float32 [2, 24], P(None, 'seq'), may hold values from 0.5 to 1.5
- out_gain: bfloat16 [2, 1536], P(None, 'shard'), may hold values from 0.5 to 1.5
- out_weight: bfloat16 [2, 1536, 768], P(None, 'shard'), may hold values from -0.15625 to 0.15625
Outputs:
- activations: bfloat16 [8, 4096, 768], P('shard', 'seq')
- input_grad: float32 [8, 4096, 768], P('shard', 'seq')
- grad_norm_gain: float32 [2, 768], P(None, 'shard')
- grad_in_weight: float32 [2, 768, 3328], P(None, 'shard')
- grad_dt_weight: float32 [2, 768, 24], P(None, 'shard')
- grad_conv_weight: float32 [2, 4, 1792], P(None, None, 'shard')
- grad_conv_bias: float32 [2, 1792], P(None, 'shard')
- grad_dt_bias: float32 [2, 24], P(None, 'seq')
- grad_a_log: float32 [2, 24], P(None, 'seq')
- grad_skip: float32 [2, 24], P(None, 'seq')
- grad_out_gain: float32 [2, 1536], P(None, 'shard')
- grad_out_weight: float32 [2, 1536, 768], P(None, 'shard')
Inputs may be any that keep to these rules, and one draw needn't show every extreme that they name: `seg_ids`: in each stream the ids never fall; id 1 begins within the first 1024 tokens and ends within the last 1024.
All inputs are finite; a program needn't handle non-finite values.
Results may differ from a plain program's by a relative error of at most 0.02.
Values may be sent and summed in bfloat16 or wider, within the bound.
No kernel may reach another device: no remote copies, remote signals or barrier semaphores. Data moves between devices by JAX's collectives and lax.ppermute only.
A program may use at most 320 MiB of HBM per device.

v0:
```python
import jax
import jax.numpy as jnp
from jax import lax
from jax.sharding import PartitionSpec as P

CONV = 4
SPAN = 256
INNER = 1536


EPS = 1e-05
HIGH = lax.Precision.HIGHEST


def passed_along(block, axis, distance):
    devices = range(lax.axis_size(axis))
    route = [(i - distance, i) for i in devices if i - distance in devices]
    return lax.ppermute(block, axis, route)


def rms(value, gain):
    return value * lax.rsqrt(jnp.mean(value * value, axis=-1, keepdims=True) + EPS) * gain


def gated_out(mixed, gate_z, gain):
    return rms(mixed * jax.nn.silu(gate_z), gain)


def conv_taps(extended, weight, bias, prev_ids, own_ids):
    taps = weight.shape[0]
    count = own_ids.shape[0]
    total = bias + jnp.zeros((count, extended.shape[1]), extended.dtype)
    for tap in range(taps):
        valid = (prev_ids[tap : tap + count] == own_ids)[:, None].astype(extended.dtype)
        total = total + weight[tap] * extended[tap : tap + count] * valid
    return jax.nn.silu(total)


def block_terms(item):
    tags, running, out_rows, in_rows, driven, entering, before = item
    length = tags.shape[0]
    lower = jnp.arange(length)[:, None] >= jnp.arange(length)[None, :]
    same = ((tags[:, None] == tags[None, :]) & lower)[..., None]
    gap = running[:, None, :] - running[None, :, :]
    decay = jnp.where(same, jnp.exp(jnp.where(same, gap, 0.0)), 0.0)
    scores = jnp.einsum("qn,sn->qs", out_rows, in_rows, precision=HIGH)
    inside = jnp.einsum("qs,qsh,shp->qhp", scores, decay, driven, precision=HIGH)
    reach = jnp.where((tags == before)[:, None], jnp.exp(running), 0.0)
    across = reach[..., None] * jnp.einsum("qn,hpn->qhp", out_rows, entering, precision=HIGH)
    return inside + across


def mixing(x, dt_raw, bc, dt_bias, a_log, skip, ids):
    length, heads = dt_raw.shape
    width = x.shape[1] // heads
    state = bc.shape[1] // 2
    blocks = length // SPAN
    step = jax.nn.softplus(dt_raw + dt_bias)
    rate = step * -jnp.exp(a_log)
    xs = x.reshape(blocks, SPAN, heads, width)
    steps = step.reshape(blocks, SPAN, heads)
    inb = bc[:, :state].reshape(blocks, SPAN, state)
    outb = bc[:, state:].reshape(blocks, SPAN, state)
    tags = ids.reshape(blocks, SPAN)
    cumul = jnp.cumsum(rate.reshape(blocks, SPAN, heads), axis=1)
    driven = steps[..., None] * xs
    last = tags[:, -1:]
    toend = jnp.where((tags == last)[..., None], jnp.exp(cumul[:, -1:, :] - cumul), 0.0)
    local = jnp.einsum("bshp,bsn->bhpn", toend[..., None] * driven, inb, precision=HIGH)
    before = jnp.concatenate([jnp.full((1,), -1, jnp.int32), tags[:-1, -1]])
    factor = jnp.where((tags[:, -1] == before)[:, None], jnp.exp(cumul[:, -1, :]), 0.0)

    def advance(carry, item):
        scale, fresh = item
        return (scale[:, None, None] * carry + fresh, carry)

    start = jnp.zeros((heads, width, state), jnp.float32)
    _, entering = lax.scan(advance, start, (factor, local))
    result = lax.map(
        jax.checkpoint(block_terms), (tags, cumul, outb, inb, driven, entering, before)
    )
    result = result + skip[:, None] * xs
    return result.reshape(length, heads * width)


def body(
    tokens,
    cotangent,
    seg_ids,
    norm_gain,
    in_weight,
    dt_weight,
    conv_weight,
    conv_bias,
    dt_bias,
    a_log,
    skip,
    out_gain,
    out_weight,
):
    layers = in_weight.shape[0]
    place = lax.axis_index("seq")
    hidden = tokens[0].astype(jnp.float32)
    rows = hidden.shape[0]
    stream_ids = seg_ids[0]
    padded_ids = jnp.concatenate([jnp.full((CONV - 1,), -1, jnp.int32), stream_ids])
    prev_ids = lax.dynamic_slice_in_dim(padded_ids, place * rows, rows + CONV - 1)
    own_ids = prev_ids[CONV - 1 :]
    fetched = []
    saved = []
    for layer in range(layers):
        weights = (
            lax.all_gather(norm_gain[layer], "shard", axis=0, tiled=True),
            lax.all_gather(in_weight[layer], "shard", axis=0, tiled=True),
            lax.all_gather(dt_weight[layer], "shard", axis=0, tiled=True),
            lax.all_gather(conv_weight[layer], "shard", axis=1, tiled=True),
            lax.all_gather(conv_bias[layer], "shard", axis=0, tiled=True),
            lax.all_gather(out_gain[layer], "shard", axis=0, tiled=True),
            lax.all_gather(out_weight[layer], "shard", axis=0, tiled=True),
        )
        fetched.append(weights)
        gain_in, w_in, w_dt, w_conv, b_conv, gain_out, w_out = weights
        normed = rms(hidden, gain_in.astype(jnp.float32)).astype(jnp.bfloat16)
        project = jnp.dot(normed, w_in, preferred_element_type=jnp.float32)
        dt_raw = jnp.dot(normed, w_dt, preferred_element_type=jnp.float32).astype(jnp.bfloat16)
        gate_z = project[:, :INNER]
        conv_in = project[:, INNER:].astype(jnp.bfloat16)
        rim = passed_along(conv_in[rows - (CONV - 1) :], "seq", 1)
        extended = jnp.concatenate([rim, conv_in], axis=0)
        active = conv_taps(
            extended.astype(jnp.float32),
            w_conv.astype(jnp.float32),
            b_conv.astype(jnp.float32),
            prev_ids,
            own_ids,
        ).astype(jnp.bfloat16)
        x_part = active[:, :INNER]
        bc_part = active[:, INNER:]
        x_heads, dt_heads = (
            lax.all_to_all(x_part, "seq", split_axis=1, concat_axis=0, tiled=True),
            lax.all_to_all(dt_raw, "seq", split_axis=1, concat_axis=0, tiled=True),
        )
        bc_whole = lax.all_gather(bc_part, "seq", axis=0, tiled=True)
        mixed = mixing(
            x_heads.astype(jnp.float32),
            dt_heads.astype(jnp.float32),
            bc_whole.astype(jnp.float32),
            dt_bias[layer],
            a_log[layer],
            skip[layer],
            stream_ids,
        )
        back = lax.all_to_all(
            mixed.astype(jnp.bfloat16), "seq", split_axis=0, concat_axis=1, tiled=True
        )
        gated = gated_out(back.astype(jnp.float32), gate_z, gain_out.astype(jnp.float32)).astype(
            jnp.bfloat16
        )
        saved.append((hidden, normed, gate_z, extended, x_heads, dt_heads, bc_whole, back, gated))
        hidden = hidden + jnp.dot(gated, w_out, preferred_element_type=jnp.float32)
    activations = hidden.astype(jnp.bfloat16)[None]
    grad = cotangent[0].astype(jnp.float32)
    results = [None] * layers
    for layer in reversed(range(layers)):
        weights = (
            lax.all_gather(norm_gain[layer], "shard", axis=0, tiled=True),
            lax.all_gather(in_weight[layer], "shard", axis=0, tiled=True),
            lax.all_gather(dt_weight[layer], "shard", axis=0, tiled=True),
            lax.all_gather(conv_weight[layer], "shard", axis=1, tiled=True),
            lax.all_gather(conv_bias[layer], "shard", axis=0, tiled=True),
            lax.all_gather(out_gain[layer], "shard", axis=0, tiled=True),
            lax.all_gather(out_weight[layer], "shard", axis=0, tiled=True),
        )
        gain_in, w_in, w_dt, w_conv, b_conv, gain_out, w_out = weights
        h_in, normed, gate_z, extended, x_heads, dt_heads, bc_whole, back, gated = saved[layer]
        grad_low = grad.astype(jnp.bfloat16)
        d_w_out = jnp.einsum("ti,td->id", gated, grad_low, preferred_element_type=jnp.float32)
        d_gated = jnp.einsum("td,id->ti", grad_low, w_out, preferred_element_type=jnp.float32)
        _, gated_pull = jax.vjp(
            gated_out, back.astype(jnp.float32), gate_z, gain_out.astype(jnp.float32)
        )
        d_back, d_gate_z, d_gain_out = gated_pull(d_gated)
        d_heads = lax.all_to_all(
            d_back.astype(jnp.bfloat16), "seq", split_axis=1, concat_axis=0, tiled=True
        )

        def mix_local(x_value, dt_value, bc_value, bias_value, log_value, skip_value):
            return mixing(
                x_value, dt_value, bc_value, bias_value, log_value, skip_value, stream_ids
            )

        _, mix_pull = jax.vjp(
            mix_local,
            x_heads.astype(jnp.float32),
            dt_heads.astype(jnp.float32),
            bc_whole.astype(jnp.float32),
            dt_bias[layer],
            a_log[layer],
            skip[layer],
        )
        d_x_heads, d_dt_heads, d_bc_heads, d_dt_bias, d_a_log, d_skip = mix_pull(
            d_heads.astype(jnp.float32)
        )
        d_x_tok, d_dt_tok = (
            lax.all_to_all(
                d_x_heads.astype(jnp.bfloat16), "seq", split_axis=0, concat_axis=1, tiled=True
            ),
            lax.all_to_all(
                d_dt_heads.astype(jnp.bfloat16), "seq", split_axis=0, concat_axis=1, tiled=True
            ),
        )
        d_bc_tok = lax.psum_scatter(
            d_bc_heads.astype(jnp.bfloat16), "seq", scatter_dimension=0, tiled=True
        )
        d_active = jnp.concatenate([d_x_tok, d_bc_tok], axis=1).astype(jnp.float32)

        def conv_local(ext_value, weight_value, bias_value):
            return conv_taps(ext_value, weight_value, bias_value, prev_ids, own_ids)

        _, conv_pull = jax.vjp(
            conv_local,
            extended.astype(jnp.float32),
            w_conv.astype(jnp.float32),
            b_conv.astype(jnp.float32),
        )
        d_ext, d_w_conv, d_b_conv = conv_pull(d_active)
        spill = passed_along(d_ext[: CONV - 1], "seq", -1)
        tail = jnp.concatenate(
            [jnp.zeros((rows - (CONV - 1), d_ext.shape[1]), jnp.float32), spill], axis=0
        )
        d_conv_in = d_ext[CONV - 1 :] + tail
        d_project = jnp.concatenate([d_gate_z, d_conv_in], axis=1).astype(jnp.bfloat16)
        d_w_in = jnp.einsum("td,tp->dp", normed, d_project, preferred_element_type=jnp.float32)
        d_w_dt = jnp.einsum("td,th->dh", normed, d_dt_tok, preferred_element_type=jnp.float32)
        d_normed = jnp.einsum("tp,dp->td", d_project, w_in, preferred_element_type=jnp.float32)
        d_normed = d_normed + jnp.einsum(
            "th,dh->td", d_dt_tok, w_dt, preferred_element_type=jnp.float32
        )
        _, norm_pull = jax.vjp(rms, h_in, gain_in.astype(jnp.float32))
        d_hidden, d_gain_in = norm_pull(d_normed)
        grad = grad + d_hidden
        grad_terms = (d_gain_in, d_w_in, d_w_dt, d_w_conv, d_b_conv, d_gain_out, d_w_out)
        shares = (
            lax.psum_scatter(
                grad_terms[0].astype(jnp.bfloat16), "shard", scatter_dimension=0, tiled=True
            ).astype(jnp.float32),
            lax.psum_scatter(
                grad_terms[1].astype(jnp.bfloat16), "shard", scatter_dimension=0, tiled=True
            ).astype(jnp.float32),
            lax.psum_scatter(
                grad_terms[2].astype(jnp.bfloat16), "shard", scatter_dimension=0, tiled=True
            ).astype(jnp.float32),
            lax.psum_scatter(
                grad_terms[3].astype(jnp.bfloat16), "shard", scatter_dimension=1, tiled=True
            ).astype(jnp.float32),
            lax.psum_scatter(
                grad_terms[4].astype(jnp.bfloat16), "shard", scatter_dimension=0, tiled=True
            ).astype(jnp.float32),
            lax.psum_scatter(
                grad_terms[5].astype(jnp.bfloat16), "shard", scatter_dimension=0, tiled=True
            ).astype(jnp.float32),
            lax.psum_scatter(
                grad_terms[6].astype(jnp.bfloat16), "shard", scatter_dimension=0, tiled=True
            ).astype(jnp.float32),
        )
        shares = (
            lax.psum(shares[0].astype(jnp.bfloat16), "seq").astype(jnp.float32),
            lax.psum(shares[1].astype(jnp.bfloat16), "seq").astype(jnp.float32),
            lax.psum(shares[2].astype(jnp.bfloat16), "seq").astype(jnp.float32),
            lax.psum(shares[3].astype(jnp.bfloat16), "seq").astype(jnp.float32),
            lax.psum(shares[4].astype(jnp.bfloat16), "seq").astype(jnp.float32),
            lax.psum(shares[5].astype(jnp.bfloat16), "seq").astype(jnp.float32),
            lax.psum(shares[6].astype(jnp.bfloat16), "seq").astype(jnp.float32),
        )
        head_sums = lax.psum((d_dt_bias, d_a_log, d_skip), "shard")
        results[layer] = (shares, head_sums)
    g_norm = jnp.stack([item[0][0] for item in results])
    g_in = jnp.stack([item[0][1] for item in results])
    g_dt = jnp.stack([item[0][2] for item in results])
    g_conv = jnp.stack([item[0][3] for item in results])
    g_bias = jnp.stack([item[0][4] for item in results])
    g_step = jnp.stack([item[1][0] for item in results])
    g_decay = jnp.stack([item[1][1] for item in results])
    g_skip = jnp.stack([item[1][2] for item in results])
    g_gain = jnp.stack([item[0][5] for item in results])
    g_out = jnp.stack([item[0][6] for item in results])
    return (
        activations,
        grad[None],
        g_norm,
        g_in,
        g_dt,
        g_conv,
        g_bias,
        g_step,
        g_decay,
        g_skip,
        g_gain,
        g_out,
    )


def solution(mesh):
    return jax.shard_map(
        body,
        mesh=mesh,
        in_specs=(
            P("shard", "seq", None),
            P("shard", "seq", None),
            P("shard", None),
            P(None, "shard"),
            P(None, "shard", None),
            P(None, "shard", None),
            P(None, None, "shard"),
            P(None, "shard"),
            P(None, "seq"),
            P(None, "seq"),
            P(None, "seq"),
            P(None, "shard"),
            P(None, "shard", None),
        ),
        out_specs=(
            P("shard", "seq", None),
            P("shard", "seq", None),
            P(None, "shard"),
            P(None, "shard", None),
            P(None, "shard", None),
            P(None, None, "shard"),
            P(None, "shard"),
            P(None, "seq"),
            P(None, "seq"),
            P(None, "seq"),
            P(None, "shard"),
            P(None, "shard", None),
        ),
        check_vma=False,
    )
```

profile of v0, /device:TPU:0, one launch (start us, length us, event | category | flops | bytes accessed | tf_op | source)
XLA Modules:
  0.0 2386.1 jit_solution(14312479547566971051)
XLA Ops:
  15.7 32.1 %all-reduce.41 = (bf16[768]{0:T(1024)(128)(2,1)S(1)}, bf16[1792]{0:T(1024)(128)(2,1)S(1)}, bf16[1536]{0:T(1024)(128)(2,1)}, bf16[768]{0:T(1024)(128)(2,1)}, bf16...) all-reduce(bf16[768]{0:T(1024)(128)(2,1)S(1)} %dynamic-update-slice.1, ...), channel_id=4, replica_groups=mesh['seq'=4,'shard'=8] {'shard'}, use_global_device_ids=true, to_apply=%add.28 | all-reduce | flops 8192 | bytes 32768
  48.6 20.4 all-gather.1
  70.9 37.1 %slice_reduce_fusion.7 = (f32[1792]{0:T(1024)S(1)}, f32[1792]{0:T(1024)S(1)}, f32[1792]{0:T(1024)S(1)}, f32[1792]{0:T(1024)S(1)}) fusion(f32[1,4,1792]{1,0,2:T(1,128)S(1)} %convert_element_type.499), kind=kLoop, calls=%fused_computation.380 | loop fusion | bytes 57344 | tf_op jit(solution)/shard_map/slice | solution.py:35
  247.0 38.8 %while.162 = (s32[]{:T(128)}, f32[6,64,128]{2,1,0:T(8,128)S(1)}, f32[16,6,64,128]{3,2,1,0:T(8,128)}, f32[16,6]{1,0:T(8,128)}, f32[16,6,64,128]{3,2,1,0:T(8,128)}, /*index=5*/s32[]{:T(128)}, s32[]{:T(128)}) while((s32[]{:T(128)}, f32[6,64,128]{2,1,0:T(8,128)S(1)}, f32[16,6,64,128]{3,2,1,0:T(8,128)}, f32[16,6]{1,0:T(8,128)}, ...), condition=%wide.region_4.5_spmd.clone, body=%wide.region_3.4_spmd.clone.sunk | while | flops 196611 | bytes 983220 | solution.py:78
  291.5 159.1 %while.158 = (s32[]{:T(128)}, f32[16,256,6,64]{1,3,2,0:T(8,128)}, f32[16,256,128]{2,1,0:T(8,128)}, f32[16,256,128]{2,1,0:T(8,128)}, s32[16,256]{1,0:T(8,128)S(1)...) while((s32[]{:T(128)}, f32[16,256,6,64]{1,3,2,0:T(8,128)}, ...), condition=%wide.region_6.7_spmd, body=%wide.region_5.6_spmd.sunk | while | flops 555616000 | bytes 3652237 | solution.py:79
  555.8 37.3 %slice_reduce_fusion.3 = (f32[1792]{0:T(1024)S(1)}, f32[1792]{0:T(1024)S(1)}, f32[1792]{0:T(1024)S(1)}, f32[1792]{0:T(1024)S(1)}) fusion(f32[1,4,1792]{1,0,2:T(1,128)S(1)} %convert_element_type.503), kind=kLoop, calls=%fused_computation.376 | loop fusion | bytes 57344 | tf_op jit(solution)/shard_map/slice | solution.py:35
  737.0 38.8 %while.163 = (s32[]{:T(128)}, f32[6,64,128]{2,1,0:T(8,128)S(1)}, f32[16,6,64,128]{3,2,1,0:T(8,128)}, f32[16,6]{1,0:T(8,128)}, f32[16,6,64,128]{3,2,1,0:T(8,128)}, /*index=5*/s32[]{:T(128)}, s32[]{:T(128)}) while((s32[]{:T(128)}, f32[6,64,128]{2,1,0:T(8,128)S(1)}, f32[16,6,64,128]{3,2,1,0:T(8,128)}, f32[16,6]{1,0:T(8,128)}, ...), condition=%wide.region_12.13_spmd.clone, body=%wide.region_11.12_spmd.clone.sunk | while | flops 196611 | bytes 983220 | solution.py:78
  781.5 158.8 %while.159 = (s32[]{:T(128)}, f32[16,256,6,64]{1,3,2,0:T(8,128)}, f32[16,256,128]{2,1,0:T(8,128)}, f32[16,256,128]{2,1,0:T(8,128)}, s32[16,256]{1,0:T(8,128)S(1)...) while((s32[]{:T(128)}, f32[16,256,6,64]{1,3,2,0:T(8,128)}, ...), condition=%wide.region_14.15_spmd, body=%wide.region_13.14_spmd.sunk | while | flops 555616000 | bytes 3652237 | solution.py:79
  980.0 27.5 %all-to-all-done.5 = bf16[4,1024,384]{1,2,0:T(8,128)(2,1)} async-done(((bf16[4,1024,384]{1,2,0:T(8,128)(2,1)}), bf16[4,1024,384]{1,2,0:T(8,128)(2,1)}, u32[]{:S(2)}, u32[]{:S(2)}) %all-to-all-start.5) | async-done | bytes 3145760 | tf_op jit(solution)/shard_map/all_to_all | solution.py:153
  1054.7 58.1 %while.164 = (s32[]{:T(128)}, f32[6,64,128]{2,1,0:T(8,128)S(1)}, f32[16,6,64,128]{3,2,1,0:T(8,128)}, f32[16,6,1,1]{1,3,2,0:T(1,128)}, f32[16,6]{1,0:T(8,128)}, /...) while((s32[]{:T(128)}, f32[6,64,128]{2,1,0:T(8,128)S(1)}, f32[16,6,64,128]{3,2,1,0:T(8,128)}, ...), condition=%wide.region_20.22_spmd.clone, body=%wide.region_19.21_spmd.clone.sunk | while | flops 196611 | bytes 984256 | solution.py:78
  1144.7 216.9 %while.160 = (s32[]{:T(128)}, f32[16,256,6]{1,2,0:T(8,128)S(1)}, f32[16,256,128]{2,1,0:T(8,128)S(1)}, f32[16,256,128]{2,1,0:T(8,128)}, f32[16,256,6,64]{1,3,2,0:...) while((s32[]{:T(128)}, f32[16,256,6]{1,2,0:T(8,128)S(1)}, ...), condition=%wide.region_25.27_spmd, body=%wide.region_21.26_spmd.sunk | while | flops 1365414656 | bytes 9037025 | solution.py:79
  1363.3 30.1 %while.165 = (s32[]{:T(128)}, f32[6,64,128]{2,1,0:T(8,128)S(1)}, f32[16,6]{1,0:T(8,128)S(1)}, f32[16,6,64,128]{3,2,1,0:T(8,128)S(1)}, f32[16,6,64,128]{3,2,1,0:T...) while((s32[]{:T(128)}, f32[6,64,128]{2,1,0:T(8,128)S(1)}, ...), condition=%wide.region_28.30_spmd.clone, body=%wide.region_26.29_spmd.clone.sunk | while | flops 294910 | bytes 1179940 | solution.py:78
  1408.4 19.8 multiply_reduce_fusion.13
  1481.4 22.9 all-to-all-done.7
  1507.6 20.5 multiply_reduce_fusion.3
  1594.0 58.3 %while.166 = (s32[]{:T(128)}, f32[6,64,128]{2,1,0:T(8,128)S(1)}, f32[16,6,64,128]{3,2,1,0:T(8,128)}, f32[16,6,1,1]{1,3,2,0:T(1,128)}, f32[16,6]{1,0:T(8,128)}, /...) while((s32[]{:T(128)}, f32[6,64,128]{2,1,0:T(8,128)S(1)}, f32[16,6,64,128]{3,2,1,0:T(8,128)}, ...), condition=%wide.region_40.42_spmd.clone, body=%wide.region_39.41_spmd.clone.sunk | while | flops 196611 | bytes 984256 | solution.py:78
  1684.3 216.9 %while.161 = (s32[]{:T(128)}, f32[16,256,6]{1,2,0:T(8,128)S(1)}, f32[16,256,128]{2,1,0:T(8,128)S(1)}, f32[16,256,128]{2,1,0:T(8,128)}, f32[16,256,6,64]{1,3,2,0:...) while((s32[]{:T(128)}, f32[16,256,6]{1,2,0:T(8,128)S(1)}, ...), condition=%wide.region_45.47_spmd, body=%wide.region_41.46_spmd.sunk | while | flops 1365414656 | bytes 9037025 | solution.py:79
  1902.9 30.1 %while.167 = (s32[]{:T(128)}, f32[6,64,128]{2,1,0:T(8,128)S(1)}, f32[16,6]{1,0:T(8,128)S(1)}, f32[16,6,64,128]{3,2,1,0:T(8,128)S(1)}, f32[16,6,64,128]{3,2,1,0:T...) while((s32[]{:T(128)}, f32[6,64,128]{2,1,0:T(8,128)S(1)}, ...), condition=%wide.region_48.50_spmd.clone, body=%wide.region_46.49_spmd.clone.sunk | while | flops 294910 | bytes 1179940 | solution.py:78
  1950.8 19.9 multiply_reduce_fusion.10
  2039.1 36.7 %all_to_all.168 = bf16[4,1024,384]{1,2,0:T(8,128)(2,1)} all-to-all(bf16[4,1024,384]{1,2,0:T(8,128)(2,1)S(1)} %copy.677), channel_id=1, replica_groups=mesh['seq'=4,'shard'=8] {'seq'}, dimensions={0} | all-to-all | bytes 6291456 | tf_op jit(solution)/shard_map/all_to_all | solution.py:205
  2171.7 42.4 %reduce-scatter.25.cloned.1.call-done = bf16[96,3328]{1,0:T(8,128)(2,1)} async-done(((bf16[768,3328]{1,0:T(8,128)(2,1)}), bf16[96,3328]{1,0:T(8,128)(2,1)}) %reduce-scatter.25.cloned.1.call-update) | async-done | bytes 638992 | tf_op jit(solution)/shard_map/reduce_scatter | solution.py:247
  2214.1 59.1 %reduce-scatter.23.cloned.1.call-done = bf16[96,3328]{1,0:T(8,128)(2,1)} async-done(((bf16[768,3328]{1,0:T(8,128)(2,1)}), bf16[96,3328]{1,0:T(8,128)(2,1)}) %reduce-scatter.23.cloned.1.call-update) | async-done | bytes 638992 | tf_op jit(solution)/shard_map/reduce_scatter | solution.py:247
  2286.6 26.0 %all-reduce.40 = (bf16[768]{0:T(1024)(128)(2,1)S(1)}, bf16[768]{0:T(1024)(128)(2,1)S(1)}, bf16[1792]{0:T(1024)(128)(2,1)S(1)}, bf16[1792]{0:T(1024)(128)(2,1)S(1...) all-reduce(bf16[768]{0:T(1024)(128)(2,1)S(1)} %copy-done.168, ...), channel_id=19, replica_groups=mesh['seq'=4,'shard'=8] {'shard'}, use_global_device_ids=true, to_apply=%region_60.62.clone | all-reduce | flops 8192 | bytes 32768
  2333.7 40.6 %all-reduce.46.cloned.1.call-done = (bf16[1,96,3328]{2,1,0:T(8,128)(2,1)}, bf16[1,96,3328]{2,1,0:T(8,128)(2,1)}, bf16[1,192,768]{2,1,0:T(8,128)(2,1)}, bf16[1,192,768]{2,1,0:T(8,128)(2,1)}) async-done(((bf16[1,96,3328]{2,1,0:T(8,128)(2,1)}, bf16[1,96,3328]{2,1,0:T(8,128)(2,1)}, bf16[1,192,768]{2,1,0:T(8,128)(2,1)}, bf16[1,192,768]{2,1,0:T(8,128)(2,1)}), (bf16[1,96,3328]{2,1,0:T(8,128)(2,1)}, ...) | async-done | bytes 1867792 | tf_op jit(solution)/shard_map/psum | solution.py:268
  (2009 shorter events, 1915.3 us)
Async XLA Ops:
  7.2 100.9 %all-gather.25.cloned.1.call-start = ((), (), s32[]{:S(2)}) async-start(), calls=%async_computation.30 | async-start | bytes 5750784 | tf_op jit(solution)/shard_map/all_gather | solution.py:114
  9.7 222.6 %all-gather.21.cloned.1.call-start = ((), (), s32[]{:S(2)}) async-start(), calls=%async_computation.22 | async-start | bytes 2621440 | tf_op jit(solution)/shard_map/all_gather | solution.py:143
  135.6 397.2 %all-gather.27.cloned.1.call-start = ((), (), s32[]{:S(2)}) async-start(), calls=%async_computation.31 | async-start | bytes 2654208 | tf_op jit(solution)/shard_map/all_gather | solution.py:119
  157.6 383.3 %all-gather.29.cloned.1.call-start = ((), (), s32[]{:S(2)}) async-start(), calls=%async_computation.32 | async-start | bytes 5750784 | tf_op jit(solution)/shard_map/all_gather | solution.py:114
  166.1 40.8 %all-to-all-start.1 = ((bf16[1024,4,384]{0,2,1:T(8,128)(2,1)}), bf16[1024,4,384]{0,2,1:T(8,128)(2,1)S(1)}, u32[]{:S(2)}, u32[]{:S(2)}) async-start(bf16[1024,4,384]{0,2,1:T(8,128)(2,1)} %bitcast.840), calls=%async_computation.1 | async-start | bytes 6291456 | tf_op jit(solution)/shard_map/all_to_all | solution.py:140
  472.0 41.2 %all-to-all-start.2 = ((bf16[4,1024,384]{1,2,0:T(8,128)(2,1)}), bf16[4,1024,384]{1,2,0:T(8,128)(2,1)}, u32[]{:S(2)}, u32[]{:S(2)}) async-start(bf16[4,1024,384]{1,2,0:T(8,128)(2,1)} %copy.602), calls=%async_computation.2 | async-start | bytes 6291456 | tf_op jit(solution)/shard_map/all_to_all | solution.py:153
  476.7 245.7 %all-gather.23.cloned.1.call-start = ((), (), s32[]{:S(2)}) async-start(), calls=%async_computation.23 | async-start | bytes 2621440 | tf_op jit(solution)/shard_map/all_gather | solution.py:143
  552.5 41.0 %collective-permute-start.1 = (bf16[3,1792]{1,0:T(4,128)(2,1)S(1)}, bf16[3,1792]{1,0:T(4,128)(2,1)S(1)}, u32[]{:S(2)}, u32[]{:S(2)}) collective-permute-start(bf16[3,1792]{1,0:T(4,128)(2,1)S(1)} %slice.414), channel_id=1, source_target_pairs={{0,8},{8,16},{16,24},{1,9},{9,17},{17,25},{2,10},{10,18},{18,26},{... | collective-permute-start | bytes 32264 | tf_op jit(solution)/shard_map/ppermute | solution.py:18
  605.2 421.9 %all-gather.31.cloned.1.call-start = ((), (), s32[]{:S(2)}) async-start(), calls=%async_computation.33 | async-start | bytes 2654208 | tf_op jit(solution)/shard_map/all_gather | solution.py:119
  633.7 63.1 %all-to-all-start.4 = ((bf16[1024,4,384]{0,2,1:T(8,128)(2,1)}), bf16[1024,4,384]{0,2,1:T(8,128)(2,1)S(1)}, u32[]{:S(2)}, u32[]{:S(2)}) async-start(bf16[1024,4,384]{0,2,1:T(8,128)(2,1)} %bitcast.837), calls=%async_computation.4 | async-start | bytes 6291456 | tf_op jit(solution)/shard_map/all_to_all | solution.py:140
  965.9 41.6 %all-to-all-start.5 = ((bf16[4,1024,384]{1,2,0:T(8,128)(2,1)}), bf16[4,1024,384]{1,2,0:T(8,128)(2,1)}, u32[]{:S(2)}, u32[]{:S(2)}) async-start(bf16[4,1024,384]{1,2,0:T(8,128)(2,1)} %copy.626), calls=%async_computation.5 | async-start | bytes 6291456 | tf_op jit(solution)/shard_map/all_to_all | solution.py:153
  1048.3 64.5 %all-to-all-start.6 = ((bf16[1024,4,384]{0,2,1:T(8,128)(2,1)}), bf16[1024,4,384]{0,2,1:T(8,128)(2,1)S(1)}, u32[]{:S(2)}, u32[]{:S(2)}) async-start(bf16[1024,4,384]{0,2,1:T(8,128)(2,1)} %bitcast.838), calls=%async_computation.6 | async-start | bytes 6291456 | tf_op jit(solution)/shard_map/all_to_all | solution.py:183
  1052.0 455.5 %reduce-scatter.19.cloned.1.call-start = ((), (), s32[]{:S(2)}) async-start(), calls=%async_computation.24 | async-start | bytes 2621440 | tf_op jit(solution)/shard_map/reduce_scatter | solution.py:212
  1586.4 65.9 %all-to-all-start.9 = ((bf16[1024,4,384]{0,2,1:T(8,128)(2,1)}), bf16[1024,4,384]{0,2,1:T(8,128)(2,1)S(1)}, u32[]{:S(2)}, u32[]{:S(2)}) async-start(bf16[1024,4,384]{0,2,1:T(8,128)(2,1)} %bitcast.839), calls=%async_computation.10 | async-start | bytes 6291456 | tf_op jit(solution)/shard_map/all_to_all | solution.py:183
  1591.3 487.8 %reduce-scatter.21.cloned.1.call-start = ((), (), s32[]{:S(2)}) async-start(), calls=%async_computation.25 | async-start | bytes 2621440 | tf_op jit(solution)/shard_map/reduce_scatter | solution.py:212
  1947.7 201.1 %reduce-scatter.33.cloned.1.call-start = ((), (), s32[]{:S(2)}) async-start(), calls=%async_computation.35 | async-start | bytes 221184
  1994.6 155.0 %reduce-scatter.37.cloned.1.call-start = ((), (), s32[]{:S(2)}) async-start(), calls=%async_computation.37 | async-start | bytes 516096
  1995.7 175.1 %reduce-scatter.31.cloned.1.call-start = ((), (), s32[]{:S(2)}) async-start(), calls=%async_computation.34 | async-start | bytes 221184
  2002.4 169.2 %reduce-scatter.29.cloned.1.call-start = ((), (), s32[]{:S(2)}) async-start(), calls=%async_computation.29 | async-start | bytes 2654208 | tf_op jit(solution)/shard_map/reduce_scatter | solution.py:262
  2010.0 161.6 %reduce-scatter.27.cloned.1.call-start = ((), (), s32[]{:S(2)}) async-start(), calls=%async_computation.28 | async-start | bytes 2654208 | tf_op jit(solution)/shard_map/reduce_scatter | solution.py:262
  2018.4 195.7 %reduce-scatter.25.cloned.1.call-start = ((), (), s32[]{:S(2)}) async-start(), calls=%async_computation.27 | async-start | bytes 5750784 | tf_op jit(solution)/shard_map/reduce_scatter | solution.py:247
  2028.6 244.6 %reduce-scatter.23.cloned.1.call-start = ((), (), s32[]{:S(2)}) async-start(), calls=%async_computation.26 | async-start | bytes 5750784 | tf_op jit(solution)/shard_map/reduce_scatter | solution.py:247
  2132.1 181.0 %reduce-scatter.35.cloned.1.call-start = ((), (), s32[]{:S(2)}) async-start(), calls=%async_computation.36 | async-start | bytes 516096
  2170.1 204.1 %all-reduce.46.cloned.1.call-start = ((), (), s32[]{:S(2)}) async-start(), calls=%async_computation.38 | async-start | bytes 3735552 | tf_op jit(solution)/shard_map/psum | solution.py:268
  (194 other events, 3825.9 us)
Sparse Core Ops, SparseCore 0:
  10.3 65.3 all-gather.24
  135.7 36.7 all-gather.20
  174.1 46.2 all-gather.26
  222.5 54.0 all-gather.28
  605.3 34.9 all-gather.22
  641.8 30.9 all-gather.30
  1408.4 35.4 reduce-scatter.18
  1947.8 35.5 reduce-scatter.20
  1985.7 30.2 reduce-scatter.32
  2018.8 29.0 reduce-scatter.36
  2050.1 28.4 reduce-scatter.30
  2081.4 34.4 reduce-scatter.28
  2118.3 35.4 reduce-scatter.26
  2156.1 57.9 reduce-scatter.24
  2216.2 56.8 reduce-scatter.22
  2276.0 29.1 reduce-scatter.34
  2308.5 65.7 all-reduce.45
where the time goes:
time: 2410 us; the launch traced here: 2390 us
  matrix products  685 us (28%)
  local copies, waits for them, and re-layouts  680 us (28%)
  other arithmetic  518 us (21%)
  waiting for transfers between devices  227 us (9%)
  blocking collectives  190 us (8%)
  starting transfers between devices  58.2 us (2%)
    dot_general x96, matrix products, block_terms(): jnp.einsum('qs,qsh,shp->qhp', scores, decay, driven, precision=HIGH)  235 us
    dot_general x128, matrix products, block_terms(): jnp.einsum('qn,hpn->qhp', out_rows, entering, precision=HIGH)  126 us
    dot_general x128, matrix products, block_terms(): scores = jnp.einsum('qn,sn->qs', out_rows, in_rows, precision=HIGH)  107 us
    dynamic_slice x160, local copies, waits for them, and re-layouts, mixing(): lax.map(jax.checkpoint(block_terms), (tags, cumul, outb, inb, driven, ent...  107 us
    dot_general x8, matrix products, mixing(): jnp.einsum('bshp,bsn->bhpn', toend[..., None] * driven, inb, precision=HIGH)  103 us
    reduce_scatter x2, waiting for transfers between devices, body(): lax.psum_scatter(grad_terms[1].astype(jnp.bfloat16), 'shard', scatter_dim...  101 us
    another operation x23, other arithmetic  90.1 us
    slice x2, local copies, waits for them, and re-layouts, conv_taps(): total = total + weight[tap] * extended[tap:tap + count] * valid  74.4 us
  transfers between devices with their start and end apart: 32, of which 9 were waited for; matrix products, arithmetic and copies ran while one was open for 48% of the time, Pallas kernels for 0%

commit v1 on v0

v1 whole, which is shorter than its diff:
```python
import functools

import jax
import jax.numpy as jnp
from jax import lax
from jax.experimental import pallas as pl
from jax.experimental.pallas import tpu as pltpu
from jax.sharding import PartitionSpec as P

CONV = 4
EPS = 1e-05
CHUNK = 128
EDGE = 16
LOG2E = 1.4426950408889634
FAR = -1e30
BF = jnp.bfloat16
F32 = jnp.float32
HIGH = lax.Precision.HIGHEST
VMEM = 56 * 1024 * 1024


def dot(left, right, left_dim, right_dim, precision=None):
    return lax.dot_general(
        left,
        right,
        (((left_dim,), (right_dim,)), ((), ())),
        precision=precision,
        preferred_element_type=F32,
    )


def col_sum(value):
    return jnp.sum(value, axis=0, keepdims=True)


def sigmoid(value):
    return 0.5 * jnp.tanh(0.5 * value) + 0.5


def per_head(rows, first, count, width):
    return jnp.concatenate(
        [jnp.broadcast_to(rows[k : k + 1], (width, rows.shape[1])) for k in range(first, first + count)]
    )


def iotas():
    down = lax.broadcasted_iota(jnp.int32, (CHUNK, CHUNK), 0)
    across = lax.broadcasted_iota(jnp.int32, (CHUNK, CHUNK), 1)
    return down, across


def step_sizes(raw, bias, log_rate):
    shifted = raw + bias
    step = jnp.maximum(shifted, 0.0) + jnp.log1p(jnp.exp(-jnp.abs(shifted)))
    rate = -jnp.exp(log_rate)
    down, across = iotas()
    upto = (down <= across).astype(F32)
    running = dot(step * (rate * LOG2E), upto, 1, 0, HIGH)
    return shifted, step, rate, running


def pair_mask(info):
    down, across = iotas()
    tags = info[0:8]
    column = jnp.transpose(tags)[:, 0:1]
    reaches = (column == info[0:1]) & (down <= across)
    return jnp.where(reaches, 0.0, FAR)


def chunk_factors(running, info):
    total = running[:, CHUNK - 1 : CHUNK]
    reach = jnp.exp2(running) * info[7:8]
    toend = jnp.exp2(total - running) * info[8:9]
    whole = jnp.exp2(jnp.broadcast_to(total, running.shape)) * info[9:10]
    return reach, toend, whole


def shape_of(heads, inner, state):
    width = inner // heads
    return width, CHUNK // width, inner // CHUNK


def conv_block(cur, prev, taps, bias, info):
    lane = lax.broadcasted_iota(jnp.int32, cur.shape, 1)
    total = bias + taps[CONV - 1] * cur
    for k in range(1, CONV):
        mixed = jnp.where(lane >= CHUNK - k, prev, cur)
        total = total + taps[CONV - 1 - k] * (pltpu.roll(mixed, k, 1) * info[k : k + 1])
    return total


def scan_kernel(
    heads,
    inner,
    qd_ref,
    halo_ref,
    taps_ref,
    bias_ref,
    log_ref,
    skip_ref,
    info_ref,
    xa_ref,
    slope_ref,
    part_ref,
    enter_ref,
    prefix_ref,
    reach_ref,
    pack_ref,
    carry,
    wide,
    state,
    prefix,
):
    step_at = pl.program_id(0)
    last = pl.num_programs(0) - 1
    channels = xa_ref.shape[0]
    padded = bias_ref.shape[0]
    n_state = (channels - inner) // 2
    width, group, blocks = shape_of(heads, inner, n_state)

    @pl.when(step_at == 0)
    def _():
        for at in range(0, channels, CHUNK):
            rows = halo_ref[:, at : at + CHUNK].astype(F32)
            rows = jnp.concatenate([jnp.zeros((CHUNK - EDGE, CHUNK), F32), rows])
            carry[at : at + CHUNK, :] = jnp.transpose(rows).astype(BF)
            for k in range(CONV + 1):
                wide[k, at : at + CHUNK, :] = jnp.broadcast_to(
                    taps_ref[at : at + CHUNK, k : k + 1], (CHUNK, CHUNK)
                )
        state[...] = jnp.zeros_like(state)
        prefix[...] = jnp.ones_like(prefix)

    info = info_ref[...]
    raw = qd_ref[channels : channels + padded, :].astype(F32)
    _, step, _, running = step_sizes(raw, bias_ref[...], log_ref[...])
    reach, toend, whole = chunk_factors(running, info)
    before = prefix[...]
    prefix_ref[0] = before
    reach_ref[...] = before * reach
    prefix[...] = before * whole
    column = jnp.transpose(running)
    mask = pair_mask(info)
    skip = skip_ref[...]

    def active(at):
        rows = pl.ds(at, CHUNK)
        pre = conv_block(
            qd_ref[rows, :].astype(F32),
            carry[rows, :].astype(F32),
            [wide[k, rows, :] for k in range(CONV)],
            wide[CONV, rows, :],
            info,
        )
        gate = sigmoid(pre)
        value = (pre * gate).astype(BF)
        xa_ref[rows, :] = value
        slope_ref[rows, :] = (gate * (1.0 + pre * (1.0 - gate))).astype(BF)
        return value

    in_t = active(inner)
    out_t = active(inner + n_state)
    scores = dot(in_t, out_t, 0, 0)
    for block in range(blocks):
        at = block * CHUNK
        rows = pl.ds(at, CHUNK)
        x = active(at).astype(F32)
        first = block * group
        entering = state[rows, :]
        entering_low = entering.astype(BF)
        enter_ref[0, rows, :] = entering_low
        driven = x * per_head(step, first, group, width)
        total = x * per_head(skip, first, group, width) + per_head(
            reach, first, group, width
        ) * dot(entering_low, out_t, 1, 0)
        driven_low = driven.astype(BF)
        inside = []
        for k in range(group):
            head = first + k
            gap = (running[head : head + 1] + mask) - column[:, head : head + 1]
            mixer = (scores * jnp.exp2(gap)).astype(BF)
            inside.append(dot(driven_low[k * width : (k + 1) * width], mixer, 1, 0))
        part_ref[rows, :] = (total + jnp.concatenate(inside)).astype(BF)
        weighted = (driven * per_head(toend, first, group, width)).astype(BF)
        state[rows, :] = entering * per_head(whole, first, group, width) + dot(weighted, in_t, 1, 1)
    carry[...] = qd_ref[0:channels, :]

    @pl.when(step_at == last)
    def _():
        pack_ref[0:inner, :] = state[...].astype(BF)
        factor = prefix[...]
        high = factor.astype(BF)
        pack_ref[inner : inner + padded, :] = high
        pack_ref[inner + padded : inner + 2 * padded, :] = (factor - high.astype(F32)).astype(BF)


def lane_block(rows):
    return pl.BlockSpec((rows, CHUNK), lambda i: (0, i))


def whole_block(shape):
    return pl.BlockSpec(shape, lambda i: (0,) * len(shape))


def scan(qd, halo, taps, bias, log_rate, skip, info, heads, inner):
    length = qd.shape[1]
    padded = bias.shape[0]
    channels = qd.shape[0] - padded
    steps = length // CHUNK
    return pl.pallas_call(
        functools.partial(scan_kernel, heads, inner),
        grid=(steps,),
        in_specs=[
            lane_block(qd.shape[0]),
            whole_block(halo.shape),
            whole_block(taps.shape),
            whole_block(bias.shape),
            whole_block(bias.shape),
            whole_block(bias.shape),
            lane_block(info.shape[0]),
        ],
        out_specs=[
            lane_block(channels),
            lane_block(channels),
            lane_block(inner),
            pl.BlockSpec((1, inner, CHUNK), lambda i: (i, 0, 0)),
            pl.BlockSpec((1, padded, CHUNK), lambda i: (i, 0, 0)),
            lane_block(padded),
            whole_block((inner + 2 * padded, CHUNK)),
        ],
        out_shape=[
            jax.ShapeDtypeStruct((channels, length), BF),
            jax.ShapeDtypeStruct((channels, length), BF),
            jax.ShapeDtypeStruct((inner, length), BF),
            jax.ShapeDtypeStruct((steps, inner, CHUNK), BF),
            jax.ShapeDtypeStruct((steps, padded, CHUNK), F32),
            jax.ShapeDtypeStruct((padded, length), F32),
            jax.ShapeDtypeStruct((inner + 2 * padded, CHUNK), BF),
        ],
        scratch_shapes=[
            pltpu.VMEM((channels, CHUNK), BF),
            pltpu.VMEM((CONV + 1, channels, CHUNK), F32),
            pltpu.VMEM((inner, CHUNK), F32),
            pltpu.VMEM((padded, CHUNK), F32),
        ],
        compiler_params=pltpu.CompilerParams(vmem_limit_bytes=VMEM),
        name="scan_forward",
    )(qd, halo, taps, bias, log_rate, skip, info)


def joined(packs, at, inner, heads, padded):
    width = inner // heads
    first = at // width
    count = CHUNK // width
    total = None
    for pack in reversed(packs):
        own = pack[at : at + CHUNK, :].astype(F32)
        if total is not None:
            high = pack[inner : inner + padded, :].astype(F32)
            low = pack[inner + padded : inner + 2 * padded, :].astype(F32)
            own = own + per_head(high + low, first, count, width) * total
        total = own
    return total


def norm_kernel(heads, n_packs, *refs):
    packs = refs[:n_packs]
    part_ref, z_ref, out_ref, reach_ref, gain_ref, yb_ref, n_ref, enter_ref, value = refs[n_packs:]
    inner = part_ref.shape[0]
    padded = reach_ref.shape[0]
    width = inner // heads
    count = CHUNK // width

    @pl.when(pl.program_id(0) == 0)
    def _():
        for at in range(0, inner, CHUNK):
            if n_packs:
                enter_ref[at : at + CHUNK, :] = joined(packs, at, inner, heads, padded).astype(BF)
            else:
                enter_ref[at : at + CHUNK, :] = jnp.zeros((CHUNK, CHUNK), BF)

    reach = reach_ref[...]
    out_t = out_ref[...]
    squares = jnp.zeros((CHUNK, CHUNK), F32)
    for at in range(0, inner, CHUNK):
        rows = pl.ds(at, CHUNK)
        late = per_head(reach, at // width, count, width) * dot(enter_ref[rows, :], out_t, 1, 0)
        mixed = (part_ref[rows, :].astype(F32) + late).astype(BF)
        yb_ref[rows, :] = mixed
        z = z_ref[rows, :].astype(F32)
        gated = mixed.astype(F32) * (z * sigmoid(z))
        value[rows, :] = gated
        squares = squares + gated * gated
    scale = lax.rsqrt(col_sum(squares) * (1.0 / inner) + EPS)
    for at in range(0, inner, CHUNK):
        rows = pl.ds(at, CHUNK)
        n_ref[rows, :] = (value[rows, :] * scale * gain_ref[rows, :]).astype(BF)


def gated_norm(packs, part, z, xa, reach, gain, heads):
    inner, length = part.shape
    channels = xa.shape[0]
    n_state = (channels - inner) // 2
    out_at = (channels - n_state) // n_state
    return pl.pallas_call(
        functools.partial(norm_kernel, heads, len(packs)),
        grid=(length // CHUNK,),
        in_specs=[whole_block(pack.shape) for pack in packs]
        + [
            lane_block(inner),
            lane_block(inner),
            pl.BlockSpec((n_state, CHUNK), lambda i: (out_at, i)),
            lane_block(reach.shape[0]),
            whole_block(gain.shape),
        ],
        out_specs=[lane_block(inner), lane_block(inner), whole_block((inner, n_state))],
        out_shape=[
            jax.ShapeDtypeStruct((inner, length), BF),
            jax.ShapeDtypeStruct((inner, length), BF),
            jax.ShapeDtypeStruct((inner, n_state), BF),
        ],
        scratch_shapes=[pltpu.VMEM((inner, CHUNK), F32)],
        compiler_params=pltpu.CompilerParams(vmem_limit_bytes=VMEM),
        name="gated_norm_forward",
    )(*packs, part, z, xa, reach, gain)


def norm_back_kernel(
    heads,
    go_ref,
    weight_ref,
    yb_ref,
    z_ref,
    out_ref,
    reach_ref,
    gain_ref,
    pack_in_ref,
    dy_ref,
    dz_ref,
    dgain_ref,
    pack_ref,
    value,
    dn,
    dgain,
    adjoint,
):
    step_at = pl.program_id(0)
    last = pl.num_programs(0) - 1
    inner = yb_ref.shape[0]
    padded = reach_ref.shape[0]
    width = inner // heads
    count = CHUNK // width

    @pl.when(step_at == 0)
    def _():
        dgain[...] = jnp.zeros_like(dgain)
        adjoint[...] = jnp.zeros_like(adjoint)

    go = go_ref[...]
    squares = jnp.zeros((CHUNK, CHUNK), F32)
    crosses = jnp.zeros((CHUNK, CHUNK), F32)
    for at in range(0, inner, CHUNK):
        rows = pl.ds(at, CHUNK)
        d_norm = dot(weight_ref[rows, :], go, 1, 0)
        z = z_ref[rows, :].astype(F32)
        gated = yb_ref[rows, :].astype(F32) * (z * sigmoid(z))
        dn[rows, :] = d_norm
        value[rows, :] = gated
        squares = squares + gated * gated
        crosses = crosses + gated * (d_norm * gain_ref[rows, :])
    scale = lax.rsqrt(col_sum(squares) * (1.0 / inner) + EPS)
    pull = col_sum(crosses) * (1.0 / inner) * scale * scale * scale
    reach = reach_ref[...]
    out_t = out_ref[...]
    for at in range(0, inner, CHUNK):
        rows = pl.ds(at, CHUNK)
        gated = value[rows, :]
        d_norm = dn[rows, :]
        dgain[rows, :] += d_norm * gated * scale
        d_gated = d_norm * gain_ref[rows, :] * scale - gated * pull
        z = z_ref[rows, :].astype(F32)
        gate = sigmoid(z)
        dy = (d_gated * (z * gate)).astype(BF)
        dy_ref[rows, :] = dy
        d_silu = d_gated * yb_ref[rows, :].astype(F32)
        dz_ref[rows, :] = (d_silu * (gate * (1.0 + z * (1.0 - gate)))).astype(BF)
        far = (dy.astype(F32) * per_head(reach, at // width, count, width)).astype(BF)
        adjoint[rows, :] += dot(far, out_t, 1, 1)

    @pl.when(step_at == last)
    def _():
        pack_ref[0:inner, :] = adjoint[...].astype(BF)
        pack_ref[inner : inner + 2 * padded, :] = pack_in_ref[inner : inner + 2 * padded, :]
        for at in range(0, inner, CHUNK):
            dgain_ref[at : at + CHUNK, :] = jnp.sum(
                dgain[at : at + CHUNK, :], axis=1, keepdims=True
            )


def gated_norm_back(go, weight, yb, z, xa, reach, gain, pack, heads):
    inner, length = yb.shape
    channels = xa.shape[0]
    n_state = (channels - inner) // 2
    out_at = (channels - n_state) // n_state
    return pl.pallas_call(
        functools.partial(norm_back_kernel, heads),
        grid=(length // CHUNK,),
        in_specs=[
            lane_block(go.shape[0]),
            whole_block(weight.shape),
            lane_block(inner),
            lane_block(inner),
            pl.BlockSpec((n_state, CHUNK), lambda i: (out_at, i)),
            lane_block(reach.shape[0]),
            whole_block(gain.shape),
            whole_block(pack.shape),
        ],
        out_specs=[
            lane_block(inner),
            lane_block(inner),
            whole_block((inner, 1)),
            whole_block(pack.shape),
        ],
        out_shape=[
            jax.ShapeDtypeStruct((inner, length), BF),
            jax.ShapeDtypeStruct((inner, length), BF),
            jax.ShapeDtypeStruct((inner, 1), F32),
            jax.ShapeDtypeStruct(pack.shape, BF),
        ],
        scratch_shapes=[
            pltpu.VMEM((inner, CHUNK), F32),
            pltpu.VMEM((inner, CHUNK), F32),
            pltpu.VMEM((inner, CHUNK), F32),
            pltpu.VMEM((inner, CHUNK), F32),
        ],
        compiler_params=pltpu.CompilerParams(vmem_limit_bytes=VMEM),
        name="gated_norm_backward",
    )(go, weight, yb, z, xa, reach, gain, pack)


def scan_back_kernel(heads, n_packs, *refs):
    packs = refs[:n_packs]
    (
        xa_ref,
        slope_ref,
        qd_ref,
        dy_ref,
        enter_ref,
        device_ref,
        prefix_ref,
        taps_ref,
        bias_ref,
        log_ref,
        skip_ref,
        info_ref,
        dqd_ref,
        dconv_ref,
        dhead_ref,
        edge_ref,
        wide,
        adjoint,
        later,
        dtaps,
        dhead,
        far_s,
        far_dy,
        far_g,
        far_x,
        rows_total,
        rows_leave,
        rows_direct,
        rows_skip,
        rows_pass,
        d_scores,
    ) = refs[n_packs:]
    step_at = pl.program_id(0)
    last = pl.num_programs(0) - 1
    channels = xa_ref.shape[0]
    inner = dy_ref.shape[0]
    padded = bias_ref.shape[0]
    n_state = (channels - inner) // 2
    width, group, blocks = shape_of(heads, inner, n_state)

    @pl.when(step_at == 0)
    def _():
        for at in range(0, channels, CHUNK):
            for k in range(CONV):
                wide[k, at : at + CHUNK, :] = jnp.broadcast_to(
                    taps_ref[at : at + CHUNK, k : k + 1], (CHUNK, CHUNK)
                )
        for at in range(0, inner, CHUNK):
            if n_packs:
                adjoint[at : at + CHUNK, :] = joined(packs, at, inner, heads, padded)
            else:
                adjoint[at : at + CHUNK, :] = jnp.zeros((CHUNK, CHUNK), F32)
        later[...] = jnp.zeros_like(later)
        dtaps[...] = jnp.zeros_like(dtaps)
        dhead[...] = jnp.zeros_like(dhead)
        for ref in (rows_total, rows_leave, rows_direct, rows_skip, rows_pass):
            ref[...] = jnp.zeros_like(ref)

    info = info_ref[...]
    raw = qd_ref[channels : channels + padded, :].astype(F32)
    shifted, step, rate, running = step_sizes(raw, bias_ref[...], log_ref[...])
    reach, toend, whole = chunk_factors(running, info)
    column = jnp.transpose(running)
    mask = pair_mask(info)
    skip = skip_ref[...]
    before = prefix_ref[0]
    in_t = xa_ref[inner : inner + n_state, :]
    out_t = xa_ref[inner + n_state :, :]
    scores = dot(in_t, out_t, 0, 0)
    lane = lax.broadcasted_iota(jnp.int32, (CHUNK, CHUNK), 1)

    def conv_back(at, d_active):
        rows = pl.ds(at, CHUNK)
        d_pre = d_active.astype(BF).astype(F32) * slope_ref[rows, :].astype(F32)
        q = qd_ref[rows, :].astype(F32)
        after = later[rows, :]
        dtaps[CONV, rows, :] += d_pre
        dtaps[CONV - 1, rows, :] += d_pre * q
        d_q = wide[CONV - 1, rows, :] * d_pre
        for k in range(1, CONV):
            mixed = jnp.where(lane < k, after, d_pre)
            moved = pltpu.roll(mixed, CHUNK - k, 1) * info[3 + k : 4 + k]
            d_q = d_q + wide[CONV - 1 - k, rows, :] * moved
            dtaps[CONV - 1 - k, rows, :] += moved * q
        later[rows, :] = d_pre
        dqd_ref[rows, :] = d_q.astype(BF)

    d_scores[...] = jnp.zeros_like(d_scores)
    for block in range(blocks):
        at = block * CHUNK
        rows = pl.ds(at, CHUNK)
        first = block * group
        x = xa_ref[rows, :].astype(F32)
        dy_low = dy_ref[rows, :]
        dy = dy_low.astype(F32)
        step_rows = per_head(step, first, group, width)
        entering = enter_ref[0, rows, :].astype(F32) + per_head(
            before, first, group, width
        ) * device_ref[rows, :].astype(F32)
        entering_low = entering.astype(BF)
        leaving = adjoint[rows, :]
        leaving_low = leaving.astype(BF)
        passed = entering * leaving
        driven_low = (x * step_rows).astype(BF)
        driven = driven_low.astype(F32)
        reach_dy = dy * per_head(reach, first, group, width)
        end_driven = driven * per_head(toend, first, group, width)
        far_dy_low = reach_dy.astype(BF)
        far_s[rows, :] = entering_low
        far_dy[rows, :] = far_dy_low
        far_g[rows, :] = leaving_low
        far_x[rows, :] = end_driven.astype(BF)
        far_out = reach_dy * dot(entering_low, out_t, 1, 0)
        far_in = dot(leaving_low, in_t, 1, 0)
        adjoint[rows, :] = leaving * per_head(whole, first, group, width) + dot(
            far_dy_low, out_t, 1, 1
        )
        near = []
        inside = []
        for k in range(group):
            head = first + k
            part = slice(k * width, (k + 1) * width)
            gap = (running[head : head + 1] + mask) - column[:, head : head + 1]
            decay = jnp.exp2(gap)
            mixer = (scores * decay).astype(BF)
            inside.append(dot(driven_low[part], mixer, 1, 0))
            near.append(dot(dy_low[part], mixer, 1, 1))
            d_scores[...] += decay * dot(driven_low[part], dy_low[part], 0, 0)
        near = jnp.concatenate(near)
        totals = dy * jnp.concatenate(inside) - driven * near + far_out
        leaves = end_driven * far_in
        d_driven = near + per_head(toend, first, group, width) * far_in
        direct = x * d_driven
        skips = x * dy
        for k in range(group):
            head = slice(first + k, first + k + 1)
            part = slice(k * width, (k + 1) * width)
            rows_total[head, :] = col_sum(totals[part])
            rows_leave[head, :] = col_sum(leaves[part])
            rows_direct[head, :] = col_sum(direct[part])
            rows_skip[head, :] = col_sum(skips[part])
            rows_pass[head, :] = col_sum(passed[part])
        conv_back(at, step_rows * d_driven + per_head(skip, first, group, width) * dy)
    d_scores_low = d_scores[...].astype(BF)
    d_in = dot(out_t, d_scores_low, 1, 1) + dot(far_g[...], far_x[...], 0, 0)
    d_out = dot(in_t, d_scores_low, 1, 0) + dot(far_s[...], far_dy[...], 0, 0)
    conv_back(inner, d_in)
    conv_back(inner + n_state, d_out)
    down, across = iotas()
    at_or_after = (down >= across).astype(F32)
    ahead = (down < across).astype(F32)
    through = jnp.sum(rows_pass[...], axis=1, keepdims=True) * whole
    d_rate = (
        dot(rows_total[...], at_or_after, 1, 0, HIGH)
        + dot(rows_leave[...], ahead, 1, 0, HIGH)
        + through
    )
    d_step = rows_direct[...] + rate * d_rate
    d_raw = d_step * sigmoid(shifted)
    dqd_ref[channels : channels + padded, :] = d_raw.astype(BF)
    dhead[0] += d_raw
    dhead[1] += d_rate * step * rate
    dhead[2] += rows_skip[...]

    @pl.when(step_at == last)
    def _():
        for k in range(3):
            dhead_ref[:, k : k + 1] = jnp.sum(dhead[k], axis=1, keepdims=True)
        for at in range(0, channels, CHUNK):
            for k in range(CONV + 1):
                dconv_ref[at : at + CHUNK, k : k + 1] = jnp.sum(
                    dtaps[k, at : at + CHUNK, :], axis=1, keepdims=True
                )
            edge_ref[:, at : at + CHUNK] = jnp.transpose(later[at : at + CHUNK, :])[0:8, :]


def scan_back(packs, xa, slope, qd, dy, enter, device, prefix, taps, bias, log_rate, skip, info, heads):
    inner, length = dy.shape
    channels = xa.shape[0]
    padded = bias.shape[0]
    steps = length // CHUNK

    def back(rows):
        return pl.BlockSpec((rows, CHUNK), lambda i: (0, steps - 1 - i))

    def back_three(rows):
        return pl.BlockSpec((1, rows, CHUNK), lambda i: (steps - 1 - i, 0, 0))

    return pl.pallas_call(
        functools.partial(scan_back_kernel, heads, len(packs)),
        grid=(steps,),
        in_specs=[whole_block(pack.shape) for pack in packs]
        + [
            back(channels),
            back(channels),
            back(channels + padded),
            back(inner),
            back_three(inner),
            whole_block(device.shape),
            back_three(padded),
            whole_block(taps.shape),
            whole_block(bias.shape),
            whole_block(bias.shape),
            whole_block(bias.shape),
            back(info.shape[0]),
        ],
        out_specs=[
            back(channels + padded),
            whole_block((channels, 8)),
            whole_block((padded, 8)),
            whole_block((8, channels)),
        ],
        out_shape=[
            jax.ShapeDtypeStruct((channels + padded, length), BF),
            jax.ShapeDtypeStruct((channels, 8), F32),
            jax.ShapeDtypeStruct((padded, 8), F32),
            jax.ShapeDtypeStruct((8, channels), F32),
        ],
        scratch_shapes=[
            pltpu.VMEM((CONV, channels, CHUNK), F32),
            pltpu.VMEM((inner, CHUNK), F32),
            pltpu.VMEM((channels, CHUNK), F32),
            pltpu.VMEM((CONV + 1, channels, CHUNK), F32),
            pltpu.VMEM((3, padded, CHUNK), F32),
            pltpu.VMEM((inner, CHUNK), BF),
            pltpu.VMEM((inner, CHUNK), BF),
            pltpu.VMEM((inner, CHUNK), BF),
            pltpu.VMEM((inner, CHUNK), BF),
        ]
        + [pltpu.VMEM((padded, CHUNK), F32)] * 5
        + [pltpu.VMEM((CHUNK, CHUNK), F32)],
        compiler_params=pltpu.CompilerParams(vmem_limit_bytes=VMEM),
        name="scan_backward",
    )(*packs, xa, slope, qd, dy, enter, device, prefix, taps, bias, log_rate, skip, info)


def edge_kernel(dqd_ref, qd_ref, edge_ref, taps_ref, info_ref, dconv_ref, out_ref, dconv_out_ref):
    channels = taps_ref.shape[0]
    lane = lax.broadcasted_iota(jnp.int32, (CHUNK, CHUNK), 1)
    info = info_ref[...]
    out_ref[...] = dqd_ref[...]
    dconv_out_ref[...] = dconv_ref[...]
    for at in range(0, channels, CHUNK):
        rows = pl.ds(at, CHUNK)
        first = jnp.concatenate([edge_ref[:, at : at + CHUNK], jnp.zeros((CHUNK - 8, CHUNK), F32)])
        d_pre = jnp.transpose(first)
        q = qd_ref[rows, :].astype(F32)
        d_q = dqd_ref[rows, :].astype(F32)
        for k in range(1, CONV):
            moved = pltpu.roll(jnp.where(lane < k, d_pre, 0.0), CHUNK - k, 1) * info[3 + k : 4 + k]
            tap = CONV - 1 - k
            d_q = d_q + taps_ref[rows, tap : tap + 1] * moved
            dconv_out_ref[rows, tap : tap + 1] += jnp.sum(moved * q, axis=1, keepdims=True)
        out_ref[rows, :] = d_q.astype(BF)


def edge_fix(dqd, qd, edge, taps, info, dconv):
    end = dqd.shape[1] // CHUNK - 1

    def final(rows):
        return pl.BlockSpec((rows, CHUNK), lambda i: (0, end))

    return pl.pallas_call(
        edge_kernel,
        grid=(1,),
        in_specs=[
            final(dqd.shape[0]),
            final(qd.shape[0]),
            whole_block(edge.shape),
            whole_block(taps.shape),
            final(info.shape[0]),
            whole_block(dconv.shape),
        ],
        out_specs=[final(dqd.shape[0]), whole_block(dconv.shape)],
        out_shape=[
            jax.ShapeDtypeStruct(dqd.shape, BF),
            jax.ShapeDtypeStruct(dconv.shape, F32),
        ],
        input_output_aliases={0: 0},
        compiler_params=pltpu.CompilerParams(vmem_limit_bytes=VMEM),
        name="edge_gradient",
    )(dqd, qd, edge, taps, info, dconv)


def passed_along(block, axis, distance):
    devices = range(lax.axis_size(axis))
    route = [(i - distance, i) for i in devices if i - distance in devices]
    return lax.ppermute(block, axis, route)


def total_over(value, axis):
    size = lax.axis_size(axis)
    if size & (size - 1):
        return lax.psum(value, axis)
    bit = 1
    while bit < size:
        other = lax.ppermute(value, axis, [(i, i ^ bit) for i in range(size)])
        value = (value.astype(F32) + other.astype(F32)).astype(value.dtype)
        bit *= 2
    return value


def token_info(stream_ids, place, rows):
    length = stream_ids.shape[0]
    margin = CHUNK
    ids = jnp.concatenate(
        [jnp.full((margin,), -1, jnp.int32), stream_ids, jnp.full((margin,), -2, jnp.int32)]
    )
    ids = lax.dynamic_slice_in_dim(ids, place * rows, rows + 2 * margin)
    own = ids[margin : margin + rows]
    lines = [own]
    lines += [(ids[margin - k : margin - k + rows] == own) for k in range(1, CONV)]
    lines += [(ids[margin + k : margin + k + rows] == own) for k in range(1, CONV)]
    by_chunk = own.reshape(-1, CHUNK)
    before = ids[margin - 1 : margin - 1 + rows].reshape(-1, CHUNK)[:, :1]
    end = by_chunk[:, -1:]
    lines += [(by_chunk == before).reshape(-1), (by_chunk == end).reshape(-1)]
    lines += [jnp.broadcast_to(before == end, by_chunk.shape).reshape(-1)]
    lines += [jnp.zeros((rows,), jnp.int32)] * (16 - len(lines))
    return jnp.stack([line.astype(F32) for line in lines])


def body(
    tokens,
    cotangent,
    seg_ids,
    norm_gain,
    in_weight,
    dt_weight,
    conv_weight,
    conv_bias,
    dt_bias,
    a_log,
    skip,
    out_gain,
    out_weight,
):
    layers, part_d, _ = in_weight.shape
    shards = lax.axis_size("shard")
    n_seq = lax.axis_size("seq")
    place = lax.axis_index("seq")
    inner = out_weight.shape[1] * shards
    channels = conv_bias.shape[1] * shards
    heads = dt_weight.shape[2]
    padded = -(-heads // 16) * 16
    rows = tokens.shape[1]
    width_d = tokens.shape[2]
    info = token_info(seg_ids[0], place, rows)

    pieces = [norm_gain, conv_weight.reshape(layers, -1), conv_bias, out_gain]
    small = lax.all_gather(jnp.concatenate(pieces, axis=1), "shard", axis=0)
    ends = [0]
    for piece in pieces:
        ends.append(ends[-1] + piece.shape[1])
    small = [small[:, :, a:b].astype(F32) for a, b in zip(ends[:-1], ends[1:])]
    gains_in = small[0].transpose(1, 0, 2).reshape(layers, -1)
    taps_all = small[1].reshape(shards, layers, CONV, -1).transpose(1, 0, 3, 2)
    taps_all = taps_all.reshape(layers, channels, CONV)
    bias_all = small[2].transpose(1, 0, 2).reshape(layers, channels, 1)
    taps_all = jnp.concatenate(
        [taps_all, bias_all, jnp.zeros((layers, channels, 8 - CONV - 1), F32)], axis=2
    )
    gains_out = small[3].transpose(1, 0, 2).reshape(layers, inner, 1)

    head_values = lax.all_gather(jnp.stack([dt_bias, a_log, skip]), "seq", axis=2, tiled=True)
    head_values = jnp.pad(head_values, ((0, 0), (0, 0), (0, padded - heads)))
    head_values = jnp.broadcast_to(head_values[..., None], head_values.shape + (CHUNK,))

    weights = []
    for layer in range(layers):
        scan_part = jnp.concatenate(
            [
                in_weight[layer, :, inner:],
                dt_weight[layer],
                jnp.zeros((part_d, padded - heads), in_weight.dtype),
            ],
            axis=1,
        )
        weights.append(
            (
                lax.all_gather(scan_part, "shard", axis=0, tiled=True),
                lax.all_gather(in_weight[layer, :, :inner], "shard", axis=0, tiled=True),
                lax.all_gather(out_weight[layer], "shard", axis=0, tiled=True),
            )
        )

    hidden = tokens[0].T.astype(F32)
    saved = []
    for layer in range(layers):
        w_scan, w_gate, w_out = weights[layer]
        taps = taps_all[layer]
        bias, log_rate, skips = (head_values[k, layer] for k in range(3))
        gain_out = gains_out[layer]
        inverse = lax.rsqrt(jnp.mean(hidden * hidden, axis=0, keepdims=True) + EPS)
        normed = (hidden * inverse * gains_in[layer][:, None]).astype(BF)
        halo = dot(normed[:, rows - EDGE :], w_scan, 0, 0).astype(BF)
        halo = passed_along(halo, "seq", 1)
        qd = dot(w_scan, normed, 0, 0).astype(BF)
        xa, slope, part, enter, prefix, reach, pack = scan(
            qd, halo, taps, bias, log_rate, skips, info, heads, inner
        )
        packs = [passed_along(pack, "seq", k) for k in range(1, n_seq)]
        z = dot(w_gate, normed, 0, 0).astype(BF)
        yb, gated, device = gated_norm(packs, part, z, xa, reach, gain_out, heads)
        saved.append((hidden, inverse, normed, qd, xa, slope, enter, prefix, reach, pack, z, yb, gated, device))
        hidden = hidden + dot(w_out, gated, 0, 0)
    activations = hidden.astype(BF).T[None]

    grad = cotangent[0].T.astype(F32)
    results = [None] * layers
    for layer in reversed(range(layers)):
        w_scan, w_gate, w_out = weights[layer]
        taps = taps_all[layer]
        bias, log_rate, skips = (head_values[k, layer] for k in range(3))
        gain_out = gains_out[layer]
        gain_in = gains_in[layer][:, None]
        h_in, inverse, normed, qd, xa, slope, enter, prefix, reach, pack, z, yb, gated, device = saved[layer]
        go = grad.astype(BF)
        dy, dz, d_gain_out, back_pack = gated_norm_back(
            go, w_out, yb, z, xa, reach, gain_out, pack, heads
        )
        back_packs = [passed_along(back_pack, "seq", -k) for k in range(1, n_seq)]
        d_w_out = dot(gated, go, 1, 1).astype(BF)
        d_w_gate = dot(normed, dz, 1, 1).astype(BF)
        share_out = lax.psum_scatter(d_w_out, "shard", scatter_dimension=0, tiled=True)
        share_gate = lax.psum_scatter(d_w_gate, "shard", scatter_dimension=0, tiled=True)
        dqd, d_conv, d_head, edge = scan_back(
            back_packs, xa, slope, qd, dy, enter, device, prefix, taps, bias, log_rate, skips, info, heads
        )
        edge = passed_along(edge, "seq", -1)
        d_normed = dot(w_gate, dz, 1, 0)
        dqd, d_conv = edge_fix(dqd, qd, edge, taps, info, d_conv)
        d_w_scan = dot(normed, dqd, 1, 1).astype(BF)
        share_scan = lax.psum_scatter(d_w_scan, "shard", scatter_dimension=0, tiled=True)
        d_normed = d_normed + dot(w_scan, dqd, 1, 0)
        scaled = d_normed * gain_in
        d_gain_in = jnp.sum(d_normed * h_in * inverse, axis=1)
        along = jnp.mean(scaled * h_in, axis=0, keepdims=True)
        grad = grad + scaled * inverse - h_in * (along * inverse * inverse * inverse)
        shares = tuple(total_over(item, "seq") for item in (share_out, share_gate, share_scan))
        vector = jnp.concatenate(
            [
                d_gain_in,
                d_conv[:, : CONV + 1].T.reshape(-1),
                d_gain_out[:, 0],
                d_head[:heads, :3].T.reshape(-1),
            ]
        )
        results[layer] = (shares, lax.psum(vector, ("seq", "shard")))
    which = lax.axis_index("shard")

    def own(vector, index, count):
        return lax.dynamic_slice_in_dim(vector, index * count, count)

    outs = [[] for _ in range(10)]
    for (share_out, share_gate, share_scan), vector in results:
        share_scan = share_scan.astype(F32)
        at = 0
        outs[0].append(own(vector[:width_d], which, width_d // shards))
        at += width_d
        wide = channels - inner
        outs[1].append(jnp.concatenate([share_gate.astype(F32), share_scan[:, :channels]], axis=1))
        outs[2].append(share_scan[:, channels : channels + heads])
        taps = vector[at : at + CONV * channels].reshape(CONV, channels)
        outs[3].append(lax.dynamic_slice_in_dim(taps, which * (channels // shards), channels // shards, 1))
        at += CONV * channels
        outs[4].append(own(vector[at : at + channels], which, channels // shards))
        at += channels
        gain = vector[at : at + inner]
        at += inner
        for k in range(3):
            outs[5 + k].append(own(vector[at : at + heads], place, heads // n_seq))
            at += heads
        outs[8].append(own(gain, which, inner // shards))
        outs[9].append(share_out.astype(F32))
    return (activations, grad.T[None]) + tuple(jnp.stack(item) for item in outs)


def solution(mesh):
    specs = (
        P(None, "shard"),
        P(None, "shard", None),
        P(None, "shard", None),
        P(None, None, "shard"),
        P(None, "shard"),
        P(None, "seq"),
        P(None, "seq"),
        P(None, "seq"),
        P(None, "shard"),
        P(None, "shard", None),
    )
    spread = P("shard", "seq", None)
    return jax.shard_map(
        body,
        mesh=mesh,
        in_specs=(spread, spread, P("shard", None)) + specs,
        out_specs=(spread, spread) + specs,
        check_vma=False,
    )
```

time: 2410 us -> 816 us (0.34)
  local copies, waits for them, and re-layouts: 680 us -> 54.6 us
  matrix products: 685 us -> 110 us
  other arithmetic: 518 us -> 33.4 us
  Pallas kernels: 0 us -> 185 us
  blocking collectives: 190 us -> 24 us
  waiting for transfers between devices: 227 us -> 332 us
    dot_general x378 -> x18, matrix products: 685 us -> 110 us  [dot(): lax.dot_general(left, right, (((left_dim,), (right_dim,)), ((), ())), pre...]
    pallas_call x0 -> x10, Pallas kernels: none -> 185 us  [the longest x2 67.2 us: scan_back(): pl.pallas_call(functools.partial(scan_back_kernel, heads, len(packs)), gr...]
    convert_element_type x24 -> x0, local copies, waits for them, and re-layouts: 135 us -> none  [the longest x6 47.9 us: body(): d_heads.astype(jnp.float32)]
    dynamic_slice x160 -> x4, local copies, waits for them, and re-layouts: 107 us -> 0.3 us  [own(): return lax.dynamic_slice_in_dim(vector, index * count, count)]
    reduce_sum x44 -> x1, other arithmetic: 104 us -> 0.36 us  [body(): inverse = lax.rsqrt(jnp.mean(hidden * hidden, axis=0, keepdims=True) + EPS)]
    squeeze x132 -> x7, local copies, waits for them, and re-layouts: 104 us -> 6.45 us  [the longest x2 2.97 us: body(): gain_out = gains_out[layer]]
    slice x31 -> x17, local copies, waits for them, and re-layouts: 103 us -> 10.8 us  [the longest x1 1.96 us: body(): in_weight[layer, :, :inner]]
    another operation x34 -> x16, other arithmetic: 99.8 us -> 7.95 us  [the longest x14 7.87 us: body(): jnp.stack(item)]
  transfers between devices with their start and end apart: 32 -> 41, of which waited for: 9 -> 22; matrix products, arithmetic and copies ran while one was open for 48% -> 20% of each run, Pallas kernels for 0% -> 8%
where the time goes in v1:
time: 816 us; the launch traced here: 807 us
  waiting for transfers between devices  332 us (41%)
  Pallas kernels  185 us (23%)
  matrix products  110 us (13%)
  local copies, waits for them, and re-layouts  54.6 us (7%)
  starting transfers between devices  53.2 us (7%)
  other arithmetic  33.4 us (4%)
  blocking collectives  24 us (3%)
  between operations  15 us (2%)
    dot_general x18, matrix products, dot(): lax.dot_general(left, right, (((left_dim,), (right_dim,)), ((), ())), pre...  110 us
    pallas_call x2, Pallas kernels, scan_back(): pl.pallas_call(functools.partial(scan_back_kernel, heads, len(packs)), gr...  67.2 us
    reduce_scatter x2, waiting for transfers between devices, body(): lax.psum_scatter(d_w_gate, 'shard', scatter_dimension=0, tiled=True)  65.3 us
    reduce_scatter x2, waiting for transfers between devices, body(): lax.psum_scatter(d_w_out, 'shard', scatter_dimension=0, tiled=True)  63.8 us
    reduce_scatter x2, waiting for transfers between devices, body(): lax.psum_scatter(d_w_scan, 'shard', scatter_dimension=0, tiled=True)  61.7 us
    psum x1, waiting for transfers between devices, body(): results[layer] = (shares, lax.psum(vector, ('seq', 'shard')))  55.7 us
    pallas_call x2, Pallas kernels, scan(): pl.pallas_call(functools.partial(scan_kernel, heads, inner), grid=(steps,...  40.4 us
    pallas_call x2, Pallas kernels, gated_norm_back(): pl.pallas_call(functools.partial(norm_back_kernel, heads), grid=(length /...  40.1 us
  transfers between devices with their start and end apart: 41, of which 22 were waited for; matrix products, arithmetic and copies ran while one was open for 20% of the time, Pallas kernels for 8%

profile of v1, /device:TPU:0, one launch (start us, length us, event | category | flops | bytes accessed | tf_op | source)
XLA Modules:
  0.0 807.4 jit_solution(2101947005462931108)
XLA Ops:
  16.3 15.8 %all-gather.5 = bf16[8,2,1408]{2,1,0:T(2,128)(2,1)S(1)} all-gather(bf16[1,2,1408]{2,1,0:T(2,128)(2,1)S(1)} %bitcast.256), channel_id=2, replica_groups=mesh['seq'=4,'shard'=8] {'shard'}, dimensions={0}, use_global_device_ids=true | all-gather | bytes 50688 | tf_op jit(solution)/shard_map/all_gather | solution.py:794
  41.3 8.1 %all_gather.30 = f32[3,2,24]{0,1,2:T(2,128)S(1)} all-gather(f32[3,2,6]{0,1,2:T(2,128)S(1)} %copy.169), channel_id=1, replica_groups=mesh['seq'=4,'shard'=8] {'seq'}, dimensions={2}, use_global_device_ids=true | all-gather | bytes 720 | tf_op jit(solution)/shard_map/all_gather | solution.py:808
  71.2 20.2 %scan_forward.2 = (bf16[1792,1024]{1,0:T(8,128)(2,1)}, bf16[1792,1024]{1,0:T(8,128)(2,1)}, bf16[1536,1024]{1,0:T(8,128)(2,1)}, bf16[8,1536,128]{2,1,0:T(8,128)(2...) custom-call(bf16[1824,1024]{1,0:T(8,128)(2,1)} %convolution_convert_fusion.3.qd_ref.refs_5_, ...), custom_call_target="tpu_custom_call" | custom-call | tf_op jit(solution)/shard_map/scan_forward/pallas_call | solution.py:210
  111.5 10.4 %gated_norm_forward.2 = (bf16[1536,1024]{1,0:T(8,128)(2,1)}, bf16[1536,1024]{1,0:T(8,128)(2,1)}, bf16[1536,128]{1,0:T(8,128)(2,1)}) custom-call(bf16[1600,128]{1,0:T(8,128)(2,1)} %copy-done.18, bf16[1600,128]{1,0:T(8,128)(2,1)} %collective-permute-done.2.refs_1_, bf16[1600,128]{1,0:T(8,128)(2,1)} %collective-permute-done.3.refs_2_, ...), custom_call_target="tpu_custom_call" | custom-call | tf_op jit(solution)/shard_map/gated_norm_forward/pallas_call | solution.py:305
  129.9 22.0 %all-gather.15.cloned.1.call-done = bf16[768,1824]{1,0:T(8,128)(2,1)} async-done(((bf16[96,1824]{1,0:T(8,128)(2,1)}), bf16[768,1824]{1,0:T(8,128)(2,1)}) %all-gather.15.cloned.1.call-update) | async-done | bytes 2801680 | tf_op jit(solution)/shard_map/all_gather | solution.py:824
  164.9 20.2 %scan_forward.3 = (bf16[1792,1024]{1,0:T(8,128)(2,1)}, bf16[1792,1024]{1,0:T(8,128)(2,1)}, bf16[1536,1024]{1,0:T(8,128)(2,1)}, bf16[8,1536,128]{2,1,0:T(8,128)(2...) custom-call(bf16[1824,1024]{1,0:T(8,128)(2,1)} %convolution_convert_fusion.1.qd_ref.refs_5_, ...), custom_call_target="tpu_custom_call" | custom-call | tf_op jit(solution)/shard_map/scan_forward/pallas_call | solution.py:210
  199.0 8.2 %collective-permute-done.6.refs_1_ = bf16[1600,128]{1,0:T(8,128)(2,1)} collective-permute-done((bf16[1600,128]{1,0:T(8,128)(2,1)}, bf16[1600,128]{1,0:T(8,128)(2,1)}, u32[]{:S(2)}, u32[]{:S(2)}) %collective-permute-start.6) | collective-permute-done | bytes 409632 | tf_op jit(solution)/shard_map/ppermute | solution.py:731
  207.3 10.4 %gated_norm_forward.3 = (bf16[1536,1024]{1,0:T(8,128)(2,1)}, bf16[1536,1024]{1,0:T(8,128)(2,1)}, bf16[1536,128]{1,0:T(8,128)(2,1)}) custom-call(bf16[1600,128]{1,0:T(8,128)(2,1)} %copy-done.19, bf16[1600,128]{1,0:T(8,128)(2,1)} %collective-permute-done.6.refs_1_, bf16[1600,128]{1,0:T(8,128)(2,1)} %collective-permute-done.7.refs_2_, ...), custom_call_target="tpu_custom_call" | custom-call | tf_op jit(solution)/shard_map/gated_norm_forward/pallas_call | solution.py:305
  217.7 20.0 %gated_norm_backward.2 = (bf16[1536,1024]{1,0:T(8,128)(2,1)}, bf16[1536,1024]{1,0:T(8,128)(2,1)}, f32[1536,1]{1,0:T(8,128)}, bf16[1600,128]{1,0:T(8,128)(2,1)}) custom-call(bf16[768,1024]{1,0:T(8,128)(2,1)} %bitcast.252, bf16[1536,768]{1,0:T(8,128)(2,1)} %bitcast.254, bf16[1536,1024]{1,0:T(8,128)(2,1)} %get-tuple-element.62.yb_ref, ...), custom_call_target="tpu_custom_call" | custom-call | tf_op jit(solution)/shard_map/gated_norm_backward/pallas_call | solution.py:405
  261.6 33.6 %scan_backward.2 = (bf16[1824,1024]{1,0:T(8,128)(2,1)}, f32[1792,8]{1,0:T(8,128)}, f32[32,8]{1,0:T(8,128)}, f32[8,1792]{1,0:T(8,128)}) custom-call(bf16[1600,128]{1,0:T(8,128)(2,1)} %copy-done.16, bf16[1600,128]{1,0:T(8,128)(2,1)} %copy-done.17, bf16[1600,128]{1,0:T(8,128)(2,1)} %copy-done.15, bf16[1792,1024]{1,0:T(8,128)(2,1)} %get-tuple-element.59.refs_5_.out_ref.refs_3_, ...), custom_call_target="tpu_custom_call" | custom-call | tf_op jit(solution)/shard_map/scan_backward/pallas_call | solution.py:632
  302.2 8.3 %edge_gradient.2 = (bf16[1824,1024]{1,0:T(8,128)(2,1)}, f32[1792,8]{1,0:T(8,128)}) custom-call(bf16[1824,1024]{1,0:T(8,128)(2,1)} %get-tuple-element.70.dqd_ref, bf16[1824,1024]{1,0:T(8,128)(2,1)} %convolution_convert_fusion.1.qd_ref.refs_5_, f32[8,1792]{1,0:T(8,128)} %copy-done.31, ...), custom_call_target="tpu_custom_call", output_to_operand_aliasing={{0}: (0, {})} | custom-call | tf_op jit(solution)/shard_map/edge_gradient/pallas_call | solution.py:706
  310.5 8.5 %multiply_reduce_fusion = (f32[768]{0:T(1024)}, f32[1024]{0:T(1024)S(1)}, f32[768,1024]{1,0:T(8,128)S(1)}) fusion(f32[1024]{0:T(1024)S(1)} %copy-done.26, f32[1024,768]{0,1:T(8,128)} %fusion.22, f32[1024,768]{0,1:T(8,128)S(1)} %copy-done.1, bf16[1,1024,768]{1,2,0:T(8,128)(2,1)S(1)} %copy.164, f32[768]{0:T(1024)S(1)} %copy-done.23, ...), kind=kOutput, calls=%fused_computation.39 | convolution fusion | flops 2875980032 | bytes 17561600 | tf_op jit(solution)/shard_map/dot_general | solution.py:23
  321.4 20.1 %gated_norm_backward.3 = (bf16[1536,1024]{1,0:T(8,128)(2,1)}, bf16[1536,1024]{1,0:T(8,128)(2,1)}, f32[1536,1]{1,0:T(8,128)}, bf16[1600,128]{1,0:T(8,128)(2,1)}) custom-call(bf16[768,1024]{1,0:T(8,128)(2,1)} %subtract_convert_fusion.go_ref, bf16[1536,768]{1,0:T(8,128)(2,1)} %bitcast.255, bf16[1536,1024]{1,0:T(8,128)(2,1)} %get-tuple-element.74.yb_ref, ...), custom_call_target="tpu_custom_call" | custom-call | tf_op jit(solution)/shard_map/gated_norm_backward/pallas_call | solution.py:405
  366.4 33.6 %scan_backward.3 = (bf16[1824,1024]{1,0:T(8,128)(2,1)}, f32[1792,8]{1,0:T(8,128)}, f32[32,8]{1,0:T(8,128)}, f32[8,1792]{1,0:T(8,128)}) custom-call(bf16[1600,128]{1,0:T(8,128)(2,1)} %copy-done.14, bf16[1600,128]{1,0:T(8,128)(2,1)} %collective-permute-done.13.refs_1_, bf16[1600,128]{1,0:T(8,128)(2,1)} %collective-permute-done.14.refs_2_, ...), custom_call_target="tpu_custom_call" | custom-call | tf_op jit(solution)/shard_map/scan_backward/pallas_call | solution.py:632
  406.8 8.1 %edge_gradient.3 = (bf16[1824,1024]{1,0:T(8,128)(2,1)}, f32[1792,8]{1,0:T(8,128)}) custom-call(bf16[1824,1024]{1,0:T(8,128)(2,1)} %get-tuple-element.82.dqd_ref, bf16[1824,1024]{1,0:T(8,128)(2,1)} %convolution_convert_fusion.3.qd_ref.refs_5_, f32[8,1792]{1,0:T(8,128)} %copy-done.30, ...), custom_call_target="tpu_custom_call", output_to_operand_aliasing={{0}: (0, {})} | custom-call | tf_op jit(solution)/shard_map/edge_gradient/pallas_call | solution.py:706
  418.6 9.3 %fusion.12 = (f32[768]{0:T(1024)S(1)}, f32[1024]{0:T(1024)S(1)}, f32[768,1024]{1,0:T(8,128)}) fusion(bf16[1,1024,768]{1,2,0:T(8,128)(2,1)S(1)} %copy.164, f32[1024]{0:T(1024)S(1)} %copy-done.35, f32[1024,768]{0,1:T(8,128)} %fusion.25, f32[768]{0:T(1024)S(1)} %copy-done.37, bf16[768,1824]{1,0:T(8,128)(2,1)} %all-gather.13.cloned.1.call-done, ...), kind=kOutput, calls=%fused_computation.25 | convolution fusion | flops 2875193600 | bytes 14415872 | tf_op jit(solution)/shard_map/dot_general | solution.py:23
  472.8 8.3 %fusion.14 = f32[1,1024,768]{1,2,0:T(8,128)} fusion(f32[1024,768]{0,1:T(8,128)} %fusion.25, f32[768,1024]{1,0:T(8,128)} %get-tuple-element.210, f32[1024,768]{0,1:T(8,128)} %fusion.22, f32[768,1024]{1,0:T(8,128)} %copy-done.4, f32[1024,768]{0,1:T(8,128)} %copy-done, bf16[1,1024,768]{1,2,0:T(8,128)(2,1)S(1)} %copy-done.2, ...), kind=kLoop, calls=%fused_computation.27 | loop fusion | flops 11796480 | bytes 22042624 | tf_op jit(solution)/shard_map/broadcast_in_dim | solution.py:919
  491.6 55.7 %all-reduce.4.cloned.1.call-done = (f32[11336]{0:T(1024)}, f32[11336]{0:T(1024)}) async-done(((f32[11336]{0:T(1024)}, f32[11336]{0:T(1024)}), (f32[11336]{0:T(1024)}, f32[11336]{0:T(1024)})) %all-reduce.4.cloned.1.call-update) | async-done | bytes 90704 | tf_op jit(solution)/shard_map/psum | solution.py:892
  558.6 28.7 %reduce-scatter.11.cloned.1.call-done = bf16[96,1536]{1,0:T(8,128)(2,1)} async-done(((bf16[768,1536]{1,0:T(8,128)(2,1)}), bf16[96,1536]{1,0:T(8,128)(2,1)}) %reduce-scatter.11.cloned.1.call-update) | async-done | bytes 294928 | tf_op jit(solution)/shard_map/reduce_scatter | solution.py:869
  589.7 35.7 %reduce-scatter.17.cloned.1.call-done = bf16[192,768]{1,0:T(8,128)(2,1)} async-done(((bf16[1536,768]{1,0:T(8,128)(2,1)}), bf16[192,768]{1,0:T(8,128)(2,1)}) %reduce-scatter.17.cloned.1.call-update) | async-done | bytes 294928 | tf_op jit(solution)/shard_map/reduce_scatter | solution.py:868
  634.7 28.1 %reduce-scatter.15.cloned.1.call-done = bf16[192,768]{1,0:T(8,128)(2,1)} async-done(((bf16[1536,768]{1,0:T(8,128)(2,1)}), bf16[192,768]{1,0:T(8,128)(2,1)}) %reduce-scatter.15.cloned.1.call-update) | async-done | bytes 294928 | tf_op jit(solution)/shard_map/reduce_scatter | solution.py:868
  664.3 36.5 %reduce-scatter.7.cloned.1.call-done = bf16[96,1536]{1,0:T(8,128)(2,1)} async-done(((bf16[768,1536]{1,0:T(8,128)(2,1)}), bf16[96,1536]{1,0:T(8,128)(2,1)}) %reduce-scatter.7.cloned.1.call-update) | async-done | bytes 294928 | tf_op jit(solution)/shard_map/reduce_scatter | solution.py:869
  709.1 31.9 %reduce-scatter.13.cloned.1.call-done = bf16[96,1824]{1,0:T(8,128)(2,1)} async-done(((bf16[768,1824]{1,0:T(8,128)(2,1)}), bf16[96,1824]{1,0:T(8,128)(2,1)}) %reduce-scatter.13.cloned.1.call-update) | async-done | bytes 350224 | tf_op jit(solution)/shard_map/reduce_scatter | solution.py:877
  752.1 29.8 %reduce-scatter.9.cloned.1.call-done = bf16[96,1824]{1,0:T(8,128)(2,1)} async-done(((bf16[768,1824]{1,0:T(8,128)(2,1)}), bf16[96,1824]{1,0:T(8,128)(2,1)}) %reduce-scatter.9.cloned.1.call-update) | async-done | bytes 350224 | tf_op jit(solution)/shard_map/reduce_scatter | solution.py:877
  (346 shorter events, 280.7 us)
Async XLA Ops:
  7.2 50.7 %all-gather.13.cloned.1.call-start = ((), (), s32[]{:S(2)}) async-start(), calls=%async_computation.6 | async-start | bytes 3317760 | tf_op jit(solution)/shard_map/all_gather | solution.py:824
  10.2 88.8 %all-gather.17.cloned.1.call-start = ((), (), s32[]{:S(2)}) async-start(), calls=%async_computation.14 | async-start | bytes 2654208 | tf_op jit(solution)/shard_map/all_gather | solution.py:825
  12.2 109.7 %all-gather.19.cloned.1.call-start = ((), (), s32[]{:S(2)}) async-start(), calls=%async_computation.15 | async-start | bytes 2654208 | tf_op jit(solution)/shard_map/all_gather | solution.py:826
  13.2 138.7 %all-gather.15.cloned.1.call-start = ((), (), s32[]{:S(2)}) async-start(), calls=%async_computation.7 | async-start | bytes 3317760 | tf_op jit(solution)/shard_map/all_gather | solution.py:824
  14.2 179.0 %all-gather.21.cloned.1.call-start = ((), (), s32[]{:S(2)}) async-start(), calls=%async_computation.16 | async-start | bytes 2654208 | tf_op jit(solution)/shard_map/all_gather | solution.py:825
  14.8 202.9 %all-gather.23.cloned.1.call-start = ((), (), s32[]{:S(2)}) async-start(), calls=%async_computation.17 | async-start | bytes 2654208 | tf_op jit(solution)/shard_map/all_gather | solution.py:826
  15.4 532.0 %all-reduce.4.cloned.1.call-start = ((), (), s32[]{:S(2)}) async-start(), calls=%async_computation.18 | async-start | bytes 196608 | tf_op jit(solution)/shard_map/psum | solution.py:892
  188.5 18.8 %collective-permute-start.6 = (bf16[1600,128]{1,0:T(8,128)(2,1)}, bf16[1600,128]{1,0:T(8,128)(2,1)}, u32[]{:S(2)}, u32[]{:S(2)}) collective-permute-start(bf16[1600,128]{1,0:T(8,128)(2,1)} %get-tuple-element.57.pack_in_ref), channel_id=1, source_target_pairs={{0,16},{8,24},{1,17},{9,25},{2,18},{10,26},{3,19},{11,27},{4,20},{... | collective-permute-start | bytes 1228808 | tf_op jit(solution)/shard_map/ppermute | solution.py:731
  240.3 20.6 %collective-permute-start.9 = (bf16[1600,128]{1,0:T(8,128)(2,1)}, bf16[1600,128]{1,0:T(8,128)(2,1)S(1)}, u32[]{:S(2)}, u32[]{:S(2)}) collective-permute-start(bf16[1600,128]{1,0:T(8,128)(2,1)} %get-tuple-element.64), channel_id=1, source_target_pairs={{16,0},{24,8},{17,1},{25,9},{18,2},{26,10},{19,3},{27,11},{20,4},{... | collective-permute-start | bytes 1228808 | tf_op jit(solution)/shard_map/ppermute | solution.py:731
  342.8 23.5 %collective-permute-start.13 = (bf16[1600,128]{1,0:T(8,128)(2,1)}, bf16[1600,128]{1,0:T(8,128)(2,1)}, u32[]{:S(2)}, u32[]{:S(2)}) collective-permute-start(bf16[1600,128]{1,0:T(8,128)(2,1)} %get-tuple-element.76), channel_id=1, source_target_pairs={{16,0},{24,8},{17,1},{25,9},{18,2},{26,10},{19,3},{27,11},{20,4},{... | collective-permute-start | bytes 1228808 | tf_op jit(solution)/shard_map/ppermute | solution.py:731
  344.1 22.2 %collective-permute-start.14 = (bf16[1600,128]{1,0:T(8,128)(2,1)}, bf16[1600,128]{1,0:T(8,128)(2,1)}, u32[]{:S(2)}, u32[]{:S(2)}) collective-permute-start(bf16[1600,128]{1,0:T(8,128)(2,1)} %get-tuple-element.76), channel_id=1, source_target_pairs={{24,0},{25,1},{26,2},{27,3},{28,4},{29,5},{30,6},{31,7}} | collective-permute-start | bytes 1228808 | tf_op jit(solution)/shard_map/ppermute | solution.py:731
  428.5 158.8 %reduce-scatter.11.cloned.1.call-start = ((), (), s32[]{:S(2)}) async-start(), calls=%async_computation.10 | async-start | bytes 2654208 | tf_op jit(solution)/shard_map/reduce_scatter | solution.py:869
  435.0 190.3 %reduce-scatter.17.cloned.1.call-start = ((), (), s32[]{:S(2)}) async-start(), calls=%async_computation.13 | async-start | bytes 2654208 | tf_op jit(solution)/shard_map/reduce_scatter | solution.py:868
  441.5 221.4 %reduce-scatter.15.cloned.1.call-start = ((), (), s32[]{:S(2)}) async-start(), calls=%async_computation.12 | async-start | bytes 2654208 | tf_op jit(solution)/shard_map/reduce_scatter | solution.py:868
  448.2 252.5 %reduce-scatter.7.cloned.1.call-start = ((), (), s32[]{:S(2)}) async-start(), calls=%async_computation.8 | async-start | bytes 2654208 | tf_op jit(solution)/shard_map/reduce_scatter | solution.py:869
  454.7 286.3 %reduce-scatter.13.cloned.1.call-start = ((), (), s32[]{:S(2)}) async-start(), calls=%async_computation.11 | async-start | bytes 3317760 | tf_op jit(solution)/shard_map/reduce_scatter | solution.py:877
  462.3 319.6 %reduce-scatter.9.cloned.1.call-start = ((), (), s32[]{:S(2)}) async-start(), calls=%async_computation.9 | async-start | bytes 3317760 | tf_op jit(solution)/shard_map/reduce_scatter | solution.py:877
  587.4 39.3 %collective-permute-start.20 = (bf16[96,1536]{1,0:T(8,128)(2,1)}, bf16[96,1536]{1,0:T(8,128)(2,1)S(1)}, u32[]{:S(2)}, u32[]{:S(2)}) collective-permute-start(bf16[96,1536]{1,0:T(8,128)(2,1)} %reduce-scatter.11.cloned.1.call-done), channel_id=1, source_target_pairs={{0,8},{8,0},{16,24},{24,16},{1,9},{9,1},{17,25},{25,17},{2,10},{10... | collective-permute-start | bytes 884744 | tf_op jit(solution)/shard_map/ppermute | solution.py:740
  627.7 74.4 %collective-permute-start.21 = (bf16[96,1536]{1,0:T(8,128)(2,1)S(1)}, bf16[96,1536]{1,0:T(8,128)(2,1)S(1)}, u32[]{:S(2)}, u32[]{:S(2)}) collective-permute-start(bf16[96,1536]{1,0:T(8,128)(2,1)S(1)} %add_convert_fusion.10), channel_id=1, source_target_pairs={{0,16},{8,24},{16,0},{24,8},{1,17},{9,25},{17,1},{25,9},{2,18},{10... | collective-permute-start | bytes 884744 | tf_op jit(solution)/shard_map/ppermute | solution.py:740
  633.3 68.8 %collective-permute-start.27 = (bf16[192,768]{1,0:T(8,128)(2,1)S(1)}, bf16[192,768]{1,0:T(8,128)(2,1)S(1)}, u32[]{:S(2)}, u32[]{:S(2)}) collective-permute-start(bf16[192,768]{1,0:T(8,128)(2,1)S(1)} %add_convert_fusion.6), channel_id=1, source_target_pairs={{0,16},{8,24},{16,0},{24,8},{1,17},{9,25},{17,1},{25,9},{2,18},{10... | collective-permute-start | bytes 884744 | tf_op jit(solution)/shard_map/ppermute | solution.py:740
  662.9 39.3 %collective-permute-start.24 = (bf16[192,768]{1,0:T(8,128)(2,1)}, bf16[192,768]{1,0:T(8,128)(2,1)S(1)}, u32[]{:S(2)}, u32[]{:S(2)}) collective-permute-start(bf16[192,768]{1,0:T(8,128)(2,1)} %reduce-scatter.15.cloned.1.call-done), channel_id=1, source_target_pairs={{0,8},{8,0},{16,24},{24,16},{1,9},{9,1},{17,25},{25,17},{2,10},{10... | collective-permute-start | bytes 884744 | tf_op jit(solution)/shard_map/ppermute | solution.py:740
  703.2 39.3 %collective-permute-start.25 = (bf16[192,768]{1,0:T(8,128)(2,1)S(1)}, bf16[192,768]{1,0:T(8,128)(2,1)S(1)}, u32[]{:S(2)}, u32[]{:S(2)}) collective-permute-start(bf16[192,768]{1,0:T(8,128)(2,1)S(1)} %add_convert_fusion.8), channel_id=1, source_target_pairs={{0,16},{8,24},{16,0},{24,8},{1,17},{9,25},{17,1},{25,9},{2,18},{10... | collective-permute-start | bytes 884744 | tf_op jit(solution)/shard_map/ppermute | solution.py:740
  707.8 44.2 %collective-permute-start.17 = (bf16[96,1536]{1,0:T(8,128)(2,1)S(1)}, bf16[96,1536]{1,0:T(8,128)(2,1)S(1)}, u32[]{:S(2)}, u32[]{:S(2)}) collective-permute-start(bf16[96,1536]{1,0:T(8,128)(2,1)S(1)} %add_convert_fusion.12), channel_id=1, source_target_pairs={{0,16},{8,24},{16,0},{24,8},{1,17},{9,25},{17,1},{25,9},{2,18},{10... | collective-permute-start | bytes 884744 | tf_op jit(solution)/shard_map/ppermute | solution.py:740
  750.4 33.0 %collective-permute-start.23 = (bf16[96,1824]{1,0:T(8,128)(2,1)S(1)}, bf16[96,1824]{1,0:T(8,128)(2,1)S(1)}, u32[]{:S(2)}, u32[]{:S(2)}) collective-permute-start(bf16[96,1824]{1,0:T(8,128)(2,1)S(1)} %add_convert_fusion.2), channel_id=1, source_target_pairs={{0,16},{8,24},{16,0},{24,8},{1,17},{9,25},{17,1},{25,9},{2,18},{10... | collective-permute-start | bytes 1050632 | tf_op jit(solution)/shard_map/ppermute | solution.py:740
  (72 other events, 668.4 us)
Sparse Core Ops, SparseCore 0:
  10.3 39.5 all-gather.12
  51.6 30.5 all-gather.16
  83.8 30.7 all-gather.18
  116.1 35.7 all-gather.14
  153.4 30.4 all-gather.20
  185.4 30.7 all-gather.22
  428.7 118.6 all-reduce.3
  550.2 37.0 reduce-scatter.10
  589.7 35.6 reduce-scatter.16
  627.5 35.2 reduce-scatter.14
  665.2 35.5 reduce-scatter.6
  702.9 38.0 reduce-scatter.12
  743.4 38.4 reduce-scatter.8

commit v2 on v1

--- a/solution.py
+++ b/solution.py
@@ -1,4 +1,5 @@
 import functools
+import math
 
 import jax
 import jax.numpy as jnp
@@ -10,6 +11,7 @@
 CONV = 4
 EPS = 1e-05
 CHUNK = 128
+STEP = 256
 EDGE = 16
 LOG2E = 1.4426950408889634
 FAR = -1e30
@@ -17,6 +19,7 @@
 F32 = jnp.float32
 HIGH = lax.Precision.HIGHEST
 VMEM = 56 * 1024 * 1024
+HBM_BYTES_PER_US = 3_690_000
 
 
 def dot(left, right, left_dim, right_dim, precision=None):
@@ -73,6 +76,11 @@
     toend = jnp.exp2(total - running) * info[8:9]
     whole = jnp.exp2(jnp.broadcast_to(total, running.shape)) * info[9:10]
     return reach, toend, whole
+
+
+def column_of(rows_ref, at):
+    block = jnp.concatenate([rows_ref[:, at : at + CHUNK], jnp.zeros((CHUNK - 8, CHUNK), F32)])
+    return jnp.transpose(block)
 
 
 def shape_of(heads, inner, state):
@@ -121,13 +129,12 @@
     @pl.when(step_at == 0)
     def _():
         for at in range(0, channels, CHUNK):
+            columns = column_of(taps_ref, at)
             rows = halo_ref[:, at : at + CHUNK].astype(F32)
             rows = jnp.concatenate([jnp.zeros((CHUNK - EDGE, CHUNK), F32), rows])
             carry[at : at + CHUNK, :] = jnp.transpose(rows).astype(BF)
             for k in range(CONV + 1):
-                wide[k, at : at + CHUNK, :] = jnp.broadcast_to(
-                    taps_ref[at : at + CHUNK, k : k + 1], (CHUNK, CHUNK)
-                )
+                wide[k, at : at + CHUNK, :] = jnp.broadcast_to(columns[:, k : k + 1], (CHUNK, CHUNK))
         state[...] = jnp.zeros_like(state)
         prefix[...] = jnp.ones_like(prefix)
 
@@ -194,8 +201,14 @@
         pack_ref[inner + padded : inner + 2 * padded, :] = (factor - high.astype(F32)).astype(BF)
 
 
-def lane_block(rows):
-    return pl.BlockSpec((rows, CHUNK), lambda i: (0, i))
+def takes(microseconds):
+    return pl.CostEstimate(
+        flops=0, transcendentals=0, bytes_accessed=int(microseconds * HBM_BYTES_PER_US)
+    )
+
+
+def lane_block(rows, lanes=CHUNK):
+    return pl.BlockSpec((rows, lanes), lambda i: (0, i))
 
 
 def whole_block(shape):
@@ -244,6 +257,7 @@
             pltpu.VMEM((padded, CHUNK), F32),
         ],
         compiler_params=pltpu.CompilerParams(vmem_limit_bytes=VMEM),
+        cost_estimate=takes(20),
         name="scan_forward",
     )(qd, halo, taps, bias, log_rate, skip, info)
 
@@ -265,7 +279,7 @@
 
 def norm_kernel(heads, n_packs, *refs):
     packs = refs[:n_packs]
-    part_ref, z_ref, out_ref, reach_ref, gain_ref, yb_ref, n_ref, enter_ref, value = refs[n_packs:]
+    part_ref, z_ref, out_ref, reach_ref, gain_ref, yb_ref, n_ref, enter_ref, value, gain = refs[n_packs:]
     inner = part_ref.shape[0]
     padded = reach_ref.shape[0]
     width = inner // heads
@@ -274,17 +288,18 @@
     @pl.when(pl.program_id(0) == 0)
     def _():
         for at in range(0, inner, CHUNK):
+            gain[at : at + CHUNK, :] = column_of(gain_ref, at)[:, 0:1]
             if n_packs:
                 enter_ref[at : at + CHUNK, :] = joined(packs, at, inner, heads, padded).astype(BF)
             else:
                 enter_ref[at : at + CHUNK, :] = jnp.zeros((CHUNK, CHUNK), BF)
 
     reach = reach_ref[...]
-    out_t = out_ref[...]
-    squares = jnp.zeros((CHUNK, CHUNK), F32)
+    value[...] = dot(enter_ref[...], out_ref[...], 1, 0)
+    squares = jnp.zeros((CHUNK, reach.shape[1]), F32)
     for at in range(0, inner, CHUNK):
         rows = pl.ds(at, CHUNK)
-        late = per_head(reach, at // width, count, width) * dot(enter_ref[rows, :], out_t, 1, 0)
+        late = per_head(reach, at // width, count, width) * value[rows, :]
         mixed = (part_ref[rows, :].astype(F32) + late).astype(BF)
         yb_ref[rows, :] = mixed
         z = z_ref[rows, :].astype(F32)
@@ -294,38 +309,44 @@
     scale = lax.rsqrt(col_sum(squares) * (1.0 / inner) + EPS)
     for at in range(0, inner, CHUNK):
         rows = pl.ds(at, CHUNK)
-        n_ref[rows, :] = (value[rows, :] * scale * gain_ref[rows, :]).astype(BF)
+        n_ref[rows, :] = (value[rows, :] * scale * gain[rows, :]).astype(BF)
 
 
 def gated_norm(packs, part, z, xa, reach, gain, heads):
     inner, length = part.shape
+    lanes = math.gcd(length, STEP)
     channels = xa.shape[0]
     n_state = (channels - inner) // 2
     out_at = (channels - n_state) // n_state
     return pl.pallas_call(
         functools.partial(norm_kernel, heads, len(packs)),
-        grid=(length // CHUNK,),
+        grid=(length // lanes,),
         in_specs=[whole_block(pack.shape) for pack in packs]
         + [
-            lane_block(inner),
-            lane_block(inner),
-            pl.BlockSpec((n_state, CHUNK), lambda i: (out_at, i)),
-            lane_block(reach.shape[0]),
+            lane_block(inner, lanes),
+            lane_block(inner, lanes),
+            pl.BlockSpec((n_state, lanes), lambda i: (out_at, i)),
+            lane_block(reach.shape[0], lanes),
             whole_block(gain.shape),
         ],
-        out_specs=[lane_block(inner), lane_block(inner), whole_block((inner, n_state))],
+        out_specs=[lane_block(inner, lanes), lane_block(inner, lanes), whole_block((inner, n_state))],
         out_shape=[
             jax.ShapeDtypeStruct((inner, length), BF),
             jax.ShapeDtypeStruct((inner, length), BF),
             jax.ShapeDtypeStruct((inner, n_state), BF),
         ],
-        scratch_shapes=[pltpu.VMEM((inner, CHUNK), F32)],
+        scratch_shapes=[pltpu.VMEM((inner, lanes), F32), pltpu.VMEM((inner, 1), F32)],
         compiler_params=pltpu.CompilerParams(vmem_limit_bytes=VMEM),
+        cost_estimate=takes(9),
         name="gated_norm_forward",
     )(*packs, part, z, xa, reach, gain)
 
 
-def norm_back_kernel(
+def norm_back_kernel(heads, n_after, *refs):
+    norm_back_step(heads, *refs[n_after:])
+
+
+def norm_back_step(
     heads,
     go_ref,
     weight_ref,
@@ -343,6 +364,8 @@
     dn,
     dgain,
     adjoint,
+    far,
+    gain,
 ):
     step_at = pl.program_id(0)
     last = pl.num_programs(0) - 1
@@ -353,92 +376,98 @@
 
     @pl.when(step_at == 0)
     def _():
+        for at in range(0, inner, CHUNK):
+            gain[at : at + CHUNK, :] = column_of(gain_ref, at)[:, 0:1]
         dgain[...] = jnp.zeros_like(dgain)
         adjoint[...] = jnp.zeros_like(adjoint)
 
     go = go_ref[...]
-    squares = jnp.zeros((CHUNK, CHUNK), F32)
-    crosses = jnp.zeros((CHUNK, CHUNK), F32)
+    dn[...] = dot(weight_ref[...], go, 1, 0)
+    squares = jnp.zeros((CHUNK, go.shape[1]), F32)
+    crosses = jnp.zeros((CHUNK, go.shape[1]), F32)
     for at in range(0, inner, CHUNK):
         rows = pl.ds(at, CHUNK)
-        d_norm = dot(weight_ref[rows, :], go, 1, 0)
+        d_norm = dn[rows, :]
         z = z_ref[rows, :].astype(F32)
         gated = yb_ref[rows, :].astype(F32) * (z * sigmoid(z))
-        dn[rows, :] = d_norm
         value[rows, :] = gated
         squares = squares + gated * gated
-        crosses = crosses + gated * (d_norm * gain_ref[rows, :])
+        crosses = crosses + gated * (d_norm * gain[rows, :])
     scale = lax.rsqrt(col_sum(squares) * (1.0 / inner) + EPS)
     pull = col_sum(crosses) * (1.0 / inner) * scale * scale * scale
     reach = reach_ref[...]
-    out_t = out_ref[...]
     for at in range(0, inner, CHUNK):
         rows = pl.ds(at, CHUNK)
         gated = value[rows, :]
         d_norm = dn[rows, :]
         dgain[rows, :] += d_norm * gated * scale
-        d_gated = d_norm * gain_ref[rows, :] * scale - gated * pull
+        d_gated = d_norm * gain[rows, :] * scale - gated * pull
         z = z_ref[rows, :].astype(F32)
         gate = sigmoid(z)
         dy = (d_gated * (z * gate)).astype(BF)
         dy_ref[rows, :] = dy
         d_silu = d_gated * yb_ref[rows, :].astype(F32)
         dz_ref[rows, :] = (d_silu * (gate * (1.0 + z * (1.0 - gate)))).astype(BF)
-        far = (dy.astype(F32) * per_head(reach, at // width, count, width)).astype(BF)
-        adjoint[rows, :] += dot(far, out_t, 1, 1)
+        far[rows, :] = (dy.astype(F32) * per_head(reach, at // width, count, width)).astype(BF)
+    adjoint[...] += dot(far[...], out_ref[...], 1, 1)
 
     @pl.when(step_at == last)
     def _():
         pack_ref[0:inner, :] = adjoint[...].astype(BF)
         pack_ref[inner : inner + 2 * padded, :] = pack_in_ref[inner : inner + 2 * padded, :]
         for at in range(0, inner, CHUNK):
-            dgain_ref[at : at + CHUNK, :] = jnp.sum(
-                dgain[at : at + CHUNK, :], axis=1, keepdims=True
-            )
-
-
-def gated_norm_back(go, weight, yb, z, xa, reach, gain, pack, heads):
+            total = jnp.sum(dgain[at : at + CHUNK, :], axis=1, keepdims=True)
+            total = jnp.transpose(jnp.broadcast_to(total, (CHUNK, CHUNK)))
+            dgain_ref[:, at : at + CHUNK] = total[0:8]
+
+
+def gated_norm_back(go, weight, yb, z, xa, reach, gain, pack, heads, after):
     inner, length = yb.shape
+    lanes = math.gcd(length, STEP)
     channels = xa.shape[0]
     n_state = (channels - inner) // 2
     out_at = (channels - n_state) // n_state
     return pl.pallas_call(
-        functools.partial(norm_back_kernel, heads),
-        grid=(length // CHUNK,),
-        in_specs=[
-            lane_block(go.shape[0]),
+        functools.partial(norm_back_kernel, heads, len(after)),
+        grid=(length // lanes,),
+        in_specs=[pl.BlockSpec(memory_space=pl.ANY)] * len(after)
+        + [
+            lane_block(go.shape[0], lanes),
             whole_block(weight.shape),
-            lane_block(inner),
-            lane_block(inner),
-            pl.BlockSpec((n_state, CHUNK), lambda i: (out_at, i)),
-            lane_block(reach.shape[0]),
+            lane_block(inner, lanes),
+            lane_block(inner, lanes),
+            pl.BlockSpec((n_state, lanes), lambda i: (out_at, i)),
+            lane_block(reach.shape[0], lanes),
             whole_block(gain.shape),
             whole_block(pack.shape),
         ],
         out_specs=[
-            lane_block(inner),
-            lane_block(inner),
-            whole_block((inner, 1)),
+            lane_block(inner, lanes),
+            lane_block(inner, lanes),
+            whole_block((8, inner)),
             whole_block(pack.shape),
         ],
         out_shape=[
             jax.ShapeDtypeStruct((inner, length), BF),
             jax.ShapeDtypeStruct((inner, length), BF),
-            jax.ShapeDtypeStruct((inner, 1), F32),
+            jax.ShapeDtypeStruct((8, inner), F32),
             jax.ShapeDtypeStruct(pack.shape, BF),
         ],
         scratch_shapes=[
-            pltpu.VMEM((inner, CHUNK), F32),
-            pltpu.VMEM((inner, CHUNK), F32),
-            pltpu.VMEM((inner, CHUNK), F32),
-            pltpu.VMEM((inner, CHUNK), F32),
+            pltpu.VMEM((inner, lanes), F32),
+            pltpu.VMEM((inner, lanes), F32),
+            pltpu.VMEM((inner, lanes), F32),
+            pltpu.VMEM((inner, n_state), F32),
+            pltpu.VMEM((inner, lanes), BF),
+            pltpu.VMEM((inner, 1), F32),
         ],
         compiler_params=pltpu.CompilerParams(vmem_limit_bytes=VMEM),
+        cost_estimate=takes(17),
         name="gated_norm_backward",
-    )(go, weight, yb, z, xa, reach, gain, pack)
-
-
-def scan_back_kernel(heads, n_packs, *refs):
+    )(*after, go, weight, yb, z, xa, reach, gain, pack)
+
+
+def scan_back_kernel(heads, n_packs, n_after, *refs):
     packs = refs[:n_packs]
     (
         xa_ref,
@@ -472,7 +501,7 @@
         rows_skip,
         rows_pass,
         d_scores,
-    ) = refs[n_packs:]
+    ) = refs[n_packs + n_after :]
     step_at = pl.program_id(0)
     last = pl.num_programs(0) - 1
     channels = xa_ref.shape[0]
@@ -484,10 +513,9 @@
     @pl.when(step_at == 0)
     def _():
         for at in range(0, channels, CHUNK):
+            columns = column_of(taps_ref, at)
             for k in range(CONV):
-                wide[k, at : at + CHUNK, :] = jnp.broadcast_to(
-                    taps_ref[at : at + CHUNK, k : k + 1], (CHUNK, CHUNK)
-                )
+                wide[k, at : at + CHUNK, :] = jnp.broadcast_to(columns[:, k : k + 1], (CHUNK, CHUNK))
         for at in range(0, inner, CHUNK):
             if n_packs:
                 adjoint[at : at + CHUNK, :] = joined(packs, at, inner, heads, padded)
@@ -610,14 +638,15 @@
         for k in range(3):
             dhead_ref[:, k : k + 1] = jnp.sum(dhead[k], axis=1, keepdims=True)
         for at in range(0, channels, CHUNK):
+            totals = jnp.zeros((CHUNK, CHUNK), F32)
             for k in range(CONV + 1):
-                dconv_ref[at : at + CHUNK, k : k + 1] = jnp.sum(
-                    dtaps[k, at : at + CHUNK, :], axis=1, keepdims=True
-                )
+                one = jnp.sum(dtaps[k, at : at + CHUNK, :], axis=1, keepdims=True)
+                totals = jnp.where(lane == k, one, totals)
+            dconv_ref[:, at : at + CHUNK] = jnp.transpose(totals)[0:8]
             edge_ref[:, at : at + CHUNK] = jnp.transpose(later[at : at + CHUNK, :])[0:8, :]
 
 
-def scan_back(packs, xa, slope, qd, dy, enter, device, prefix, taps, bias, log_rate, skip, info, heads):
+def scan_back(packs, xa, slope, qd, dy, enter, device, prefix, taps, bias, log_rate, skip, info, heads, after):
     inner, length = dy.shape
     channels = xa.shape[0]
     padded = bias.shape[0]
@@ -630,9 +659,10 @@
         return pl.BlockSpec((1, rows, CHUNK), lambda i: (steps - 1 - i, 0, 0))
 
     return pl.pallas_call(
-        functools.partial(scan_back_kernel, heads, len(packs)),
+        functools.partial(scan_back_kernel, heads, len(packs), len(after)),
         grid=(steps,),
         in_specs=[whole_block(pack.shape) for pack in packs]
+        + [pl.BlockSpec(memory_space=pl.ANY)] * len(after)
         + [
             back(channels),
             back(channels),
@@ -649,13 +679,13 @@
         ],
         out_specs=[
             back(channels + padded),
-            whole_block((channels, 8)),
+            whole_block((8, channels)),
             whole_block((padded, 8)),
             whole_block((8, channels)),
         ],
         out_shape=[
             jax.ShapeDtypeStruct((channels + padded, length), BF),
-            jax.ShapeDtypeStruct((channels, 8), F32),
+            jax.ShapeDtypeStruct((8, channels), F32),
             jax.ShapeDtypeStruct((padded, 8), F32),
             jax.ShapeDtypeStruct((8, channels), F32),
         ],
@@ -673,56 +703,48 @@
         + [pltpu.VMEM((padded, CHUNK), F32)] * 5
         + [pltpu.VMEM((CHUNK, CHUNK), F32)],
         compiler_params=pltpu.CompilerParams(vmem_limit_bytes=VMEM),
+        cost_estimate=takes(33),
         name="scan_backward",
-    )(*packs, xa, slope, qd, dy, enter, device, prefix, taps, bias, log_rate, skip, info)
-
-
-def edge_kernel(dqd_ref, qd_ref, edge_ref, taps_ref, info_ref, dconv_ref, out_ref, dconv_out_ref):
-    channels = taps_ref.shape[0]
-    lane = lax.broadcasted_iota(jnp.int32, (CHUNK, CHUNK), 1)
-    info = info_ref[...]
+    )(*packs, *after, xa, slope, qd, dy, enter, device, prefix, taps, bias, log_rate, skip, info)
+
+
+def edge_kernel(n_after, dqd_ref, fix_ref, *refs):
+    out_ref = refs[n_after]
+    channels = fix_ref.shape[1]
     out_ref[...] = dqd_ref[...]
-    dconv_out_ref[...] = dconv_ref[...]
     for at in range(0, channels, CHUNK):
         rows = pl.ds(at, CHUNK)
-        first = jnp.concatenate([edge_ref[:, at : at + CHUNK], jnp.zeros((CHUNK - 8, CHUNK), F32)])
-        d_pre = jnp.transpose(first)
-        q = qd_ref[rows, :].astype(F32)
-        d_q = dqd_ref[rows, :].astype(F32)
-        for k in range(1, CONV):
-            moved = pltpu.roll(jnp.where(lane < k, d_pre, 0.0), CHUNK - k, 1) * info[3 + k : 4 + k]
-            tap = CONV - 1 - k
-            d_q = d_q + taps_ref[rows, tap : tap + 1] * moved
-            dconv_out_ref[rows, tap : tap + 1] += jnp.sum(moved * q, axis=1, keepdims=True)
-        out_ref[rows, :] = d_q.astype(BF)
-
-
-def edge_fix(dqd, qd, edge, taps, info, dconv):
+        fix = jnp.concatenate(
+            [jnp.zeros((CHUNK - 8, CHUNK), F32), fix_ref[:, at : at + CHUNK]]
+        )
+        out_ref[rows, :] = (dqd_ref[rows, :].astype(F32) + jnp.transpose(fix)).astype(BF)
+
+
+def edge_fix(dqd, fix, after):
     end = dqd.shape[1] // CHUNK - 1
-
-    def final(rows):
-        return pl.BlockSpec((rows, CHUNK), lambda i: (0, end))
-
+    block = pl.BlockSpec((dqd.shape[0], CHUNK), lambda i: (0, end))
     return pl.pallas_call(
-        edge_kernel,
+        functools.partial(edge_kernel, len(after)),
         grid=(1,),
-        in_specs=[
-            final(dqd.shape[0]),
-            final(qd.shape[0]),
-            whole_block(edge.shape),
-            whole_block(taps.shape),
-            final(info.shape[0]),
-            whole_block(dconv.shape),
-        ],
-        out_specs=[final(dqd.shape[0]), whole_block(dconv.shape)],
-        out_shape=[
-            jax.ShapeDtypeStruct(dqd.shape, BF),
-            jax.ShapeDtypeStruct(dconv.shape, F32),
-        ],
+        in_specs=[block, whole_block(fix.shape)] + [pl.BlockSpec(memory_space=pl.ANY)] * len(after),
+        out_specs=block,
+        out_shape=jax.ShapeDtypeStruct(dqd.shape, BF),
         input_output_aliases={0: 0},
         compiler_params=pltpu.CompilerParams(vmem_limit_bytes=VMEM),
+        cost_estimate=takes(2),
         name="edge_gradient",
-    )(dqd, qd, edge, taps, info, dconv)
+    )(dqd, fix, *after)
+
+
+def edge_terms(edge, last_q, taps, info):
+    rows = edge.shape[0]
+    moved = []
+    for k in range(1, CONV):
+        below = jnp.concatenate([jnp.zeros((rows - k, edge.shape[1]), F32), edge[:k]])
+        moved.append(below * info[3 + k, -rows:][:, None])
+    fix = sum(taps[CONV - 1 - k][None, :] * moved[k - 1] for k in range(1, CONV))
+    d_taps = [jnp.sum(moved[k - 1] * last_q, axis=0) for k in range(CONV - 1, 0, -1)]
+    return fix, jnp.stack(d_taps)
 
 
 def passed_along(block, axis, distance):
@@ -734,11 +756,43 @@
 def total_over(value, axis):
     size = lax.axis_size(axis)
     if size & (size - 1):
+        return jnp.sum(lax.all_gather(value, axis).astype(F32), axis=0)
+    terms = [value] + [
+        lax.ppermute(value, axis, [(i, i ^ k) for i in range(size)]) for k in range(1, size)
+    ]
+    terms = [term.astype(F32) for term in terms]
+    while len(terms) > 1:
+        terms = [terms[k] + terms[k + 1] for k in range(0, len(terms), 2)]
+    return terms[0]
+
+
+def split_total_over(value, axis):
+    size = lax.axis_size(axis)
+    if size & (size - 1) or value.shape[0] % size:
         return lax.psum(value, axis)
+    me = lax.axis_index(axis)
+    parts = value.reshape((size, -1) + value.shape[1:])
+
+    def swap(item, k):
+        return lax.ppermute(item, axis, [(i, i ^ k) for i in range(size)])
+
+    total = lax.dynamic_index_in_dim(parts, me, keepdims=False).astype(F32)
+    for k in range(1, size):
+        total = total + swap(lax.dynamic_index_in_dim(parts, me ^ k, keepdims=False), k).astype(F32)
+    total = total.astype(value.dtype)
+    for k in range(size):
+        item = swap(total, k) if k else total
+        parts = lax.dynamic_update_index_in_dim(parts, item, me ^ k, 0)
+    return parts.reshape(value.shape)
+
+
+def doubled(value, axis):
+    size = lax.axis_size(axis)
+    if size & (size - 1):
+        return jnp.sum(lax.all_gather(value, axis), axis=0)
     bit = 1
     while bit < size:
-        other = lax.ppermute(value, axis, [(i, i ^ bit) for i in range(size)])
-        value = (value.astype(F32) + other.astype(F32)).astype(value.dtype)
+        value = value + lax.ppermute(value, axis, [(i, i ^ bit) for i in range(size)])
         bit *= 2
     return value
 
@@ -797,13 +851,14 @@
         ends.append(ends[-1] + piece.shape[1])
     small = [small[:, :, a:b].astype(F32) for a, b in zip(ends[:-1], ends[1:])]
     gains_in = small[0].transpose(1, 0, 2).reshape(layers, -1)
-    taps_all = small[1].reshape(shards, layers, CONV, -1).transpose(1, 0, 3, 2)
-    taps_all = taps_all.reshape(layers, channels, CONV)
-    bias_all = small[2].transpose(1, 0, 2).reshape(layers, channels, 1)
+    taps_all = small[1].reshape(shards, layers, CONV, -1).transpose(1, 2, 0, 3)
+    taps_all = taps_all.reshape(layers, CONV, channels)
+    bias_all = small[2].transpose(1, 0, 2).reshape(layers, 1, channels)
     taps_all = jnp.concatenate(
-        [taps_all, bias_all, jnp.zeros((layers, channels, 8 - CONV - 1), F32)], axis=2
+        [taps_all, bias_all, jnp.zeros((layers, 8 - CONV - 1, channels), F32)], axis=1
     )
-    gains_out = small[3].transpose(1, 0, 2).reshape(layers, inner, 1)
+    gains_out = small[3].transpose(1, 0, 2).reshape(layers, 1, inner)
+    gains_out = jnp.broadcast_to(gains_out, (layers, 8, inner))
 
     head_values = lax.all_gather(jnp.stack([dt_bias, a_log, skip]), "seq", axis=2, tiled=True)
     head_values = jnp.pad(head_values, ((0, 0), (0, 0), (0, padded - heads)))
@@ -837,6 +892,7 @@
         inverse = lax.rsqrt(jnp.mean(hidden * hidden, axis=0, keepdims=True) + EPS)
         normed = (hidden * inverse * gains_in[layer][:, None]).astype(BF)
         halo = dot(normed[:, rows - EDGE :], w_scan, 0, 0).astype(BF)
+        last_q = halo[EDGE - 8 :, :channels]
         halo = passed_along(halo, "seq", 1)
         qd = dot(w_scan, normed, 0, 0).astype(BF)
         xa, slope, part, enter, prefix, reach, pack = scan(
@@ -845,77 +901,89 @@
         packs = [passed_along(pack, "seq", k) for k in range(1, n_seq)]
         z = dot(w_gate, normed, 0, 0).astype(BF)
         yb, gated, device = gated_norm(packs, part, z, xa, reach, gain_out, heads)
-        saved.append((hidden, inverse, normed, qd, xa, slope, enter, prefix, reach, pack, z, yb, gated, device))
+        saved.append((last_q, hidden, inverse, normed, qd, xa, slope, enter, prefix, reach, pack, z, yb, gated, device))
         hidden = hidden + dot(w_out, gated, 0, 0)
     activations = hidden.astype(BF).T[None]
 
     grad = cotangent[0].T.astype(F32)
     results = [None] * layers
+    before_norm = []
     for layer in reversed(range(layers)):
         w_scan, w_gate, w_out = weights[layer]
         taps = taps_all[layer]
         bias, log_rate, skips = (head_values[k, layer] for k in range(3))
         gain_out = gains_out[layer]
         gain_in = gains_in[layer][:, None]
-        h_in, inverse, normed, qd, xa, slope, enter, prefix, reach, pack, z, yb, gated, device = saved[layer]
+        last_q, h_in, inverse, normed, qd, xa, slope, enter, prefix, reach, pack, z, yb, gated, device = saved[layer]
         go = grad.astype(BF)
         dy, dz, d_gain_out, back_pack = gated_norm_back(
-            go, w_out, yb, z, xa, reach, gain_out, pack, heads
+            go, w_out, yb, z, xa, reach, gain_out, pack, heads, before_norm
         )
         back_packs = [passed_along(back_pack, "seq", -k) for k in range(1, n_seq)]
         d_w_out = dot(gated, go, 1, 1).astype(BF)
         d_w_gate = dot(normed, dz, 1, 1).astype(BF)
-        share_out = lax.psum_scatter(d_w_out, "shard", scatter_dimension=0, tiled=True)
-        share_gate = lax.psum_scatter(d_w_gate, "shard", scatter_dimension=0, tiled=True)
+        joint = jnp.concatenate(
+            [d_w_out.reshape(shards, -1, width_d)]
+            + [
+                d_w_gate[:, at : at + width_d].reshape(shards, part_d, width_d)
+                for at in range(0, inner, width_d)
+            ],
+            axis=1,
+        )
+        share_joint = lax.psum_scatter(joint, "shard", scatter_dimension=0, tiled=True)[0]
+        d_normed = dot(w_gate, dz, 1, 0)
         dqd, d_conv, d_head, edge = scan_back(
-            back_packs, xa, slope, qd, dy, enter, device, prefix, taps, bias, log_rate, skips, info, heads
+            back_packs, xa, slope, qd, dy, enter, device, prefix, taps, bias, log_rate, skips, info, heads,
+            [joint, d_normed],
         )
         edge = passed_along(edge, "seq", -1)
-        d_normed = dot(w_gate, dz, 1, 0)
-        dqd, d_conv = edge_fix(dqd, qd, edge, taps, info, d_conv)
+        fix, d_taps = edge_terms(edge, last_q.astype(F32), taps, info)
+        dqd = edge_fix(dqd, fix, [])
         d_w_scan = dot(normed, dqd, 1, 1).astype(BF)
+        dqd, d_w_scan, share_joint = lax.optimization_barrier((dqd, d_w_scan, share_joint))
         share_scan = lax.psum_scatter(d_w_scan, "shard", scatter_dimension=0, tiled=True)
         d_normed = d_normed + dot(w_scan, dqd, 1, 0)
         scaled = d_normed * gain_in
         d_gain_in = jnp.sum(d_normed * h_in * inverse, axis=1)
         along = jnp.mean(scaled * h_in, axis=0, keepdims=True)
         grad = grad + scaled * inverse - h_in * (along * inverse * inverse * inverse)
-        shares = tuple(total_over(item, "seq") for item in (share_out, share_gate, share_scan))
-        vector = jnp.concatenate(
-            [
-                d_gain_in,
-                d_conv[:, : CONV + 1].T.reshape(-1),
-                d_gain_out[:, 0],
-                d_head[:heads, :3].T.reshape(-1),
-            ]
-        )
-        results[layer] = (shares, lax.psum(vector, ("seq", "shard")))
+        shares = (share_joint, total_over(share_scan, "seq"))
+        before_norm = [d_w_scan]
+        conv_rows = d_conv[: CONV + 1] + jnp.pad(d_taps, ((0, 2), (0, 0)))
+        pieces = [d_gain_in, conv_rows.reshape(-1), d_gain_out[0], d_head[:heads, :3].T.reshape(-1)]
+        results[layer] = (shares, pieces)
+    joint = jnp.concatenate([shares[0] for shares, _ in results])
+    joint = split_total_over(joint, "seq").astype(F32).reshape(layers, -1, width_d)
+    small = jnp.concatenate([item for _, pieces in results for item in pieces])
+    small = doubled(doubled(small, "shard"), "seq")
     which = lax.axis_index("shard")
 
     def own(vector, index, count):
         return lax.dynamic_slice_in_dim(vector, index * count, count)
 
     outs = [[] for _ in range(10)]
-    for (share_out, share_gate, share_scan), vector in results:
-        share_scan = share_scan.astype(F32)
-        at = 0
-        outs[0].append(own(vector[:width_d], which, width_d // shards))
+    part_i = inner // shards
+    part_c = channels // shards
+    at = 0
+    for share_joint, ((_, share_scan), _) in zip(joint, results):
+        share_gate = jnp.concatenate(
+            [share_joint[k : k + part_d] for k in range(part_i, share_joint.shape[0], part_d)], axis=1
+        )
+        outs[0].append(own(small[at : at + width_d], which, part_d))
         at += width_d
-        wide = channels - inner
-        outs[1].append(jnp.concatenate([share_gate.astype(F32), share_scan[:, :channels]], axis=1))
+        outs[1].append(jnp.concatenate([share_gate, share_scan[:, :channels]], axis=1))
         outs[2].append(share_scan[:, channels : channels + heads])
-        taps = vector[at : at + CONV * channels].reshape(CONV, channels)
-        outs[3].append(lax.dynamic_slice_in_dim(taps, which * (channels // shards), channels // shards, 1))
+        taps = small[at : at + CONV * channels].reshape(CONV, channels)
+        outs[3].append(lax.dynamic_slice_in_dim(taps, which * part_c, part_c, 1))
         at += CONV * channels
-        outs[4].append(own(vector[at : at + channels], which, channels // shards))
+        outs[4].append(own(small[at : at + channels], which, part_c))
         at += channels
-        gain = vector[at : at + inner]
+        outs[8].append(own(small[at : at + inner], which, part_i))
         at += inner
         for k in range(3):
-            outs[5 + k].append(own(vector[at : at + heads], place, heads // n_seq))
+            outs[5 + k].append(own(small[at : at + heads], place, heads // n_seq))
             at += heads
-        outs[8].append(own(gain, which, inner // shards))
-        outs[9].append(share_out.astype(F32))
+        outs[9].append(share_joint[:part_i])
     return (activations, grad.T[None]) + tuple(jnp.stack(item) for item in outs)
 
 

time: 816 us -> 563 us (0.69)
  waiting for transfers between devices: 332 us -> 114 us
  Pallas kernels: 185 us -> 165 us
  matrix products: 110 us -> 101 us
    reduce_scatter x4 -> x2, waiting for transfers between devices: 129 us -> 0.01 us  [body(): lax.psum_scatter(joint, 'shard', scatter_dimension=0, tiled=True)[0]]
    reduce_scatter x2, waiting for transfers between devices: 61.7 us -> 0.02 us  [body(): lax.psum_scatter(d_w_scan, 'shard', scatter_dimension=0, tiled=True)]
    psum x1 -> x0, waiting for transfers between devices: 55.7 us -> none  [body(): results[layer] = (shares, lax.psum(vector, ('seq', 'shard')))]
    pallas_call x6, Pallas kernels: 124 us -> 107 us  [the longest x2 67.3 us: scan_back(): pl.pallas_call(functools.partial(scan_back_kernel, heads, len(packs), len...]
    ppermute x12 -> x17, waiting for transfers between devices: 23.6 us -> 34 us  [the longest x6 25.7 us: total_over(): lax.ppermute(value, axis, [(i, i ^ k) for i in range(size)])]
    dot_general x18, matrix products: 110 us -> 101 us  [dot(): lax.dot_general(left, right, (((left_dim,), (right_dim,)), ((), ())), pre...]
    all_gather x2, waiting for transfers between devices: 22 us -> 31.3 us  [body(): lax.all_gather(scan_part, 'shard', axis=0, tiled=True)]
    ppermute x16, waiting for transfers between devices: 38.6 us -> 47.3 us  [passed_along(): return lax.ppermute(block, axis, route)]
  transfers between devices with their start and end apart: 41 -> 43, of which waited for: 22 -> 17; matrix products, arithmetic and copies ran while one was open for 20% -> 26% of each run, Pallas kernels for 8% -> 27%
where the time goes in v2:
time: 563 us; the launch traced here: 554 us
  Pallas kernels  165 us (29%)
  waiting for transfers between devices  114 us (20%)
  matrix products  101 us (18%)
  starting transfers between devices  54.4 us (10%)
  local copies, waits for them, and re-layouts  46.6 us (8%)
  other arithmetic  34.7 us (6%)
  blocking collectives  24 us (4%)
  between operations  15.7 us (3%)
    dot_general x18, matrix products, dot(): lax.dot_general(left, right, (((left_dim,), (right_dim,)), ((), ())), pre...  101 us
    pallas_call x2, Pallas kernels, scan_back(): pl.pallas_call(functools.partial(scan_back_kernel, heads, len(packs), len...  67.3 us
    ppermute x16, waiting for transfers between devices, passed_along(): return lax.ppermute(block, axis, route)  47.3 us
    pallas_call x2, Pallas kernels, scan(): pl.pallas_call(functools.partial(scan_kernel, heads, inner), grid=(steps,...  40.1 us
    pallas_call x2, Pallas kernels, gated_norm_back(): pl.pallas_call(functools.partial(norm_back_kernel, heads, len(after)), gr...  35 us
    ppermute x16, starting transfers between devices, passed_along(): return lax.ppermute(block, axis, route)  33.4 us
    all_gather x2, waiting for transfers between devices, body(): lax.all_gather(scan_part, 'shard', axis=0, tiled=True)  31.3 us
    ppermute x6, waiting for transfers between devices, total_over(): lax.ppermute(value, axis, [(i, i ^ k) for i in range(size)])  25.7 us
  transfers between devices with their start and end apart: 43, of which 17 were waited for; matrix products, arithmetic and copies ran while one was open for 26% of the time, Pallas kernels for 27%

profile of v2, /device:TPU:0, one launch (start us, length us, event | category | flops | bytes accessed | tf_op | source)
XLA Modules:
  0.0 554.4 jit_solution(1246964402008980414)
XLA Ops:
  16.4 15.8 %all-gather.5 = bf16[8,2,1408]{2,1,0:T(2,128)(2,1)S(1)} all-gather(bf16[1,2,1408]{2,1,0:T(2,128)(2,1)S(1)} %bitcast.294), channel_id=2, replica_groups=mesh['seq'=4,'shard'=8] {'shard'}, dimensions={0}, use_global_device_ids=true | all-gather | bytes 50688 | tf_op jit(solution)/shard_map/all_gather | solution.py:848
  32.6 8.1 %all_gather.30 = f32[3,2,24]{0,1,2:T(2,128)S(1)} all-gather(f32[3,2,6]{0,1,2:T(2,128)S(1)} %copy.122), channel_id=1, replica_groups=mesh['seq'=4,'shard'=8] {'seq'}, dimensions={2}, use_global_device_ids=true | all-gather | bytes 720 | tf_op jit(solution)/shard_map/all_gather | solution.py:863
  62.6 20.1 %scan_forward.2 = (bf16[1792,1024]{1,0:T(8,128)(2,1)}, bf16[1792,1024]{1,0:T(8,128)(2,1)}, bf16[1536,1024]{1,0:T(8,128)(2,1)}, bf16[8,1536,128]{2,1,0:T(8,128)(2...) custom-call(bf16[1824,1024]{1,0:T(8,128)(2,1)} %convolution_convert_fusion.3.qd_ref.refs_7_, ...), custom_call_target="tpu_custom_call" | custom-call | bytes 73800000 | tf_op jit(solution)/shard_map/scan_forward/pallas_call | solution.py:223
  96.5 8.9 %collective-permute-done.2.refs_1_ = bf16[1600,128]{1,0:T(8,128)(2,1)} collective-permute-done((bf16[1600,128]{1,0:T(8,128)(2,1)}, bf16[1600,128]{1,0:T(8,128)(2,1)}, u32[]{:S(2)}, u32[]{:S(2)}) %collective-permute-start.2) | collective-permute-done | bytes 409632 | tf_op jit(solution)/shard_map/ppermute | solution.py:753
  106.0 8.9 %gated_norm_forward.2 = (bf16[1536,1024]{1,0:T(8,128)(2,1)}, bf16[1536,1024]{1,0:T(8,128)(2,1)}, bf16[1536,128]{1,0:T(8,128)(2,1)}) custom-call(bf16[1600,128]{1,0:T(8,128)(2,1)} %collective-permute-done.1.refs_0_, bf16[1600,128]{1,0:T(8,128)(2,1)} %collective-permute-done.2.refs_1_, bf16[1600,128]{1,0:T(8,128)(2,1)} %collective-permute-done.3.refs_2_, ...), custom_call_target="tpu_custom_call" | custom-call | bytes 33210000 | tf_op jit(solution)/shard_map/gated_norm_forward/pallas_call | solution.py:321
  122.5 30.0 %all-gather.15.cloned.1.call-done = bf16[768,1824]{1,0:T(8,128)(2,1)} async-done(((bf16[96,1824]{1,0:T(8,128)(2,1)}), bf16[768,1824]{1,0:T(8,128)(2,1)}) %all-gather.15.cloned.1.call-update) | async-done | bytes 2801680 | tf_op jit(solution)/shard_map/all_gather | solution.py:879
  165.1 20.1 %scan_forward.3 = (bf16[1792,1024]{1,0:T(8,128)(2,1)}, bf16[1792,1024]{1,0:T(8,128)(2,1)}, bf16[1536,1024]{1,0:T(8,128)(2,1)}, bf16[8,1536,128]{2,1,0:T(8,128)(2...) custom-call(bf16[1824,1024]{1,0:T(8,128)(2,1)} %convolution_convert_fusion.1.qd_ref.refs_7_, ...), custom_call_target="tpu_custom_call" | custom-call | bytes 73800000 | tf_op jit(solution)/shard_map/scan_forward/pallas_call | solution.py:223
  198.8 9.1 %collective-permute-done.6.refs_1_ = bf16[1600,128]{1,0:T(8,128)(2,1)} collective-permute-done((bf16[1600,128]{1,0:T(8,128)(2,1)}, bf16[1600,128]{1,0:T(8,128)(2,1)}, u32[]{:S(2)}, u32[]{:S(2)}) %collective-permute-start.6) | collective-permute-done | bytes 409632 | tf_op jit(solution)/shard_map/ppermute | solution.py:753
  208.5 8.8 %gated_norm_forward.3 = (bf16[1536,1024]{1,0:T(8,128)(2,1)}, bf16[1536,1024]{1,0:T(8,128)(2,1)}, bf16[1536,128]{1,0:T(8,128)(2,1)}) custom-call(bf16[1600,128]{1,0:T(8,128)(2,1)} %collective-permute-done.5.refs_0_, bf16[1600,128]{1,0:T(8,128)(2,1)} %collective-permute-done.6.refs_1_, bf16[1600,128]{1,0:T(8,128)(2,1)} %collective-permute-done.7.refs_2_, ...), custom_call_target="tpu_custom_call" | custom-call | bytes 33210000 | tf_op jit(solution)/shard_map/gated_norm_forward/pallas_call | solution.py:321
  217.4 17.4 %gated_norm_backward.2 = (bf16[1536,1024]{1,0:T(8,128)(2,1)}, bf16[1536,1024]{1,0:T(8,128)(2,1)}, f32[8,1536]{1,0:T(8,128)}, bf16[1600,128]{1,0:T(8,128)(2,1)}) custom-call(bf16[768,1024]{1,0:T(8,128)(2,1)} %bitcast.277, bf16[1536,768]{1,0:T(8,128)(2,1)} %bitcast.287, bf16[1536,1024]{1,0:T(8,128)(2,1)} %get-tuple-element.64.refs_2_, ...), custom_call_target="tpu_custom_call" | custom-call | bytes 62730000 | tf_op jit(solution)/shard_map/gated_norm_backward/pallas_call | solution.py:430
  251.7 7.2 %fusion.22 = f32[1024,768]{0,1:T(8,128)} fusion(bf16[1536,1024]{1,0:T(8,128)(2,1)} %get-tuple-element.65, bf16[1,768,1536]{2,1,0:T(8,128)(2,1)} %all-gather.21.cloned.1.call-done), kind=kOutput, calls=%fused_computation.46 | convolution fusion | flops 2415919104 | bytes 8650752 | tf_op jit(solution)/shard_map/dot_general | solution.py:26
  262.8 7.3 %collective-permute-done.9.refs_1_ = bf16[1600,128]{1,0:T(8,128)(2,1)S(1)} collective-permute-done((bf16[1600,128]{1,0:T(8,128)(2,1)}, bf16[1600,128]{1,0:T(8,128)(2,1)S(1)}, u32[]{:S(2)}, u32[]{:S(2)}) %collective-permute-start.9) | collective-permute-done | bytes 409632 | tf_op jit(solution)/shard_map/ppermute | solution.py:753
  270.9 33.7 %scan_backward.2 = (bf16[1824,1024]{1,0:T(8,128)(2,1)}, f32[8,1792]{1,0:T(8,128)}, f32[32,8]{1,0:T(8,128)}, f32[8,1792]{1,0:T(8,128)}) custom-call(bf16[1600,128]{1,0:T(8,128)(2,1)} %copy-done.23, bf16[1600,128]{1,0:T(8,128)(2,1)} %copy-done.22, bf16[1600,128]{1,0:T(8,128)(2,1)} %copy-done.20, bf16[8,384,768]{2,1,0:T(8,128)(2,1)} %pad_maximum_fusion.refs_3_, ...), custom_call_target="tpu_custom_call" | custom-call | bytes 121770000 | tf_op jit(solution)/shard_map/scan_backward/pallas_call | solution.py:661
  313.8 6.8 %convolution_convert_fusion.7.refs_0_ = bf16[768,1824]{1,0:T(8,128)(2,1)} fusion(bf16[768,1024]{1,0:T(8,128)(2,1)S(1)} %multiply_convert_fusion, bf16[1824,1024]{1,0:T(8,128)(2,1)} %edge_gradient.2), kind=kOutput, calls=%fused_computation.17 | convolution fusion | flops 2870304768 | bytes 8110080 | tf_op jit(solution)/shard_map/dot_general | solution.py:26
  320.9 9.4 %multiply_reduce_fusion = (f32[768]{0:T(1024)}, f32[1024]{0:T(1024)S(1)}, f32[768,1024]{1,0:T(8,128)S(1)}) fusion(f32[1024]{0:T(1024)S(1)} %add_rsqrt_fusion, f32[1024,768]{0,1:T(8,128)} %fusion.22, f32[1024,768]{0,1:T(8,128)} %copy-done, bf16[1,1024,768]{1,2,0:T(8,128)(2,1)S(1)} %copy.118, f32[768]{0:T(1024)S(1)} %mul.339, ...), kind=kOutput, calls=%fused_computation.39 | convolution fusion | flops 2875980032 | bytes 17561600 | tf_op jit(solution)/shard_map/dot_general | solution.py:26
  332.7 17.6 %gated_norm_backward.3 = (bf16[1536,1024]{1,0:T(8,128)(2,1)}, bf16[1536,1024]{1,0:T(8,128)(2,1)}, f32[8,1536]{1,0:T(8,128)}, bf16[1600,128]{1,0:T(8,128)(2,1)}) custom-call(bf16[768,1824]{1,0:T(8,128)(2,1)} %convolution_convert_fusion.7.refs_0_, bf16[768,1024]{1,0:T(8,128)(2,1)} %subtract_convert_fusion.refs_1_, bf16[1536,768]{1,0:T(8,128)(2,1)} %bitcast.288, ...), custom_call_target="tpu_custom_call" | custom-call | bytes 62730000 | tf_op jit(solution)/shard_map/gated_norm_backward/pallas_call | solution.py:430
  363.0 7.4 %fusion.29 = bf16[1,1024,768]{1,2,0:T(8,128)(2,1)} fusion(bf16[1536,1024]{1,0:T(8,128)(2,1)} %get-tuple-element.63, f32[1024,768]{0,1:T(8,128)} %copy-done, bf16[1,1024,768]{1,2,0:T(8,128)(2,1)S(1)} %copy.118, bf16[1,1536,768]{2,1,0:T(8,128)(2,1)} %all-gather.23.cloned.1.call-done), kind=kOutput, calls=%fused_computation.55 | convolution fusion | flops 2419064832 | bytes 11796480 | tf_op jit(solution)/shard_map/dot_general | solution.py:26
  380.4 6.9 %fusion.25 = f32[1024,768]{0,1:T(8,128)} fusion(bf16[1536,1024]{1,0:T(8,128)(2,1)} %get-tuple-element.77, bf16[1,768,1536]{2,1,0:T(8,128)(2,1)} %all-gather.17.cloned.1.call-done), kind=kOutput, calls=%fused_computation.49 | convolution fusion | flops 2415919104 | bytes 8650752 | tf_op jit(solution)/shard_map/dot_general | solution.py:26
  390.5 6.7 %collective-permute-done.13.refs_1_ = bf16[1600,128]{1,0:T(8,128)(2,1)S(1)} collective-permute-done((bf16[1600,128]{1,0:T(8,128)(2,1)}, bf16[1600,128]{1,0:T(8,128)(2,1)S(1)}, u32[]{:S(2)}, u32[]{:S(2)}) %collective-permute-start.13) | collective-permute-done | bytes 409632 | tf_op jit(solution)/shard_map/ppermute | solution.py:753
  398.1 33.6 %scan_backward.3 = (bf16[1824,1024]{1,0:T(8,128)(2,1)}, f32[8,1792]{1,0:T(8,128)}, f32[32,8]{1,0:T(8,128)}, f32[8,1792]{1,0:T(8,128)}) custom-call(bf16[1600,128]{1,0:T(8,128)(2,1)} %copy-done.21, bf16[1600,128]{1,0:T(8,128)(2,1)} %copy-done.19, bf16[1600,128]{1,0:T(8,128)(2,1)} %copy-done.18, bf16[8,384,768]{2,1,0:T(8,128)(2,1)} %pad_maximum_fusion.1.refs_3_, ...), custom_call_target="tpu_custom_call" | custom-call | bytes 121770000 | tf_op jit(solution)/shard_map/scan_backward/pallas_call | solution.py:661
  443.8 6.8 %convolution_convert_fusion.4 = bf16[768,1824]{1,0:T(8,128)(2,1)} fusion(bf16[768,1024]{1,0:T(8,128)(2,1)S(1)} %copy-done.14, bf16[1824,1024]{1,0:T(8,128)(2,1)} %edge_gradient.3), kind=kOutput, calls=%fused_computation.14 | convolution fusion | flops 2870304768 | bytes 8110080 | tf_op jit(solution)/shard_map/dot_general | solution.py:26
  471.6 9.2 %fusion.12 = (f32[768]{0:T(1024)S(1)}, f32[1024]{0:T(1024)S(1)}, f32[768,1024]{1,0:T(8,128)}) fusion(bf16[1,1024,768]{1,2,0:T(8,128)(2,1)S(1)} %copy.118, f32[1024]{0:T(1024)} %copy-done.31, f32[1024,768]{0,1:T(8,128)} %fusion.25, f32[768]{0:T(1024)} %copy-done.30, bf16[768,1824]{1,0:T(8,128)(2,1)} %all-gather.13.cloned.1.call-done, ...), kind=kOutput, calls=%fused_computation.27 | convolution fusion | flops 2875193600 | bytes 14415872 | tf_op jit(solution)/shard_map/dot_general | solution.py:26
  490.3 7.0 %fusion.14 = f32[1,1024,768]{1,2,0:T(8,128)} fusion(f32[1024,768]{0,1:T(8,128)} %fusion.25, f32[768,1024]{1,0:T(8,128)} %get-tuple-element.237, f32[1024,768]{0,1:T(8,128)} %fusion.22, f32[768,1024]{1,0:T(8,128)} %copy-done.7, f32[1024,768]{0,1:T(8,128)S(1)} %copy-done.2, bf16[1,1024,768]{1,2,0:T(8,128)(2,1)S(1)} %copy-done.4, ...), kind=kLoop, calls=%fused_computation.29 | loop fusion | flops 11796480 | bytes 22042624 | tf_op jit(solution)/shard_map/broadcast_in_dim | solution.py:987
  528.3 9.1 %collective-permute-done.29 = bf16[96,1824]{1,0:T(8,128)(2,1)S(1)} collective-permute-done((bf16[96,1824]{1,0:T(8,128)(2,1)}, bf16[96,1824]{1,0:T(8,128)(2,1)S(1)}, u32[]{:S(2)}, u32[]{:S(2)}) %collective-permute-start.29) | collective-permute-done | bytes 350240 | tf_op jit(solution)/shard_map/ppermute | solution.py:761
  (359 shorter events, 222.6 us)
Async XLA Ops:
  7.2 42.8 %all-gather.13.cloned.1.call-start = ((), (), s32[]{:S(2)}) async-start(), calls=%async_computation.4 | async-start | bytes 3317760 | tf_op jit(solution)/shard_map/all_gather | solution.py:879
  10.2 80.3 %all-gather.17.cloned.1.call-start = ((), (), s32[]{:S(2)}) async-start(), calls=%async_computation.10 | async-start | bytes 2654208 | tf_op jit(solution)/shard_map/all_gather | solution.py:880
  12.3 102.6 %all-gather.19.cloned.1.call-start = ((), (), s32[]{:S(2)}) async-start(), calls=%async_computation.11 | async-start | bytes 2654208 | tf_op jit(solution)/shard_map/all_gather | solution.py:881
  13.3 139.2 %all-gather.15.cloned.1.call-start = ((), (), s32[]{:S(2)}) async-start(), calls=%async_computation.5 | async-start | bytes 3317760 | tf_op jit(solution)/shard_map/all_gather | solution.py:879
  14.3 178.8 %all-gather.21.cloned.1.call-start = ((), (), s32[]{:S(2)}) async-start(), calls=%async_computation.12 | async-start | bytes 2654208 | tf_op jit(solution)/shard_map/all_gather | solution.py:880
  14.9 202.5 %all-gather.23.cloned.1.call-start = ((), (), s32[]{:S(2)}) async-start(), calls=%async_computation.13 | async-start | bytes 2654208 | tf_op jit(solution)/shard_map/all_gather | solution.py:881
  15.4 305.2 %reduce-scatter.5.cloned.1.call-start = ((), (), s32[]{:S(2)}) async-start(), calls=%async_computation.6 | async-start | bytes 5308416 | tf_op jit(solution)/shard_map/reduce_scatter | solution.py:933
  85.8 19.6 %collective-permute-start.2 = (bf16[1600,128]{1,0:T(8,128)(2,1)}, bf16[1600,128]{1,0:T(8,128)(2,1)}, u32[]{:S(2)}, u32[]{:S(2)}) collective-permute-start(bf16[1600,128]{1,0:T(8,128)(2,1)} %get-tuple-element.54.refs_8_), channel_id=1, source_target_pairs={{0,16},{8,24},{1,17},{9,25},{2,18},{10,26},{3,19},{11,27},{4,20},{... | collective-permute-start | bytes 1228808 | tf_op jit(solution)/shard_map/ppermute | solution.py:753
  88.2 17.2 %collective-permute-start.1 = (bf16[1600,128]{1,0:T(8,128)(2,1)}, bf16[1600,128]{1,0:T(8,128)(2,1)}, u32[]{:S(2)}, u32[]{:S(2)}) collective-permute-start(bf16[1600,128]{1,0:T(8,128)(2,1)} %get-tuple-element.54.refs_8_), channel_id=1, source_target_pairs={{0,8},{8,16},{16,24},{1,9},{9,17},{17,25},{2,10},{10,18},{18,26},{... | collective-permute-start | bytes 1228808 | tf_op jit(solution)/shard_map/ppermute | solution.py:753
  188.3 19.6 %collective-permute-start.6 = (bf16[1600,128]{1,0:T(8,128)(2,1)}, bf16[1600,128]{1,0:T(8,128)(2,1)}, u32[]{:S(2)}, u32[]{:S(2)}) collective-permute-start(bf16[1600,128]{1,0:T(8,128)(2,1)} %get-tuple-element.59.refs_7_), channel_id=1, source_target_pairs={{0,16},{8,24},{1,17},{9,25},{2,18},{10,26},{3,19},{11,27},{4,20},{... | collective-permute-start | bytes 1228808 | tf_op jit(solution)/shard_map/ppermute | solution.py:753
  190.7 17.2 %collective-permute-start.5 = (bf16[1600,128]{1,0:T(8,128)(2,1)}, bf16[1600,128]{1,0:T(8,128)(2,1)}, u32[]{:S(2)}, u32[]{:S(2)}) collective-permute-start(bf16[1600,128]{1,0:T(8,128)(2,1)} %get-tuple-element.59.refs_7_), channel_id=1, source_target_pairs={{0,8},{8,16},{16,24},{1,9},{9,17},{17,25},{2,10},{10,18},{18,26},{... | collective-permute-start | bytes 1228808 | tf_op jit(solution)/shard_map/ppermute | solution.py:753
  247.2 203.5 %reduce-scatter.11.cloned.1.call-start = ((), (), s32[]{:S(2)}) async-start(), calls=%async_computation.9 | async-start | bytes 3317760 | tf_op jit(solution)/shard_map/reduce_scatter | solution.py:944
  247.4 15.4 %collective-permute-start.10 = (bf16[1600,128]{1,0:T(8,128)(2,1)}, bf16[1600,128]{1,0:T(8,128)(2,1)S(1)}, u32[]{:S(2)}, u32[]{:S(2)}) collective-permute-start(bf16[1600,128]{1,0:T(8,128)(2,1)} %get-tuple-element.66), channel_id=1, source_target_pairs={{24,0},{25,1},{26,2},{27,3},{28,4},{29,5},{30,6},{31,7}} | collective-permute-start | bytes 1228808 | tf_op jit(solution)/shard_map/ppermute | solution.py:753
  248.6 21.4 %collective-permute-start.9 = (bf16[1600,128]{1,0:T(8,128)(2,1)}, bf16[1600,128]{1,0:T(8,128)(2,1)S(1)}, u32[]{:S(2)}, u32[]{:S(2)}) collective-permute-start(bf16[1600,128]{1,0:T(8,128)(2,1)} %get-tuple-element.66), channel_id=1, source_target_pairs={{16,0},{24,8},{17,1},{25,9},{18,2},{26,10},{19,3},{27,11},{20,4},{... | collective-permute-start | bytes 1228808 | tf_op jit(solution)/shard_map/ppermute | solution.py:753
  249.9 20.1 %collective-permute-start.8 = (bf16[1600,128]{1,0:T(8,128)(2,1)}, bf16[1600,128]{1,0:T(8,128)(2,1)S(1)}, u32[]{:S(2)}, u32[]{:S(2)}) collective-permute-start(bf16[1600,128]{1,0:T(8,128)(2,1)} %get-tuple-element.66), channel_id=1, source_target_pairs={{8,0},{16,8},{24,16},{9,1},{17,9},{25,17},{10,2},{18,10},{26,18},{... | collective-permute-start | bytes 1228808 | tf_op jit(solution)/shard_map/ppermute | solution.py:753
  320.7 150.8 %reduce-scatter.7.cloned.1.call-start = ((), (), s32[]{:S(2)}) async-start(), calls=%async_computation.7 | async-start | bytes 5308416 | tf_op jit(solution)/shard_map/reduce_scatter | solution.py:933
  362.7 162.0 %reduce-scatter.9.cloned.1.call-start = ((), (), s32[]{:S(2)}) async-start(), calls=%async_computation.8 | async-start | bytes 3317760 | tf_op jit(solution)/shard_map/reduce_scatter | solution.py:944
  376.4 20.8 %collective-permute-start.13 = (bf16[1600,128]{1,0:T(8,128)(2,1)}, bf16[1600,128]{1,0:T(8,128)(2,1)S(1)}, u32[]{:S(2)}, u32[]{:S(2)}) collective-permute-start(bf16[1600,128]{1,0:T(8,128)(2,1)} %get-tuple-element.78), channel_id=1, source_target_pairs={{16,0},{24,8},{17,1},{25,9},{18,2},{26,10},{19,3},{27,11},{20,4},{... | collective-permute-start | bytes 1228808 | tf_op jit(solution)/shard_map/ppermute | solution.py:753
  377.7 19.6 %collective-permute-start.12 = (bf16[1600,128]{1,0:T(8,128)(2,1)}, bf16[1600,128]{1,0:T(8,128)(2,1)S(1)}, u32[]{:S(2)}, u32[]{:S(2)}) collective-permute-start(bf16[1600,128]{1,0:T(8,128)(2,1)} %get-tuple-element.78), channel_id=1, source_target_pairs={{8,0},{16,8},{24,16},{9,1},{17,9},{25,17},{10,2},{18,10},{26,18},{... | collective-permute-start | bytes 1228808 | tf_op jit(solution)/shard_map/ppermute | solution.py:753
  450.6 17.9 %collective-permute-start.31 = (bf16[96,1824]{1,0:T(8,128)(2,1)}, bf16[96,1824]{1,0:T(8,128)(2,1)}, u32[]{:S(2)}, u32[]{:S(2)}) collective-permute-start(bf16[96,1824]{1,0:T(8,128)(2,1)} %reduce-scatter.11.cloned.1.call-done), channel_id=1, source_target_pairs={{0,16},{8,24},{16,0},{24,8},{1,17},{9,25},{17,1},{25,9},{2,18},{10... | collective-permute-start | bytes 1050632 | tf_op jit(solution)/shard_map/ppermute | solution.py:761
  485.2 18.0 %collective-permute-start.21 = (bf16[192,768]{1,0:T(8,128)(2,1)}, bf16[192,768]{1,0:T(8,128)(2,1)}, u32[]{:S(2)}, u32[]{:S(2)}) collective-permute-start(bf16[192,768]{1,0:T(8,128)(2,1)} %get-tuple-element.199), channel_id=1, source_target_pairs={{0,8},{8,0},{16,24},{24,16},{1,9},{9,1},{17,25},{25,17},{2,10},{10... | collective-permute-start | bytes 884744 | tf_op jit(solution)/shard_map/ppermute | solution.py:777
  486.5 16.6 %collective-permute-start.23 = (bf16[192,768]{1,0:T(8,128)(2,1)}, bf16[192,768]{1,0:T(8,128)(2,1)}, u32[]{:S(2)}, u32[]{:S(2)}) collective-permute-start(bf16[192,768]{1,0:T(8,128)(2,1)} %get-tuple-element.200), channel_id=1, source_target_pairs={{0,24},{8,16},{16,8},{24,0},{1,25},{9,17},{17,9},{25,1},{2,26},{10... | collective-permute-start | bytes 884744 | tf_op jit(solution)/shard_map/ppermute | solution.py:777
  526.5 16.9 %collective-permute-start.28 = (bf16[96,1824]{1,0:T(8,128)(2,1)}, bf16[96,1824]{1,0:T(8,128)(2,1)S(1)}, u32[]{:S(2)}, u32[]{:S(2)}) collective-permute-start(bf16[96,1824]{1,0:T(8,128)(2,1)} %reduce-scatter.9.cloned.1.call-done), channel_id=1, source_target_pairs={{0,16},{8,24},{16,0},{24,8},{1,17},{9,25},{17,1},{25,9},{2,18},{10... | collective-permute-start | bytes 1050632 | tf_op jit(solution)/shard_map/ppermute | solution.py:761
  527.2 16.2 %collective-permute-start.27 = (bf16[96,1824]{1,0:T(8,128)(2,1)}, bf16[96,1824]{1,0:T(8,128)(2,1)S(1)}, u32[]{:S(2)}, u32[]{:S(2)}) collective-permute-start(bf16[96,1824]{1,0:T(8,128)(2,1)} %reduce-scatter.9.cloned.1.call-done), channel_id=1, source_target_pairs={{0,8},{8,0},{16,24},{24,16},{1,9},{9,1},{17,25},{25,17},{2,10},{10... | collective-permute-start | bytes 1050632 | tf_op jit(solution)/shard_map/ppermute | solution.py:761
  (70 other events, 814.1 us)
Sparse Core Ops, SparseCore 0:
  10.3 39.5 all-gather.12
  51.6 30.5 all-gather.16
  83.8 30.7 all-gather.18
  116.7 35.7 all-gather.14
  154.0 30.4 all-gather.20
  186.0 30.7 all-gather.22
  247.3 53.9 reduce-scatter.4
  320.8 38.4 reduce-scatter.10
  362.8 54.5 reduce-scatter.6
  481.6 39.2 reduce-scatter.8

commit v3 on v2

--- a/solution.py
+++ b/solution.py
@@ -708,6 +708,95 @@
     )(*packs, *after, xa, slope, qd, dy, enter, device, prefix, taps, bias, log_rate, skip, info)
 
 
+def input_back_kernel(
+    token_major,
+    w_ref,
+    dqd_ref,
+    part_ref,
+    h_ref,
+    gain_ref,
+    grad_ref,
+    out_ref,
+    *refs,
+):
+    go_refs, (dgain_ref, d_norm, dgain, gain) = refs[:-4], refs[-4:]
+    step_at = pl.program_id(0)
+    last = pl.num_programs(0) - 1
+    depth, lanes = h_ref.shape
+
+    @pl.when(step_at == 0)
+    def _():
+        for at in range(0, depth, CHUNK):
+            gain[at : at + CHUNK, :] = column_of(gain_ref, at)[:, 0:1]
+        dgain[...] = jnp.zeros_like(dgain)
+
+    d_norm[...] = dot(w_ref[...], dqd_ref[...], 1, 0) + part_ref[...]
+    squares = jnp.zeros((CHUNK, lanes), F32)
+    crosses = jnp.zeros((CHUNK, lanes), F32)
+    for at in range(0, depth, CHUNK):
+        rows = pl.ds(at, CHUNK)
+        h = h_ref[rows, :]
+        squares = squares + h * h
+        crosses = crosses + d_norm[rows, :] * gain[rows, :] * h
+    inverse = lax.rsqrt(col_sum(squares) * (1.0 / depth) + EPS)
+    along = col_sum(crosses) * (1.0 / depth) * inverse * inverse * inverse
+    for at in range(0, depth, CHUNK):
+        rows = pl.ds(at, CHUNK)
+        h = h_ref[rows, :]
+        scaled = d_norm[rows, :] * inverse
+        dgain[rows, :] += scaled * h
+        grad = grad_ref[rows, :] + scaled * gain[rows, :] - h * along
+        if token_major:
+            for lane in range(0, lanes, CHUNK):
+                out_ref[lane : lane + CHUNK, at : at + CHUNK] = jnp.transpose(
+                    grad[:, lane : lane + CHUNK]
+                )
+        else:
+            out_ref[rows, :] = grad
+            go_refs[0][rows, :] = grad.astype(BF)
+
+    @pl.when(step_at == last)
+    def _():
+        for at in range(0, depth, CHUNK):
+            total = jnp.sum(dgain[at : at + CHUNK, :], axis=1, keepdims=True)
+            total = jnp.transpose(jnp.broadcast_to(total, (CHUNK, CHUNK)))
+            dgain_ref[:, at : at + CHUNK] = total[0:8]
+
+
+def input_back(w_scan, dqd, part, hidden, gain, grad, token_major):
+    depth, length = hidden.shape
+    lanes = math.gcd(length, STEP)
+    out_specs = [lane_block(depth, lanes), lane_block(depth, lanes)]
+    out_shape = [
+        jax.ShapeDtypeStruct((depth, length), F32),
+        jax.ShapeDtypeStruct((depth, length), BF),
+    ]
+    if token_major:
+        out_specs = [pl.BlockSpec((lanes, depth), lambda i: (i, 0))]
+        out_shape = [jax.ShapeDtypeStruct((length, depth), F32)]
+    return pl.pallas_call(
+        functools.partial(input_back_kernel, token_major),
+        grid=(length // lanes,),
+        in_specs=[
+            whole_block(w_scan.shape),
+            lane_block(dqd.shape[0], lanes),
+            lane_block(depth, lanes),
+            lane_block(depth, lanes),
+            whole_block(gain.shape),
+            lane_block(depth, lanes),
+        ],
+        out_specs=out_specs + [whole_block((8, depth))],
+        out_shape=out_shape + [jax.ShapeDtypeStruct((8, depth), F32)],
+        scratch_shapes=[
+            pltpu.VMEM((depth, lanes), F32),
+            pltpu.VMEM((depth, lanes), F32),
+            pltpu.VMEM((depth, 1), F32),
+        ],
+        compiler_params=pltpu.CompilerParams(vmem_limit_bytes=VMEM),
+        name="input_backward",
+    )(w_scan, dqd, part, hidden, gain, grad)
+
+
 def edge_kernel(n_after, dqd_ref, fix_ref, *refs):
     out_ref = refs[n_after]
     channels = fix_ref.shape[1]
@@ -901,11 +990,12 @@
         packs = [passed_along(pack, "seq", k) for k in range(1, n_seq)]
         z = dot(w_gate, normed, 0, 0).astype(BF)
         yb, gated, device = gated_norm(packs, part, z, xa, reach, gain_out, heads)
-        saved.append((last_q, hidden, inverse, normed, qd, xa, slope, enter, prefix, reach, pack, z, yb, gated, device))
+        saved.append((last_q, hidden, normed, qd, xa, slope, enter, prefix, reach, pack, z, yb, gated, device))
         hidden = hidden + dot(w_out, gated, 0, 0)
     activations = hidden.astype(BF).T[None]
 
-    grad = cotangent[0].T.astype(F32)
+    go = cotangent[0].T
+    grad = go.astype(F32)
     results = [None] * layers
     before_norm = []
     for layer in reversed(range(layers)):
@@ -913,9 +1003,8 @@
         taps = taps_all[layer]
         bias, log_rate, skips = (head_values[k, layer] for k in range(3))
         gain_out = gains_out[layer]
-        gain_in = gains_in[layer][:, None]
-        last_q, h_in, inverse, normed, qd, xa, slope, enter, prefix, reach, pack, z, yb, gated, device = saved[layer]
-        go = grad.astype(BF)
+        gain_in = jnp.broadcast_to(gains_in[layer][None], (8, width_d))
+        last_q, h_in, normed, qd, xa, slope, enter, prefix, reach, pack, z, yb, gated, device = saved[layer]
         dy, dz, d_gain_out, back_pack = gated_norm_back(
             go, w_out, yb, z, xa, reach, gain_out, pack, heads, before_norm
         )
@@ -942,11 +1031,12 @@
         d_w_scan = dot(normed, dqd, 1, 1).astype(BF)
         dqd, d_w_scan, share_joint = lax.optimization_barrier((dqd, d_w_scan, share_joint))
         share_scan = lax.psum_scatter(d_w_scan, "shard", scatter_dimension=0, tiled=True)
-        d_normed = d_normed + dot(w_scan, dqd, 1, 0)
-        scaled = d_normed * gain_in
-        d_gain_in = jnp.sum(d_normed * h_in * inverse, axis=1)
-        along = jnp.mean(scaled * h_in, axis=0, keepdims=True)
-        grad = grad + scaled * inverse - h_in * (along * inverse * inverse * inverse)
+        grad, *low, d_gain_in = input_back(
+            w_scan, dqd, d_normed, h_in, gain_in, grad, layer == 0
+        )
+        if low:
+            go = low[0]
+        d_gain_in = d_gain_in[0]
         shares = (share_joint, total_over(share_scan, "seq"))
         before_norm = [d_w_scan]
         conv_rows = d_conv[: CONV + 1] + jnp.pad(d_taps, ((0, 2), (0, 0)))
@@ -984,7 +1074,7 @@
             outs[5 + k].append(own(small[at : at + heads], place, heads // n_seq))
             at += heads
         outs[9].append(share_joint[:part_i])
-    return (activations, grad.T[None]) + tuple(jnp.stack(item) for item in outs)
+    return (activations, grad[None]) + tuple(jnp.stack(item) for item in outs)
 
 
 def solution(mesh):

time: 563 us -> 549 us (0.975)
  Pallas kernels: 165 us -> 187 us
  matrix products: 101 us -> 82.8 us
  other arithmetic: 34.7 us -> 24.7 us
  local copies, waits for them, and re-layouts: 46.6 us -> 39.4 us
    pallas_call x0 -> x2, Pallas kernels: none -> 22.4 us  [input_back(): pl.pallas_call(functools.partial(input_back_kernel, token_major), grid=(l...]
    dot_general x18 -> x16, matrix products: 101 us -> 82.8 us  [dot(): lax.dot_general(left, right, (((left_dim,), (right_dim,)), ((), ())), pre...]
    ppermute x5, waiting for transfers between devices: 7.49 us -> 20.7 us  [doubled(): lax.ppermute(value, axis, [(i, i ^ bit) for i in range(size)])]
    ppermute x6, waiting for transfers between devices: 25.7 us -> 13.6 us  [total_over(): lax.ppermute(value, axis, [(i, i ^ k) for i in range(size)])]
    broadcast_in_dim x1 -> x0, other arithmetic: 6.98 us -> none  [body(): grad.T[None]]
    unnamed x104 -> x81, local copies, waits for them, and re-layouts: 18.4 us -> 14.7 us
  transfers between devices with their start and end apart: 43 -> 43, of which waited for: 17 -> 18; matrix products, arithmetic and copies ran while one was open for 26% -> 23% of each run, Pallas kernels for 27% -> 31%
where the time goes in v3:
time: 549 us; the launch traced here: 540 us
  Pallas kernels  187 us (34%)
  waiting for transfers between devices  114 us (21%)
  matrix products  82.8 us (15%)
  starting transfers between devices  52 us (9%)
  local copies, waits for them, and re-layouts  39.4 us (7%)
  other arithmetic  24.7 us (4%)
  blocking collectives  24 us (4%)
  between operations  15.7 us (3%)
    dot_general x16, matrix products, dot(): lax.dot_general(left, right, (((left_dim,), (right_dim,)), ((), ())), pre...  82.8 us
    pallas_call x2, Pallas kernels, scan_back(): pl.pallas_call(functools.partial(scan_back_kernel, heads, len(packs), len...  67.3 us
    ppermute x16, waiting for transfers between devices, passed_along(): return lax.ppermute(block, axis, route)  47.6 us
    pallas_call x2, Pallas kernels, scan(): pl.pallas_call(functools.partial(scan_kernel, heads, inner), grid=(steps,...  40.2 us
    pallas_call x2, Pallas kernels, gated_norm_back(): pl.pallas_call(functools.partial(norm_back_kernel, heads, len(after)), gr...  35.2 us
    ppermute x16, starting transfers between devices, passed_along(): return lax.ppermute(block, axis, route)  34.8 us
    all_gather x2, waiting for transfers between devices, body(): lax.all_gather(scan_part, 'shard', axis=0, tiled=True)  30.3 us
    pallas_call x2, Pallas kernels, input_back(): pl.pallas_call(functools.partial(input_back_kernel, token_major), grid=(l...  22.4 us
  transfers between devices with their start and end apart: 43, of which 18 were waited for; matrix products, arithmetic and copies ran while one was open for 23% of the time, Pallas kernels for 31%

profile of v3, /device:TPU:0, one launch (start us, length us, event | category | flops | bytes accessed | tf_op | source)
XLA Modules:
  0.0 540.1 jit_solution(1371225363907900864)
XLA Ops:
  15.7 15.9 %all-gather.5 = bf16[8,2,1408]{2,1,0:T(2,128)(2,1)S(1)} all-gather(bf16[1,2,1408]{2,1,0:T(2,128)(2,1)S(1)} %bitcast.216), channel_id=2, replica_groups=mesh['seq'=4,'shard'=8] {'shard'}, dimensions={0}, use_global_device_ids=true | all-gather | bytes 50688 | tf_op jit(solution)/shard_map/all_gather | solution.py:937
  35.2 8.1 %all_gather.30 = f32[3,2,24]{0,1,2:T(2,128)S(1)} all-gather(f32[3,2,6]{0,1,2:T(2,128)S(1)} %copy.110), channel_id=1, replica_groups=mesh['seq'=4,'shard'=8] {'seq'}, dimensions={2}, use_global_device_ids=true | all-gather | bytes 720 | tf_op jit(solution)/shard_map/all_gather | solution.py:952
  62.6 20.1 %scan_forward.2 = (bf16[1792,1024]{1,0:T(8,128)(2,1)}, bf16[1792,1024]{1,0:T(8,128)(2,1)}, bf16[1536,1024]{1,0:T(8,128)(2,1)}, bf16[8,1536,128]{2,1,0:T(8,128)(2...) custom-call(bf16[1824,1024]{1,0:T(8,128)(2,1)} %convolution_convert_fusion.3.qd_ref.refs_7_, ...), custom_call_target="tpu_custom_call" | custom-call | bytes 73800000 | tf_op jit(solution)/shard_map/scan_forward/pallas_call | solution.py:223
  96.9 8.0 %collective-permute-done.2.refs_1_ = bf16[1600,128]{1,0:T(8,128)(2,1)} collective-permute-done((bf16[1600,128]{1,0:T(8,128)(2,1)}, bf16[1600,128]{1,0:T(8,128)(2,1)}, u32[]{:S(2)}, u32[]{:S(2)}) %collective-permute-start.2) | collective-permute-done | bytes 409632 | tf_op jit(solution)/shard_map/ppermute | solution.py:842
  105.5 8.9 %gated_norm_forward.2 = (bf16[1536,1024]{1,0:T(8,128)(2,1)}, bf16[1536,1024]{1,0:T(8,128)(2,1)}, bf16[1536,128]{1,0:T(8,128)(2,1)}) custom-call(bf16[1600,128]{1,0:T(8,128)(2,1)} %collective-permute-done.1.refs_0_, bf16[1600,128]{1,0:T(8,128)(2,1)} %collective-permute-done.2.refs_1_, bf16[1600,128]{1,0:T(8,128)(2,1)} %collective-permute-done.3.refs_2_, ...), custom_call_target="tpu_custom_call" | custom-call | bytes 33210000 | tf_op jit(solution)/shard_map/gated_norm_forward/pallas_call | solution.py:321
  114.5 7.1 %multiply_reduce_fusion = (f32[1024]{0:T(1024)S(1)}, f32[768,1024]{1,0:T(8,128)S(1)}, f32[1024,768]{0,1:T(8,128)}) fusion(bf16[1,1024,768]{1,2,0:T(8,128)(2,1)S(1)} %copy.106, bf16[1536,1024]{1,0:T(8,128)(2,1)} %get-tuple-element.63, bf16[1,1536,768]{2,1,0:T(8,128)(2,1)} %all-gather.19.cloned.1.call-done), kind=kOutput, calls=%fused_computation.20 | convolution fusion | flops 2419063808 | bytes 13373440 | tf_op jit(solution)/shard_map/dot_general | solution.py:26
  123.6 28.2 %all-gather.15.cloned.1.call-done.w_ref = bf16[768,1824]{1,0:T(8,128)(2,1)} async-done(((bf16[96,1824]{1,0:T(8,128)(2,1)}), bf16[768,1824]{1,0:T(8,128)(2,1)}) %all-gather.15.cloned.1.call-update) | async-done | bytes 2801680 | tf_op jit(solution)/shard_map/all_gather | solution.py:968
  164.4 20.1 %scan_forward.3 = (bf16[1792,1024]{1,0:T(8,128)(2,1)}, bf16[1792,1024]{1,0:T(8,128)(2,1)}, bf16[1536,1024]{1,0:T(8,128)(2,1)}, bf16[8,1536,128]{2,1,0:T(8,128)(2...) custom-call(bf16[1824,1024]{1,0:T(8,128)(2,1)} %convolution_convert_fusion.1.qd_ref.refs_7_, ...), custom_call_target="tpu_custom_call" | custom-call | bytes 73800000 | tf_op jit(solution)/shard_map/scan_forward/pallas_call | solution.py:223
  199.0 7.8 %collective-permute-done.6.refs_1_ = bf16[1600,128]{1,0:T(8,128)(2,1)} collective-permute-done((bf16[1600,128]{1,0:T(8,128)(2,1)}, bf16[1600,128]{1,0:T(8,128)(2,1)}, u32[]{:S(2)}, u32[]{:S(2)}) %collective-permute-start.6) | collective-permute-done | bytes 409632 | tf_op jit(solution)/shard_map/ppermute | solution.py:842
  207.4 8.9 %gated_norm_forward.3 = (bf16[1536,1024]{1,0:T(8,128)(2,1)}, bf16[1536,1024]{1,0:T(8,128)(2,1)}, bf16[1536,128]{1,0:T(8,128)(2,1)}) custom-call(bf16[1600,128]{1,0:T(8,128)(2,1)} %collective-permute-done.5.refs_0_, bf16[1600,128]{1,0:T(8,128)(2,1)} %collective-permute-done.6.refs_1_, bf16[1600,128]{1,0:T(8,128)(2,1)} %collective-permute-done.7.refs_2_, ...), custom_call_target="tpu_custom_call" | custom-call | bytes 33210000 | tf_op jit(solution)/shard_map/gated_norm_forward/pallas_call | solution.py:321
  216.4 17.5 %gated_norm_backward.2 = (bf16[1536,1024]{1,0:T(8,128)(2,1)}, bf16[1536,1024]{1,0:T(8,128)(2,1)}, f32[8,1536]{1,0:T(8,128)}, bf16[1600,128]{1,0:T(8,128)(2,1)}) custom-call(bf16[768,1024]{1,0:T(8,128)(2,1)} %bitcast.201, bf16[1536,768]{1,0:T(8,128)(2,1)} %bitcast.207, bf16[1536,1024]{1,0:T(8,128)(2,1)} %get-tuple-element.69.refs_2_, ...), custom_call_target="tpu_custom_call" | custom-call | bytes 62730000 | tf_op jit(solution)/shard_map/gated_norm_backward/pallas_call | solution.py:430
  250.5 7.2 %fusion.13.refs_4_.part_ref = f32[768,1024]{1,0:T(8,128)} fusion(bf16[1536,1024]{1,0:T(8,128)(2,1)} %get-tuple-element.71, bf16[1,768,1536]{2,1,0:T(8,128)(2,1)} %all-gather.21.cloned.1.call-done), kind=kOutput, calls=%fused_computation.33 | convolution fusion | flops 2415919104 | bytes 8650752 | tf_op jit(solution)/shard_map/dot_general | solution.py:26
  259.9 10.9 %collective-permute-done.9.refs_1_ = bf16[1600,128]{1,0:T(8,128)(2,1)S(1)} collective-permute-done((bf16[1600,128]{1,0:T(8,128)(2,1)}, bf16[1600,128]{1,0:T(8,128)(2,1)S(1)}, u32[]{:S(2)}, u32[]{:S(2)}) %collective-permute-start.9) | collective-permute-done | bytes 409632 | tf_op jit(solution)/shard_map/ppermute | solution.py:842
  271.7 33.7 %scan_backward.2 = (bf16[1824,1024]{1,0:T(8,128)(2,1)}, f32[8,1792]{1,0:T(8,128)}, f32[32,8]{1,0:T(8,128)}, f32[8,1792]{1,0:T(8,128)}) custom-call(bf16[1600,128]{1,0:T(8,128)(2,1)} %copy-done.17, bf16[1600,128]{1,0:T(8,128)(2,1)} %copy-done.19, bf16[1600,128]{1,0:T(8,128)(2,1)} %copy-done.20, bf16[8,384,768]{2,1,0:T(8,128)(2,1)} %pad_maximum_fusion.refs_3_, ...), custom_call_target="tpu_custom_call" | custom-call | bytes 121770000 | tf_op jit(solution)/shard_map/scan_backward/pallas_call | solution.py:661
  314.6 6.9 %convolution_convert_fusion.7.refs_0_ = bf16[768,1824]{1,0:T(8,128)(2,1)} fusion(bf16[768,1024]{1,0:T(8,128)(2,1)S(1)} %multiply_convert_fusion, bf16[1824,1024]{1,0:T(8,128)(2,1)} %edge_gradient.2.dqd_ref), kind=kOutput, calls=%fused_computation.11 | convolution fusion | flops 2870304768 | bytes 8110080 | tf_op jit(solution)/shard_map/dot_general | solution.py:26
  325.6 11.1 %input_backward.2 = (f32[768,1024]{1,0:T(8,128)}, bf16[768,1024]{1,0:T(8,128)(2,1)}, f32[8,768]{1,0:T(8,128)}) custom-call(bf16[768,1824]{1,0:T(8,128)(2,1)} %all-gather.15.cloned.1.call-done.w_ref, bf16[1824,1024]{1,0:T(8,128)(2,1)} %edge_gradient.2.dqd_ref, f32[768,1024]{1,0:T(8,128)} %fusion.13.refs_4_.part_ref, f32[768,1024]{1,0:T(8,128)} %copy-done.1, ...), custom_call_target="tpu_custom_call" | custom-call | tf_op jit(solution)/shard_map/input_backward/pallas_call | solution.py:777
  336.7 17.6 %gated_norm_backward.3 = (bf16[1536,1024]{1,0:T(8,128)(2,1)}, bf16[1536,1024]{1,0:T(8,128)(2,1)}, f32[8,1536]{1,0:T(8,128)}, bf16[1600,128]{1,0:T(8,128)(2,1)}) custom-call(bf16[768,1824]{1,0:T(8,128)(2,1)} %convolution_convert_fusion.7.refs_0_, bf16[768,1024]{1,0:T(8,128)(2,1)} %get-tuple-element.81.refs_1_, bf16[1536,768]{1,0:T(8,128)(2,1)} %bitcast.208, ...), custom_call_target="tpu_custom_call" | custom-call | bytes 62730000 | tf_op jit(solution)/shard_map/gated_norm_backward/pallas_call | solution.py:430
  385.2 7.0 %fusion.10.refs_4_.part_ref = f32[768,1024]{1,0:T(8,128)} fusion(bf16[1536,1024]{1,0:T(8,128)(2,1)} %get-tuple-element.84, bf16[1,768,1536]{2,1,0:T(8,128)(2,1)} %all-gather.17.cloned.1.call-done), kind=kOutput, calls=%fused_computation.32 | convolution fusion | flops 2415919104 | bytes 8650752 | tf_op jit(solution)/shard_map/dot_general | solution.py:26
  392.2 10.0 %collective-permute-done.13.refs_1_ = bf16[1600,128]{1,0:T(8,128)(2,1)S(1)} collective-permute-done((bf16[1600,128]{1,0:T(8,128)(2,1)S(1)}, bf16[1600,128]{1,0:T(8,128)(2,1)S(1)}, u32[]{:S(2)}, u32[]{:S(2)}) %collective-permute-start.13) | collective-permute-done | bytes 409632 | tf_op jit(solution)/shard_map/ppermute | solution.py:842
  403.1 33.6 %scan_backward.3 = (bf16[1824,1024]{1,0:T(8,128)(2,1)}, f32[8,1792]{1,0:T(8,128)}, f32[32,8]{1,0:T(8,128)}, f32[8,1792]{1,0:T(8,128)}) custom-call(bf16[1600,128]{1,0:T(8,128)(2,1)} %copy-done.15, bf16[1600,128]{1,0:T(8,128)(2,1)} %copy-done.16, bf16[1600,128]{1,0:T(8,128)(2,1)} %copy-done.18, bf16[8,384,768]{2,1,0:T(8,128)(2,1)} %pad_maximum_fusion.1.refs_3_, ...), custom_call_target="tpu_custom_call" | custom-call | bytes 121770000 | tf_op jit(solution)/shard_map/scan_backward/pallas_call | solution.py:661
  446.8 6.8 %convolution_convert_fusion.4 = bf16[768,1824]{1,0:T(8,128)(2,1)} fusion(bf16[768,1024]{1,0:T(8,128)(2,1)S(1)} %copy-done.7, bf16[1824,1024]{1,0:T(8,128)(2,1)} %edge_gradient.3.dqd_ref), kind=kOutput, calls=%fused_computation.8 | convolution fusion | flops 2870304768 | bytes 8110080 | tf_op jit(solution)/shard_map/dot_general | solution.py:26
  457.8 11.2 %input_backward.3 = (f32[1024,768]{1,0:T(8,128)}, f32[8,768]{1,0:T(8,128)}) custom-call(bf16[768,1824]{1,0:T(8,128)(2,1)} %all-gather.13.cloned.1.call-done.w_ref, bf16[1824,1024]{1,0:T(8,128)(2,1)} %edge_gradient.3.dqd_ref, f32[768,1024]{1,0:T(8,128)} %fusion.10.refs_4_.part_ref, f32[768,1024]{1,0:T(8,128)} %convert_bitcast_fusion.h_ref, ...), custom_call_target="tpu_custom_call" | custom-call | tf_op jit(solution)/shard_map/input_backward/pallas_call | solution.py:777
  482.6 10.0 %collective-permute-done.18 = f32[22672]{0:T(1024)S(1)} collective-permute-done((f32[22672]{0:T(1024)S(1)}, f32[22672]{0:T(1024)S(1)}, u32[]{:S(2)}, u32[]{:S(2)}) %collective-permute-start.18) | collective-permute-done | bytes 90720 | tf_op jit(solution)/shard_map/ppermute | solution.py:884
  516.4 9.1 %collective-permute-done.29 = bf16[96,1824]{1,0:T(8,128)(2,1)S(1)} collective-permute-done((bf16[96,1824]{1,0:T(8,128)(2,1)}, bf16[96,1824]{1,0:T(8,128)(2,1)S(1)}, u32[]{:S(2)}, u32[]{:S(2)}) %collective-permute-start.29) | collective-permute-done | bytes 350240 | tf_op jit(solution)/shard_map/ppermute | solution.py:850
  (336 shorter events, 198.5 us)
Async XLA Ops:
  7.2 42.7 %all-gather.13.cloned.1.call-start = ((), (), s32[]{:S(2)}) async-start(), calls=%async_computation.4 | async-start | bytes 3317760 | tf_op jit(solution)/shard_map/all_gather | solution.py:968
  10.2 81.0 %all-gather.17.cloned.1.call-start = ((), (), s32[]{:S(2)}) async-start(), calls=%async_computation.10 | async-start | bytes 2654208 | tf_op jit(solution)/shard_map/all_gather | solution.py:969
  12.3 102.2 %all-gather.19.cloned.1.call-start = ((), (), s32[]{:S(2)}) async-start(), calls=%async_computation.11 | async-start | bytes 2654208 | tf_op jit(solution)/shard_map/all_gather | solution.py:970
  13.2 138.6 %all-gather.15.cloned.1.call-start = ((), (), s32[]{:S(2)}) async-start(), calls=%async_computation.5 | async-start | bytes 3317760 | tf_op jit(solution)/shard_map/all_gather | solution.py:968
  14.3 179.0 %all-gather.21.cloned.1.call-start = ((), (), s32[]{:S(2)}) async-start(), calls=%async_computation.12 | async-start | bytes 2654208 | tf_op jit(solution)/shard_map/all_gather | solution.py:969
  14.9 201.5 %all-gather.23.cloned.1.call-start = ((), (), s32[]{:S(2)}) async-start(), calls=%async_computation.13 | async-start | bytes 2654208 | tf_op jit(solution)/shard_map/all_gather | solution.py:970
  15.4 306.1 %reduce-scatter.5.cloned.1.call-start = ((), (), s32[]{:S(2)}) async-start(), calls=%async_computation.6 | async-start | bytes 5308416 | tf_op jit(solution)/shard_map/reduce_scatter | solution.py:1022
  86.8 18.1 %collective-permute-start.2 = (bf16[1600,128]{1,0:T(8,128)(2,1)}, bf16[1600,128]{1,0:T(8,128)(2,1)}, u32[]{:S(2)}, u32[]{:S(2)}) collective-permute-start(bf16[1600,128]{1,0:T(8,128)(2,1)} %get-tuple-element.59.refs_8_), channel_id=1, source_target_pairs={{0,16},{8,24},{1,17},{9,25},{2,18},{10,26},{3,19},{11,27},{4,20},{... | collective-permute-start | bytes 1228808 | tf_op jit(solution)/shard_map/ppermute | solution.py:842
  88.8 16.0 %collective-permute-start.3 = (bf16[1600,128]{1,0:T(8,128)(2,1)}, bf16[1600,128]{1,0:T(8,128)(2,1)}, u32[]{:S(2)}, u32[]{:S(2)}) collective-permute-start(bf16[1600,128]{1,0:T(8,128)(2,1)} %get-tuple-element.59.refs_8_), channel_id=1, source_target_pairs={{0,24},{1,25},{2,26},{3,27},{4,28},{5,29},{6,30},{7,31}} | collective-permute-start | bytes 1228808 | tf_op jit(solution)/shard_map/ppermute | solution.py:842
  188.7 18.1 %collective-permute-start.6 = (bf16[1600,128]{1,0:T(8,128)(2,1)}, bf16[1600,128]{1,0:T(8,128)(2,1)}, u32[]{:S(2)}, u32[]{:S(2)}) collective-permute-start(bf16[1600,128]{1,0:T(8,128)(2,1)} %get-tuple-element.64.refs_7_), channel_id=1, source_target_pairs={{0,16},{8,24},{1,17},{9,25},{2,18},{10,26},{3,19},{11,27},{4,20},{... | collective-permute-start | bytes 1228808 | tf_op jit(solution)/shard_map/ppermute | solution.py:842
  190.8 16.0 %collective-permute-start.7 = (bf16[1600,128]{1,0:T(8,128)(2,1)}, bf16[1600,128]{1,0:T(8,128)(2,1)}, u32[]{:S(2)}, u32[]{:S(2)}) collective-permute-start(bf16[1600,128]{1,0:T(8,128)(2,1)} %get-tuple-element.64.refs_7_), channel_id=1, source_target_pairs={{0,24},{1,25},{2,26},{3,27},{4,28},{5,29},{6,30},{7,31}} | collective-permute-start | bytes 1228808 | tf_op jit(solution)/shard_map/ppermute | solution.py:842
  246.2 207.5 %reduce-scatter.11.cloned.1.call-start = ((), (), s32[]{:S(2)}) async-start(), calls=%async_computation.9 | async-start | bytes 3317760 | tf_op jit(solution)/shard_map/reduce_scatter | solution.py:1033
  247.7 23.1 %collective-permute-start.9 = (bf16[1600,128]{1,0:T(8,128)(2,1)}, bf16[1600,128]{1,0:T(8,128)(2,1)S(1)}, u32[]{:S(2)}, u32[]{:S(2)}) collective-permute-start(bf16[1600,128]{1,0:T(8,128)(2,1)} %get-tuple-element.70), channel_id=1, source_target_pairs={{16,0},{24,8},{17,1},{25,9},{18,2},{26,10},{19,3},{27,11},{20,4},{... | collective-permute-start | bytes 1228808 | tf_op jit(solution)/shard_map/ppermute | solution.py:842
  249.0 21.8 %collective-permute-start.10 = (bf16[1600,128]{1,0:T(8,128)(2,1)}, bf16[1600,128]{1,0:T(8,128)(2,1)S(1)}, u32[]{:S(2)}, u32[]{:S(2)}) collective-permute-start(bf16[1600,128]{1,0:T(8,128)(2,1)} %get-tuple-element.70), channel_id=1, source_target_pairs={{24,0},{25,1},{26,2},{27,3},{28,4},{29,5},{30,6},{31,7}} | collective-permute-start | bytes 1228808 | tf_op jit(solution)/shard_map/ppermute | solution.py:842
  321.6 135.6 %reduce-scatter.7.cloned.1.call-start = ((), (), s32[]{:S(2)}) async-start(), calls=%async_computation.7 | async-start | bytes 5308416 | tf_op jit(solution)/shard_map/reduce_scatter | solution.py:1022
  366.8 145.9 %reduce-scatter.9.cloned.1.call-start = ((), (), s32[]{:S(2)}) async-start(), calls=%async_computation.8 | async-start | bytes 3317760 | tf_op jit(solution)/shard_map/reduce_scatter | solution.py:1033
  380.7 21.4 %collective-permute-start.13 = (bf16[1600,128]{1,0:T(8,128)(2,1)S(1)}, bf16[1600,128]{1,0:T(8,128)(2,1)S(1)}, u32[]{:S(2)}, u32[]{:S(2)}) collective-permute-start(bf16[1600,128]{1,0:T(8,128)(2,1)S(1)} %copy-done.37), channel_id=1, source_target_pairs={{16,0},{24,8},{17,1},{25,9},{18,2},{26,10},{19,3},{27,11},{20,4},{... | collective-permute-start | bytes 1228808 | tf_op jit(solution)/shard_map/ppermute | solution.py:842
  382.0 20.1 %collective-permute-start.14 = (bf16[1600,128]{1,0:T(8,128)(2,1)S(1)}, bf16[1600,128]{1,0:T(8,128)(2,1)S(1)}, u32[]{:S(2)}, u32[]{:S(2)}) collective-permute-start(bf16[1600,128]{1,0:T(8,128)(2,1)S(1)} %copy-done.37), channel_id=1, source_target_pairs={{24,0},{25,1},{26,2},{27,3},{28,4},{29,5},{30,6},{31,7}} | collective-permute-start | bytes 1228808 | tf_op jit(solution)/shard_map/ppermute | solution.py:842
  453.7 20.8 %collective-permute-start.32 = (bf16[96,1824]{1,0:T(8,128)(2,1)}, bf16[96,1824]{1,0:T(8,128)(2,1)S(1)}, u32[]{:S(2)}, u32[]{:S(2)}) collective-permute-start(bf16[96,1824]{1,0:T(8,128)(2,1)} %reduce-scatter.11.cloned.1.call-done), channel_id=1, source_target_pairs={{0,24},{8,16},{16,8},{24,0},{1,25},{9,17},{17,9},{25,1},{2,26},{10... | collective-permute-start | bytes 1050632 | tf_op jit(solution)/shard_map/ppermute | solution.py:850
  453.7 21.8 %collective-permute-start.31 = (bf16[96,1824]{1,0:T(8,128)(2,1)}, bf16[96,1824]{1,0:T(8,128)(2,1)}, u32[]{:S(2)}, u32[]{:S(2)}) collective-permute-start(bf16[96,1824]{1,0:T(8,128)(2,1)} %reduce-scatter.11.cloned.1.call-done), channel_id=1, source_target_pairs={{0,16},{8,24},{16,0},{24,8},{1,17},{9,25},{17,1},{25,9},{2,18},{10... | collective-permute-start | bytes 1050632 | tf_op jit(solution)/shard_map/ppermute | solution.py:850
  456.2 20.3 %collective-permute-start.30 = (bf16[96,1824]{1,0:T(8,128)(2,1)}, bf16[96,1824]{1,0:T(8,128)(2,1)}, u32[]{:S(2)}, u32[]{:S(2)}) collective-permute-start(bf16[96,1824]{1,0:T(8,128)(2,1)} %reduce-scatter.11.cloned.1.call-done), channel_id=1, source_target_pairs={{0,8},{8,0},{16,24},{24,16},{1,9},{9,1},{17,25},{25,17},{2,10},{10... | collective-permute-start | bytes 1050632 | tf_op jit(solution)/shard_map/ppermute | solution.py:850
  470.9 21.8 %collective-permute-start.23 = (bf16[192,768]{1,0:T(8,128)(2,1)}, bf16[192,768]{1,0:T(8,128)(2,1)}, u32[]{:S(2)}, u32[]{:S(2)}) collective-permute-start(bf16[192,768]{1,0:T(8,128)(2,1)} %get-tuple-element.208), channel_id=1, source_target_pairs={{0,24},{8,16},{16,8},{24,0},{1,25},{9,17},{17,9},{25,1},{2,26},{10... | collective-permute-start | bytes 884744 | tf_op jit(solution)/shard_map/ppermute | solution.py:866
  471.5 21.3 %collective-permute-start.22 = (bf16[192,768]{1,0:T(8,128)(2,1)}, bf16[192,768]{1,0:T(8,128)(2,1)}, u32[]{:S(2)}, u32[]{:S(2)}) collective-permute-start(bf16[192,768]{1,0:T(8,128)(2,1)} %get-tuple-element.209), channel_id=1, source_target_pairs={{0,16},{8,24},{16,0},{24,8},{1,17},{9,25},{17,1},{25,9},{2,18},{10... | collective-permute-start | bytes 884744 | tf_op jit(solution)/shard_map/ppermute | solution.py:866
  474.5 18.3 %collective-permute-start.21 = (bf16[192,768]{1,0:T(8,128)(2,1)S(1)}, bf16[192,768]{1,0:T(8,128)(2,1)}, u32[]{:S(2)}, u32[]{:S(2)}) collective-permute-start(bf16[192,768]{1,0:T(8,128)(2,1)S(1)} %get-tuple-element.207), channel_id=1, source_target_pairs={{0,8},{8,0},{16,24},{24,16},{1,9},{9,1},{17,25},{25,17},{2,10},{10... | collective-permute-start | bytes 884744 | tf_op jit(solution)/shard_map/ppermute | solution.py:866
  (58 other events, 530.5 us)
Sparse Core Ops, SparseCore 0:
  10.2 39.5 all-gather.12
  51.5 30.5 all-gather.16
  83.7 30.7 all-gather.18
  116.0 35.7 all-gather.14
  153.3 30.4 all-gather.20
  185.3 30.7 all-gather.22
  246.3 55.2 reduce-scatter.4
  321.7 36.7 reduce-scatter.10
  366.9 53.0 reduce-scatter.6
  471.6 40.6 reduce-scatter.8

commit v4 on v3

--- a/solution.py
+++ b/solution.py
@@ -735,17 +735,17 @@
     crosses = jnp.zeros((CHUNK, lanes), F32)
     for at in range(0, depth, CHUNK):
         rows = pl.ds(at, CHUNK)
-        h = h_ref[rows, :]
+        h = h_ref[rows, :].astype(F32)
         squares = squares + h * h
         crosses = crosses + d_norm[rows, :] * gain[rows, :] * h
     inverse = lax.rsqrt(col_sum(squares) * (1.0 / depth) + EPS)
     along = col_sum(crosses) * (1.0 / depth) * inverse * inverse * inverse
     for at in range(0, depth, CHUNK):
         rows = pl.ds(at, CHUNK)
-        h = h_ref[rows, :]
+        h = h_ref[rows, :].astype(F32)
         scaled = d_norm[rows, :] * inverse
         dgain[rows, :] += scaled * h
-        grad = grad_ref[rows, :] + scaled * gain[rows, :] - h * along
+        grad = grad_ref[rows, :].astype(F32) + scaled * gain[rows, :] - h * along
         if token_major:
             for lane in range(0, lanes, CHUNK):
                 out_ref[lane : lane + CHUNK, at : at + CHUNK] = jnp.transpose(
@@ -971,7 +971,8 @@
             )
         )
 
-    hidden = tokens[0].T.astype(F32)
+    first = tokens[0].T
+    hidden = first.astype(F32)
     saved = []
     for layer in range(layers):
         w_scan, w_gate, w_out = weights[layer]
@@ -994,8 +995,7 @@
         hidden = hidden + dot(w_out, gated, 0, 0)
     activations = hidden.astype(BF).T[None]
 
-    go = cotangent[0].T
-    grad = go.astype(F32)
+    go = grad = cotangent[0].T
     results = [None] * layers
     before_norm = []
     for layer in reversed(range(layers)):
@@ -1008,7 +1008,11 @@
         dy, dz, d_gain_out, back_pack = gated_norm_back(
             go, w_out, yb, z, xa, reach, gain_out, pack, heads, before_norm
         )
-        back_packs = [passed_along(back_pack, "seq", -k) for k in range(1, n_seq)]
+        back_packs = []
+        for k in reversed(range(1, n_seq)):
+            if back_packs and layer == 0:
+                back_pack, back_packs[0] = lax.optimization_barrier((back_pack, back_packs[0]))
+            back_packs.insert(0, passed_along(back_pack, "seq", -k))
         d_w_out = dot(gated, go, 1, 1).astype(BF)
         d_w_gate = dot(normed, dz, 1, 1).astype(BF)
         joint = jnp.concatenate(
@@ -1032,7 +1036,7 @@
         dqd, d_w_scan, share_joint = lax.optimization_barrier((dqd, d_w_scan, share_joint))
         share_scan = lax.psum_scatter(d_w_scan, "shard", scatter_dimension=0, tiled=True)
         grad, *low, d_gain_in = input_back(
-            w_scan, dqd, d_normed, h_in, gain_in, grad, layer == 0
+            w_scan, dqd, d_normed, h_in if layer else first, gain_in, grad, layer == 0
         )
         if low:
             go = low[0]

time: 549 us -> 549 us (level)
    unnamed x81 -> x117, local copies, waits for them, and re-layouts: 14.7 us -> 13.3 us
where the time goes in v4:
time: 549 us; the launch traced here: 540 us
  Pallas kernels  187 us (34%)
  waiting for transfers between devices  111 us (20%)
  matrix products  86.7 us (16%)
  starting transfers between devices  55.3 us (10%)
  local copies, waits for them, and re-layouts  38.3 us (7%)
  blocking collectives  24 us (4%)
  other arithmetic  22.7 us (4%)
  between operations  15.8 us (3%)
    dot_general x16, matrix products, dot(): lax.dot_general(left, right, (((left_dim,), (right_dim,)), ((), ())), pre...  86.7 us
    pallas_call x2, Pallas kernels, scan_back(): pl.pallas_call(functools.partial(scan_back_kernel, heads, len(packs), len...  67.3 us
    ppermute x16, waiting for transfers between devices, passed_along(): return lax.ppermute(block, axis, route)  45.6 us
    pallas_call x2, Pallas kernels, scan(): pl.pallas_call(functools.partial(scan_kernel, heads, inner), grid=(steps,...  40.2 us
    pallas_call x2, Pallas kernels, gated_norm_back(): pl.pallas_call(functools.partial(norm_back_kernel, heads, len(after)), gr...  35.2 us
    ppermute x16, starting transfers between devices, passed_along(): return lax.ppermute(block, axis, route)  34.8 us
    all_gather x2, waiting for transfers between devices, body(): lax.all_gather(scan_part, 'shard', axis=0, tiled=True)  29.3 us
    pallas_call x2, Pallas kernels, input_back(): pl.pallas_call(functools.partial(input_back_kernel, token_major), grid=(l...  21.9 us
  transfers between devices with their start and end apart: 43, of which 18 were waited for; matrix products, arithmetic and copies ran while one was open for 23% of the time, Pallas kernels for 31%

profile of v4, /device:TPU:0, one launch (start us, length us, event | category | flops | bytes accessed | tf_op | source)
XLA Modules:
  0.0 540.5 jit_solution(2299938063453012805)
XLA Ops:
  15.7 15.9 %all-gather.5 = bf16[8,2,1408]{2,1,0:T(2,128)(2,1)S(1)} all-gather(bf16[1,2,1408]{2,1,0:T(2,128)(2,1)S(1)} %bitcast.208), channel_id=2, replica_groups=mesh['seq'=4,'shard'=8] {'shard'}, dimensions={0}, use_global_device_ids=true | all-gather | bytes 50688 | tf_op jit(solution)/shard_map/all_gather | solution.py:937
  35.1 8.1 %all_gather.30 = f32[3,2,24]{0,1,2:T(2,128)S(1)} all-gather(f32[3,2,6]{0,1,2:T(2,128)S(1)} %copy.110), channel_id=1, replica_groups=mesh['seq'=4,'shard'=8] {'seq'}, dimensions={2}, use_global_device_ids=true | all-gather | bytes 720 | tf_op jit(solution)/shard_map/all_gather | solution.py:952
  62.6 20.1 %scan_forward.2 = (bf16[1792,1024]{1,0:T(8,128)(2,1)}, bf16[1792,1024]{1,0:T(8,128)(2,1)}, bf16[1536,1024]{1,0:T(8,128)(2,1)}, bf16[8,1536,128]{2,1,0:T(8,128)(2...) custom-call(bf16[1824,1024]{1,0:T(8,128)(2,1)} %convolution_convert_fusion.3.qd_ref.refs_7_, ...), custom_call_target="tpu_custom_call" | custom-call | bytes 73800000 | tf_op jit(solution)/shard_map/scan_forward/pallas_call | solution.py:223
  97.0 7.9 %collective-permute-done.2.refs_1_ = bf16[1600,128]{1,0:T(8,128)(2,1)} collective-permute-done((bf16[1600,128]{1,0:T(8,128)(2,1)}, bf16[1600,128]{1,0:T(8,128)(2,1)}, u32[]{:S(2)}, u32[]{:S(2)}) %collective-permute-start.2) | collective-permute-done | bytes 409632 | tf_op jit(solution)/shard_map/ppermute | solution.py:842
  105.5 8.9 %gated_norm_forward.2 = (bf16[1536,1024]{1,0:T(8,128)(2,1)}, bf16[1536,1024]{1,0:T(8,128)(2,1)}, bf16[1536,128]{1,0:T(8,128)(2,1)}) custom-call(bf16[1600,128]{1,0:T(8,128)(2,1)} %collective-permute-done.1.refs_0_, bf16[1600,128]{1,0:T(8,128)(2,1)} %collective-permute-done.2.refs_1_, bf16[1600,128]{1,0:T(8,128)(2,1)} %collective-permute-done.3.refs_2_, ...), custom_call_target="tpu_custom_call" | custom-call | bytes 33210000 | tf_op jit(solution)/shard_map/gated_norm_forward/pallas_call | solution.py:321
  115.1 7.1 %multiply_reduce_fusion = (f32[1024]{0:T(1024)S(1)}, f32[768,1024]{1,0:T(8,128)S(1)}, f32[1024,768]{0,1:T(8,128)}) fusion(bf16[1,1024,768]{1,2,0:T(8,128)(2,1)S(1)} %copy.106, bf16[1536,1024]{1,0:T(8,128)(2,1)} %get-tuple-element.67, bf16[1,1536,768]{2,1,0:T(8,128)(2,1)} %all-gather.19.cloned.1.call-done), kind=kOutput, calls=%fused_computation.22 | convolution fusion | flops 2419063808 | bytes 13373440 | tf_op jit(solution)/shard_map/dot_general | solution.py:26
  125.4 27.0 %all-gather.15.cloned.1.call-done.w_ref = bf16[768,1824]{1,0:T(8,128)(2,1)} async-done(((bf16[96,1824]{1,0:T(8,128)(2,1)}), bf16[768,1824]{1,0:T(8,128)(2,1)}) %all-gather.15.cloned.1.call-update) | async-done | bytes 2801680 | tf_op jit(solution)/shard_map/all_gather | solution.py:968
  166.9 20.1 %scan_forward.3 = (bf16[1792,1024]{1,0:T(8,128)(2,1)}, bf16[1792,1024]{1,0:T(8,128)(2,1)}, bf16[1536,1024]{1,0:T(8,128)(2,1)}, bf16[8,1536,128]{2,1,0:T(8,128)(2...) custom-call(bf16[1824,1024]{1,0:T(8,128)(2,1)} %convolution_convert_fusion.1.qd_ref.refs_7_, ...), custom_call_target="tpu_custom_call" | custom-call | bytes 73800000 | tf_op jit(solution)/shard_map/scan_forward/pallas_call | solution.py:223
  201.9 7.3 %collective-permute-done.6.refs_1_ = bf16[1600,128]{1,0:T(8,128)(2,1)} collective-permute-done((bf16[1600,128]{1,0:T(8,128)(2,1)}, bf16[1600,128]{1,0:T(8,128)(2,1)}, u32[]{:S(2)}, u32[]{:S(2)}) %collective-permute-start.6) | collective-permute-done | bytes 409632 | tf_op jit(solution)/shard_map/ppermute | solution.py:842
  209.8 8.8 %gated_norm_forward.3 = (bf16[1536,1024]{1,0:T(8,128)(2,1)}, bf16[1536,1024]{1,0:T(8,128)(2,1)}, bf16[1536,128]{1,0:T(8,128)(2,1)}) custom-call(bf16[1600,128]{1,0:T(8,128)(2,1)} %collective-permute-done.5.refs_0_, bf16[1600,128]{1,0:T(8,128)(2,1)} %collective-permute-done.6.refs_1_, bf16[1600,128]{1,0:T(8,128)(2,1)} %collective-permute-done.7.refs_2_, ...), custom_call_target="tpu_custom_call" | custom-call | bytes 33210000 | tf_op jit(solution)/shard_map/gated_norm_forward/pallas_call | solution.py:321
  218.7 17.6 %gated_norm_backward.2 = (bf16[1536,1024]{1,0:T(8,128)(2,1)}, bf16[1536,1024]{1,0:T(8,128)(2,1)}, f32[8,1536]{1,0:T(8,128)}, bf16[1600,128]{1,0:T(8,128)(2,1)}) custom-call(bf16[768,1024]{1,0:T(8,128)(2,1)} %bitcast.192, bf16[1536,768]{1,0:T(8,128)(2,1)} %bitcast.199, bf16[1536,1024]{1,0:T(8,128)(2,1)} %get-tuple-element.73.refs_2_, ...), custom_call_target="tpu_custom_call" | custom-call | bytes 62730000 | tf_op jit(solution)/shard_map/gated_norm_backward/pallas_call | solution.py:430
  253.1 7.2 %fusion.14.refs_4_.part_ref = f32[768,1024]{1,0:T(8,128)} fusion(bf16[1536,1024]{1,0:T(8,128)(2,1)} %get-tuple-element.75, bf16[1,768,1536]{2,1,0:T(8,128)(2,1)} %all-gather.21.cloned.1.call-done), kind=kOutput, calls=%fused_computation.33 | convolution fusion | flops 2415919104 | bytes 8650752 | tf_op jit(solution)/shard_map/dot_general | solution.py:26
  262.3 10.8 %collective-permute-done.9.refs_1_ = bf16[1600,128]{1,0:T(8,128)(2,1)S(1)} collective-permute-done((bf16[1600,128]{1,0:T(8,128)(2,1)}, bf16[1600,128]{1,0:T(8,128)(2,1)S(1)}, u32[]{:S(2)}, u32[]{:S(2)}) %collective-permute-start.9) | collective-permute-done | bytes 409632 | tf_op jit(solution)/shard_map/ppermute | solution.py:842
  274.0 33.7 %scan_backward.2 = (bf16[1824,1024]{1,0:T(8,128)(2,1)}, f32[8,1792]{1,0:T(8,128)}, f32[32,8]{1,0:T(8,128)}, f32[8,1792]{1,0:T(8,128)}) custom-call(bf16[1600,128]{1,0:T(8,128)(2,1)} %copy-done.16, bf16[1600,128]{1,0:T(8,128)(2,1)} %copy-done.17, bf16[1600,128]{1,0:T(8,128)(2,1)} %copy-done.18, bf16[8,384,768]{2,1,0:T(8,128)(2,1)} %pad_maximum_fusion.refs_3_, ...), custom_call_target="tpu_custom_call" | custom-call | bytes 121770000 | tf_op jit(solution)/shard_map/scan_backward/pallas_call | solution.py:661
  324.8 10.8 %input_backward.2 = (f32[768,1024]{1,0:T(8,128)}, bf16[768,1024]{1,0:T(8,128)(2,1)}, f32[8,768]{1,0:T(8,128)}) custom-call(bf16[768,1824]{1,0:T(8,128)(2,1)} %all-gather.15.cloned.1.call-done.w_ref, bf16[1824,1024]{1,0:T(8,128)(2,1)} %edge_gradient.2.dqd_ref, f32[768,1024]{1,0:T(8,128)} %fusion.14.refs_4_.part_ref, f32[768,1024]{1,0:T(8,128)} %copy-done.1, ...), custom_call_target="tpu_custom_call" | custom-call | tf_op jit(solution)/shard_map/input_backward/pallas_call | solution.py:777
  335.6 17.6 %gated_norm_backward.3 = (bf16[1536,1024]{1,0:T(8,128)(2,1)}, bf16[1536,1024]{1,0:T(8,128)(2,1)}, f32[8,1536]{1,0:T(8,128)}, bf16[1600,128]{1,0:T(8,128)(2,1)}) custom-call(bf16[768,1824]{1,0:T(8,128)(2,1)} %convolution_convert_fusion.7.refs_0_, bf16[768,1024]{1,0:T(8,128)(2,1)} %get-tuple-element.85.refs_1_, bf16[1536,768]{1,0:T(8,128)(2,1)} %bitcast.200, ...), custom_call_target="tpu_custom_call" | custom-call | bytes 62730000 | tf_op jit(solution)/shard_map/gated_norm_backward/pallas_call | solution.py:430
  367.1 7.9 %fusion.17 = bf16[1,1024,768]{1,2,0:T(8,128)(2,1)} fusion(f32[1024,768]{0,1:T(8,128)} %get-tuple-element.250, bf16[1,1024,768]{1,2,0:T(8,128)(2,1)S(1)} %copy.106, bf16[1536,1024]{1,0:T(8,128)(2,1)} %get-tuple-element.72, bf16[1,1536,768]{2,1,0:T(8,128)(2,1)} %all-gather.23.cloned.1.call-done), kind=kOutput, calls=%fused_computation.34 | convolution fusion | flops 2419064832 | bytes 11796480 | tf_op jit(solution)/shard_map/dot_general | solution.py:26
  381.5 7.6 %collective-permute-done.13.refs_1_ = bf16[1600,128]{1,0:T(8,128)(2,1)S(1)} collective-permute-done((bf16[1600,128]{1,0:T(8,128)(2,1)S(1)}, bf16[1600,128]{1,0:T(8,128)(2,1)S(1)}, u32[]{:S(2)}, u32[]{:S(2)}) %collective-permute-start.13) | collective-permute-done | bytes 409632 | tf_op jit(solution)/shard_map/ppermute | solution.py:842
  390.6 6.9 %fusion.11.refs_4_.part_ref = f32[768,1024]{1,0:T(8,128)} fusion(bf16[1536,1024]{1,0:T(8,128)(2,1)} %get-tuple-element.92, bf16[1,768,1536]{2,1,0:T(8,128)(2,1)} %all-gather.17.cloned.1.call-done), kind=kOutput, calls=%fused_computation.32 | convolution fusion | flops 2415919104 | bytes 8650752 | tf_op jit(solution)/shard_map/dot_general | solution.py:26
  399.8 33.6 %scan_backward.3 = (bf16[1824,1024]{1,0:T(8,128)(2,1)}, f32[8,1792]{1,0:T(8,128)}, f32[32,8]{1,0:T(8,128)}, f32[8,1792]{1,0:T(8,128)}) custom-call(bf16[1600,128]{1,0:T(8,128)(2,1)} %copy-done.19, bf16[1600,128]{1,0:T(8,128)(2,1)} %copy-done.15, bf16[1600,128]{1,0:T(8,128)(2,1)} %copy-done.14, bf16[8,384,768]{2,1,0:T(8,128)(2,1)} %pad_maximum_fusion.1.refs_3_, ...), custom_call_target="tpu_custom_call" | custom-call | bytes 121770000 | tf_op jit(solution)/shard_map/scan_backward/pallas_call | solution.py:661
  444.9 6.9 %convolution_convert_fusion.4 = bf16[768,1824]{1,0:T(8,128)(2,1)} fusion(bf16[768,1024]{1,0:T(8,128)(2,1)S(1)} %fusion.4, bf16[1824,1024]{1,0:T(8,128)(2,1)} %edge_gradient.3.dqd_ref), kind=kOutput, calls=%fused_computation.9 | convolution fusion | flops 2870304768 | bytes 8110080 | tf_op jit(solution)/shard_map/dot_general | solution.py:26
  456.7 11.1 %input_backward.3 = (f32[1024,768]{1,0:T(8,128)}, f32[8,768]{1,0:T(8,128)}) custom-call(bf16[768,1824]{1,0:T(8,128)(2,1)} %all-gather.13.cloned.1.call-done.w_ref, bf16[1824,1024]{1,0:T(8,128)(2,1)} %edge_gradient.3.dqd_ref, f32[768,1024]{1,0:T(8,128)} %fusion.11.refs_4_.part_ref, bf16[768,1024]{1,0:T(8,128)(2,1)} %bitcast.188, ...), custom_call_target="tpu_custom_call" | custom-call | tf_op jit(solution)/shard_map/input_backward/pallas_call | solution.py:777
  481.4 9.4 %collective-permute-done.18 = f32[22672]{0:T(1024)S(1)} collective-permute-done((f32[22672]{0:T(1024)S(1)}, f32[22672]{0:T(1024)S(1)}, u32[]{:S(2)}, u32[]{:S(2)}) %collective-permute-start.18) | collective-permute-done | bytes 90720 | tf_op jit(solution)/shard_map/ppermute | solution.py:884
  516.1 9.1 %collective-permute-done.29 = bf16[96,1824]{1,0:T(8,128)(2,1)S(1)} collective-permute-done((bf16[96,1824]{1,0:T(8,128)(2,1)}, bf16[96,1824]{1,0:T(8,128)(2,1)S(1)}, u32[]{:S(2)}, u32[]{:S(2)}) %collective-permute-start.29) | collective-permute-done | bytes 350240 | tf_op jit(solution)/shard_map/ppermute | solution.py:850
  (370 shorter events, 203.3 us)
Async XLA Ops:
  7.2 42.7 %all-gather.13.cloned.1.call-start = ((), (), s32[]{:S(2)}) async-start(), calls=%async_computation.4 | async-start | bytes 3317760 | tf_op jit(solution)/shard_map/all_gather | solution.py:968
  10.2 80.9 %all-gather.17.cloned.1.call-start = ((), (), s32[]{:S(2)}) async-start(), calls=%async_computation.10 | async-start | bytes 2654208 | tf_op jit(solution)/shard_map/all_gather | solution.py:969
  12.3 102.8 %all-gather.19.cloned.1.call-start = ((), (), s32[]{:S(2)}) async-start(), calls=%async_computation.11 | async-start | bytes 2654208 | tf_op jit(solution)/shard_map/all_gather | solution.py:970
  13.2 139.2 %all-gather.15.cloned.1.call-start = ((), (), s32[]{:S(2)}) async-start(), calls=%async_computation.5 | async-start | bytes 3317760 | tf_op jit(solution)/shard_map/all_gather | solution.py:968
  14.2 181.3 %all-gather.21.cloned.1.call-start = ((), (), s32[]{:S(2)}) async-start(), calls=%async_computation.12 | async-start | bytes 2654208 | tf_op jit(solution)/shard_map/all_gather | solution.py:969
  14.8 203.9 %all-gather.23.cloned.1.call-start = ((), (), s32[]{:S(2)}) async-start(), calls=%async_computation.13 | async-start | bytes 2654208 | tf_op jit(solution)/shard_map/all_gather | solution.py:970
  15.4 308.5 %reduce-scatter.5.cloned.1.call-start = ((), (), s32[]{:S(2)}) async-start(), calls=%async_computation.6 | async-start | bytes 5308416 | tf_op jit(solution)/shard_map/reduce_scatter | solution.py:1026
  86.8 18.0 %collective-permute-start.2 = (bf16[1600,128]{1,0:T(8,128)(2,1)}, bf16[1600,128]{1,0:T(8,128)(2,1)}, u32[]{:S(2)}, u32[]{:S(2)}) collective-permute-start(bf16[1600,128]{1,0:T(8,128)(2,1)} %get-tuple-element.63.refs_8_), channel_id=1, source_target_pairs={{0,16},{8,24},{1,17},{9,25},{2,18},{10,26},{3,19},{11,27},{4,20},{... | collective-permute-start | bytes 1228808 | tf_op jit(solution)/shard_map/ppermute | solution.py:842
  88.8 16.0 %collective-permute-start.3 = (bf16[1600,128]{1,0:T(8,128)(2,1)}, bf16[1600,128]{1,0:T(8,128)(2,1)}, u32[]{:S(2)}, u32[]{:S(2)}) collective-permute-start(bf16[1600,128]{1,0:T(8,128)(2,1)} %get-tuple-element.63.refs_8_), channel_id=1, source_target_pairs={{0,24},{1,25},{2,26},{3,27},{4,28},{5,29},{6,30},{7,31}} | collective-permute-start | bytes 1228808 | tf_op jit(solution)/shard_map/ppermute | solution.py:842
  191.2 18.1 %collective-permute-start.6 = (bf16[1600,128]{1,0:T(8,128)(2,1)}, bf16[1600,128]{1,0:T(8,128)(2,1)}, u32[]{:S(2)}, u32[]{:S(2)}) collective-permute-start(bf16[1600,128]{1,0:T(8,128)(2,1)} %get-tuple-element.68.refs_7_), channel_id=1, source_target_pairs={{0,16},{8,24},{1,17},{9,25},{2,18},{10,26},{3,19},{11,27},{4,20},{... | collective-permute-start | bytes 1228808 | tf_op jit(solution)/shard_map/ppermute | solution.py:842
  193.2 16.0 %collective-permute-start.7 = (bf16[1600,128]{1,0:T(8,128)(2,1)}, bf16[1600,128]{1,0:T(8,128)(2,1)}, u32[]{:S(2)}, u32[]{:S(2)}) collective-permute-start(bf16[1600,128]{1,0:T(8,128)(2,1)} %get-tuple-element.68.refs_7_), channel_id=1, source_target_pairs={{0,24},{1,25},{2,26},{3,27},{4,28},{5,29},{6,30},{7,31}} | collective-permute-start | bytes 1228808 | tf_op jit(solution)/shard_map/ppermute | solution.py:842
  248.6 203.1 %reduce-scatter.11.cloned.1.call-start = ((), (), s32[]{:S(2)}) async-start(), calls=%async_computation.9 | async-start | bytes 3317760 | tf_op jit(solution)/shard_map/reduce_scatter | solution.py:1037
  250.1 23.0 %collective-permute-start.9 = (bf16[1600,128]{1,0:T(8,128)(2,1)}, bf16[1600,128]{1,0:T(8,128)(2,1)S(1)}, u32[]{:S(2)}, u32[]{:S(2)}) collective-permute-start(bf16[1600,128]{1,0:T(8,128)(2,1)} %get-tuple-element.74), channel_id=1, source_target_pairs={{16,0},{24,8},{17,1},{25,9},{18,2},{26,10},{19,3},{27,11},{20,4},{... | collective-permute-start | bytes 1228808 | tf_op jit(solution)/shard_map/ppermute | solution.py:842
  251.4 21.7 %collective-permute-start.10 = (bf16[1600,128]{1,0:T(8,128)(2,1)}, bf16[1600,128]{1,0:T(8,128)(2,1)S(1)}, u32[]{:S(2)}, u32[]{:S(2)}) collective-permute-start(bf16[1600,128]{1,0:T(8,128)(2,1)} %get-tuple-element.74), channel_id=1, source_target_pairs={{24,0},{25,1},{26,2},{27,3},{28,4},{29,5},{30,6},{31,7}} | collective-permute-start | bytes 1228808 | tf_op jit(solution)/shard_map/ppermute | solution.py:842
  323.9 132.1 %reduce-scatter.7.cloned.1.call-start = ((), (), s32[]{:S(2)}) async-start(), calls=%async_computation.7 | async-start | bytes 5308416 | tf_op jit(solution)/shard_map/reduce_scatter | solution.py:1026
  365.7 146.8 %reduce-scatter.9.cloned.1.call-start = ((), (), s32[]{:S(2)}) async-start(), calls=%async_computation.8 | async-start | bytes 3317760 | tf_op jit(solution)/shard_map/reduce_scatter | solution.py:1037
  451.7 22.5 %collective-permute-start.32 = (bf16[96,1824]{1,0:T(8,128)(2,1)}, bf16[96,1824]{1,0:T(8,128)(2,1)S(1)}, u32[]{:S(2)}, u32[]{:S(2)}) collective-permute-start(bf16[96,1824]{1,0:T(8,128)(2,1)} %reduce-scatter.11.cloned.1.call-done), channel_id=1, source_target_pairs={{0,24},{8,16},{16,8},{24,0},{1,25},{9,17},{17,9},{25,1},{2,26},{10... | collective-permute-start | bytes 1050632 | tf_op jit(solution)/shard_map/ppermute | solution.py:850
  452.7 21.6 %collective-permute-start.31 = (bf16[96,1824]{1,0:T(8,128)(2,1)}, bf16[96,1824]{1,0:T(8,128)(2,1)}, u32[]{:S(2)}, u32[]{:S(2)}) collective-permute-start(bf16[96,1824]{1,0:T(8,128)(2,1)} %reduce-scatter.11.cloned.1.call-done), channel_id=1, source_target_pairs={{0,16},{8,24},{16,0},{24,8},{1,17},{9,25},{17,1},{25,9},{2,18},{10... | collective-permute-start | bytes 1050632 | tf_op jit(solution)/shard_map/ppermute | solution.py:850
  456.1 19.7 %collective-permute-start.30 = (bf16[96,1824]{1,0:T(8,128)(2,1)}, bf16[96,1824]{1,0:T(8,128)(2,1)}, u32[]{:S(2)}, u32[]{:S(2)}) collective-permute-start(bf16[96,1824]{1,0:T(8,128)(2,1)} %reduce-scatter.11.cloned.1.call-done), channel_id=1, source_target_pairs={{0,8},{8,0},{16,24},{24,16},{1,9},{9,1},{17,25},{25,17},{2,10},{10... | collective-permute-start | bytes 1050632 | tf_op jit(solution)/shard_map/ppermute | solution.py:850
  469.7 22.8 %collective-permute-start.23 = (bf16[192,768]{1,0:T(8,128)(2,1)}, bf16[192,768]{1,0:T(8,128)(2,1)}, u32[]{:S(2)}, u32[]{:S(2)}) collective-permute-start(bf16[192,768]{1,0:T(8,128)(2,1)} %get-tuple-element.216), channel_id=1, source_target_pairs={{0,24},{8,16},{16,8},{24,0},{1,25},{9,17},{17,9},{25,1},{2,26},{10... | collective-permute-start | bytes 884744 | tf_op jit(solution)/shard_map/ppermute | solution.py:866
  471.2 21.3 %collective-permute-start.22 = (bf16[192,768]{1,0:T(8,128)(2,1)}, bf16[192,768]{1,0:T(8,128)(2,1)}, u32[]{:S(2)}, u32[]{:S(2)}) collective-permute-start(bf16[192,768]{1,0:T(8,128)(2,1)} %get-tuple-element.217), channel_id=1, source_target_pairs={{0,16},{8,24},{16,0},{24,8},{1,17},{9,25},{17,1},{25,9},{2,18},{10... | collective-permute-start | bytes 884744 | tf_op jit(solution)/shard_map/ppermute | solution.py:866
  474.2 18.3 %collective-permute-start.21 = (bf16[192,768]{1,0:T(8,128)(2,1)S(1)}, bf16[192,768]{1,0:T(8,128)(2,1)}, u32[]{:S(2)}, u32[]{:S(2)}) collective-permute-start(bf16[192,768]{1,0:T(8,128)(2,1)S(1)} %get-tuple-element.215), channel_id=1, source_target_pairs={{0,8},{8,0},{16,24},{24,16},{1,9},{9,1},{17,25},{25,17},{2,10},{10... | collective-permute-start | bytes 884744 | tf_op jit(solution)/shard_map/ppermute | solution.py:866
  514.5 15.9 %collective-permute-start.28 = (bf16[96,1824]{1,0:T(8,128)(2,1)}, bf16[96,1824]{1,0:T(8,128)(2,1)S(1)}, u32[]{:S(2)}, u32[]{:S(2)}) collective-permute-start(bf16[96,1824]{1,0:T(8,128)(2,1)} %reduce-scatter.9.cloned.1.call-done), channel_id=1, source_target_pairs={{0,16},{8,24},{16,0},{24,8},{1,17},{9,25},{17,1},{25,9},{2,18},{10... | collective-permute-start | bytes 1050632 | tf_op jit(solution)/shard_map/ppermute | solution.py:850
  515.4 15.0 %collective-permute-start.27 = (bf16[96,1824]{1,0:T(8,128)(2,1)}, bf16[96,1824]{1,0:T(8,128)(2,1)S(1)}, u32[]{:S(2)}, u32[]{:S(2)}) collective-permute-start(bf16[96,1824]{1,0:T(8,128)(2,1)} %reduce-scatter.9.cloned.1.call-done), channel_id=1, source_target_pairs={{0,8},{8,0},{16,24},{24,16},{1,9},{9,1},{17,25},{25,17},{2,10},{10... | collective-permute-start | bytes 1050632 | tf_op jit(solution)/shard_map/ppermute | solution.py:850
  (76 other events, 1434.8 us)
Sparse Core Ops, SparseCore 0:
  10.2 39.5 all-gather.12
  52.1 30.5 all-gather.16
  84.3 30.7 all-gather.18
  116.5 35.7 all-gather.14
  153.9 30.4 all-gather.20
  185.9 30.7 all-gather.22
  248.7 55.2 reduce-scatter.4
  324.1 36.4 reduce-scatter.10
  365.8 52.6 reduce-scatter.6
  471.3 40.1 reduce-scatter.8
